TPU v7x, 256 devices: a whole 4x4x8 slice. The times are simulated.
256 devices in a mesh: seq: 32 (over y, z), tp: 8 (over x, core).
Axes of the slice: x: 4, y: 4, z: 8, core: 2. Of those that a mesh axis runs over, the one named last changes fastest.
Arguments:
- queries: bfloat16 [12288, 5120], P('seq', 'tp'), may hold values from -8 to 8
- key_rows: bfloat16 [12288, 5120], P('seq', 'tp'), may hold values from -8 to 8
- values: bfloat16 [12288, 5120], P('seq', 'tp'), may hold values from -6 to 6
- out_weight: bfloat16 [5120, 5120], P('tp', 'seq'), may hold values from -0.3125 to 0.3125
- grad_out: bfloat16 [12288, 5120], P('seq', 'tp'), may hold values from -1.5 to 1.5
- labels: int32 [12288], P('seq'), may hold values from 0 to 127, as said below
- owner_map: int32 [128], replicated, may hold values from 0 to 31, as said below
- pair_mask: int32 [128, 128], replicated, may hold values from 0 to 1, as said below
Outputs:
- output: bfloat16 [12288, 5120], P('seq', 'tp')
- grad_queries: bfloat16 [12288, 5120], P('seq', 'tp')
- grad_keys: bfloat16 [12288, 5120], P('seq', 'tp')
- grad_values: bfloat16 [12288, 5120], P('seq', 'tp')
Inputs may be any that keep to these rules, and one draw needn't show every extreme that they name: `labels`: of the 384 tokens of one index of seq, at most 24 lie in clusters of any one owner; in every draw some owner receives exactly 24 from every index, 768 in all. `owner_map`: every owner index holds exactly 4 clusters. pair_mask[a, b] is 1 only where owner_map[a] == owner_map[b], and pair_mask[a, a] = 1.
All inputs are finite; a program needn't handle non-finite values.
Results may differ from a plain program's by a relative error of at most 0.017.
Values may be sent and summed in bfloat16 or wider, within the bound.
No kernel may reach another device: no remote copies, remote signals or barrier semaphores. Data moves between devices by JAX's collectives and lax.ppermute only.
A program may use at most 64 MiB of HBM per device.

v0:
```python
import jax
import jax.numpy as jnp
from jax import lax
from jax.sharding import PartitionSpec as P

HEAD = 128


NEG_FILL = -1e30


def head_weights(query_head, key_head, allowed, head_scale):
    scores = (
        lax.dot_general(
            query_head, key_head, (((1,), (1,)), ((), ())), preferred_element_type=jnp.float32
        )
        * head_scale
    )
    scores = jnp.where(allowed, scores, NEG_FILL)
    row_top = jnp.max(scores, axis=1, keepdims=True)
    exp_terms = jnp.exp(scores - row_top)
    return exp_terms / jnp.sum(exp_terms, axis=1, keepdims=True)


def head_forward(query_head, key_head, value_head, allowed, head_scale):
    weights = head_weights(query_head, key_head, allowed, head_scale)
    return jnp.dot(
        weights.astype(jnp.bfloat16), value_head, preferred_element_type=jnp.float32
    ).astype(jnp.bfloat16)


def head_backward(query_head, key_head, value_head, attended, grad_att, allowed, head_scale):
    weights = head_weights(query_head, key_head, allowed, head_scale)
    weights_low = weights.astype(jnp.bfloat16)
    grad_probs = lax.dot_general(
        grad_att, value_head, (((1,), (1,)), ((), ())), preferred_element_type=jnp.float32
    )
    delta_rows = jnp.sum(
        grad_att.astype(jnp.float32) * attended.astype(jnp.float32), axis=1, keepdims=True
    )
    grad_scores = (weights * (grad_probs - delta_rows)).astype(jnp.bfloat16)
    grad_query = (
        jnp.dot(grad_scores, key_head, preferred_element_type=jnp.float32) * head_scale
    ).astype(jnp.bfloat16)
    grad_key = (
        lax.dot_general(
            grad_scores, query_head, (((0,), (0,)), ((), ())), preferred_element_type=jnp.float32
        )
        * head_scale
    ).astype(jnp.bfloat16)
    grad_value = lax.dot_general(
        weights_low, grad_att, (((0,), (0,)), ((), ())), preferred_element_type=jnp.float32
    ).astype(jnp.bfloat16)
    return (grad_query, grad_key, grad_value)


def per_heads(function, matrices):
    head_total = matrices[0].shape[1] // HEAD

    def one_head(head_index):
        return function(
            tuple(
                (
                    lax.dynamic_slice_in_dim(matrix, head_index * HEAD, HEAD, 1)
                    for matrix in matrices
                )
            )
        )

    return lax.map(one_head, jnp.arange(head_total, dtype=jnp.int32))


def join_heads(stacked):
    return jnp.transpose(stacked, (1, 0, 2)).reshape(stacked.shape[1], -1)


def body(queries, key_rows, values, out_weight, grad_out, labels, owner_map, pair_mask):
    seq_count = lax.axis_size("seq")
    row_count = queries.shape[0]
    width_local = queries.shape[1]
    slot_size = 2 * row_count // seq_count
    buffer_rows = seq_count * slot_size
    head_scale = HEAD ** (-0.5)
    cluster_ids = jnp.arange(owner_map.shape[0], dtype=jnp.int32)
    token_owner = jnp.sum(
        jnp.where(labels[:, None] == cluster_ids[None, :], owner_map[None, :], 0), axis=1
    )
    owner_hits = (token_owner[:, None] == jnp.arange(seq_count, dtype=jnp.int32)[None, :]).astype(
        jnp.int32
    )
    within = jnp.sum((jnp.cumsum(owner_hits, axis=0) - 1) * owner_hits, axis=1)
    dest_index = token_owner * slot_size + within
    source_row = (
        jnp.zeros((buffer_rows,), jnp.int32)
        .at[dest_index]
        .set(jnp.arange(row_count, dtype=jnp.int32))
    )
    filled = jnp.zeros((buffer_rows,), jnp.bool_).at[dest_index].set(True)

    def pack_rows(matrix):
        picked = jnp.where(filled[:, None], matrix[source_row], jnp.zeros((), matrix.dtype))
        return picked.reshape(seq_count, slot_size, matrix.shape[1])

    def unpack_rows(blocks):
        return blocks.reshape(buffer_rows, blocks.shape[2])[dest_index]

    label_code = (labels + 1).astype(jnp.bfloat16)[:, None]
    sent = (
        lax.all_to_all(pack_rows(queries), "seq", split_axis=0, concat_axis=0, tiled=True),
        lax.all_to_all(pack_rows(key_rows), "seq", split_axis=0, concat_axis=0, tiled=True),
        lax.all_to_all(pack_rows(values), "seq", split_axis=0, concat_axis=0, tiled=True),
        lax.all_to_all(pack_rows(label_code), "seq", split_axis=0, concat_axis=0, tiled=True),
    )
    owned_q, owned_k, owned_v, owned_code = [
        received.reshape(buffer_rows, received.shape[2]) for received in sent
    ]
    code_int = owned_code[:, 0].astype(jnp.int32)
    onehot = (code_int[:, None] == cluster_ids[None, :] + 1).astype(jnp.bfloat16)
    linked = jnp.dot(
        onehot, pair_mask.astype(jnp.bfloat16), preferred_element_type=jnp.float32
    ).astype(jnp.bfloat16)
    allowed = (
        lax.dot_general(
            linked, onehot, (((1,), (1,)), ((), ())), preferred_element_type=jnp.float32
        )
        > 0.5
    )
    attended = join_heads(
        per_heads(
            lambda pieces: head_forward(pieces[0], pieces[1], pieces[2], allowed, head_scale),
            (owned_q, owned_k, owned_v),
        )
    )
    returned = lax.all_to_all(
        attended.reshape(seq_count, slot_size, width_local),
        "seq",
        split_axis=0,
        concat_axis=0,
        tiled=True,
    )
    attended_local = unpack_rows(returned)
    full_weight = lax.all_gather(out_weight, "seq", axis=1, tiled=True)
    partial_out = jnp.dot(attended_local, full_weight, preferred_element_type=jnp.float32)
    output = lax.psum_scatter(
        partial_out.astype(jnp.bfloat16), "tp", scatter_dimension=1, tiled=True
    )
    grad_full = lax.all_gather(grad_out, "tp", axis=1, tiled=True)
    grad_att = lax.dot_general(
        grad_full, full_weight, (((1,), (1,)), ((), ())), preferred_element_type=jnp.float32
    )
    grad_att = grad_att.astype(jnp.bfloat16)
    grad_owned = lax.all_to_all(
        pack_rows(grad_att), "seq", split_axis=0, concat_axis=0, tiled=True
    ).reshape(buffer_rows, width_local)
    stacked = per_heads(
        lambda pieces: head_backward(
            pieces[0], pieces[1], pieces[2], pieces[3], pieces[4], allowed, head_scale
        ),
        (owned_q, owned_k, owned_v, attended, grad_owned),
    )
    grad_q_rows = join_heads(stacked[0]).reshape(seq_count, slot_size, width_local)
    grad_k_rows = join_heads(stacked[1]).reshape(seq_count, slot_size, width_local)
    grad_v_rows = join_heads(stacked[2]).reshape(seq_count, slot_size, width_local)
    back_q, back_k, back_v = (
        lax.all_to_all(grad_q_rows, "seq", split_axis=0, concat_axis=0, tiled=True),
        lax.all_to_all(grad_k_rows, "seq", split_axis=0, concat_axis=0, tiled=True),
        lax.all_to_all(grad_v_rows, "seq", split_axis=0, concat_axis=0, tiled=True),
    )
    return (output, unpack_rows(back_q), unpack_rows(back_k), unpack_rows(back_v))


def solution(mesh):
    in_specs = (
        P("seq", "tp"),
        P("seq", "tp"),
        P("seq", "tp"),
        P("tp", "seq"),
        P("seq", "tp"),
        P("seq"),
        P(),
        P(),
    )
    out_specs = (P("seq", "tp"), P("seq", "tp"), P("seq", "tp"), P("seq", "tp"))
    return jax.shard_map(body, mesh=mesh, in_specs=in_specs, out_specs=out_specs, check_vma=False)
```

profile of v0, /device:TPU:4, one launch (start us, length us, event | category | flops | bytes accessed | tf_op | source)
XLA Modules:
  0.0 514.2 jit_solution(5709064129453234233)
XLA Ops:
  10.9 2.9 scatter_custom_fusion.1
  13.8 2.0 scatter_custom_fusion
  16.5 5.0 gather_fusion.2
  22.2 11.5 %all-to-all-start.2 = ((bf16[32,24,1]{1,2,0:T(2,128)(2,1)}), bf16[32,24,1]{1,2,0:T(2,128)(2,1)S(1)}, u32[]{:S(2)}, u32[]{:S(2)}) async-start(bf16[32,24,1]{1,2,0:T(2,128)(2,1)} %reshape.243), calls=%async_computation.2 | async-start | bytes 32768 | tf_op jit(solution)/shard_map/all_to_all | solution.py:112
  33.8 2.8 gather_fusion.1
  36.6 3.4 gather_fusion.3
  40.1 3.4 gather_fusion
  45.1 93.6 %all-gather.3.cloned.1.call-done = bf16[640,5120]{0,1:T(8,128)(2,1)} async-done(((bf16[640,160]{0,1:T(8,128)(2,1)}), bf16[640,5120]{0,1:T(8,128)(2,1)}) %all-gather.3.cloned.1.call-update) | async-done | bytes 6553616 | tf_op jit(solution)/shard_map/all_gather | solution.py:142
  138.7 7.3 %convolution_convert_fusion.1 = bf16[384,640]{1,0:T(8,128)(2,1)S(1)} fusion(bf16[384,5120]{1,0:T(8,128)(2,1)} %all-gather.5.cloned.1.call-done, bf16[640,5120]{0,1:T(8,128)(2,1)} %all-gather.3.cloned.1.call-done), kind=kOutput, calls=%fused_computation.58 | convolution fusion | flops 2516828160 | bytes 10977280 | tf_op jit(solution)/shard_map/dot_general | solution.py:148
  146.0 3.4 gather_fusion.5
  149.4 3.9 broadcast_select_fusion
  153.3 32.7 %all_to_all.45 = bf16[32,24,640]{2,1,0:T(8,128)(2,1)S(1)} all-to-all(bf16[32,24,640]{2,1,0:T(8,128)(2,1)S(1)} %get-tuple-element.219), channel_id=1, replica_groups=mesh['seq'=32,'tp'=8] {'seq'}, dimensions={0} | all-to-all | bytes 1966080 | tf_op jit(solution)/shard_map/all_to_all | solution.py:109
  186.0 31.7 %all_to_all.46 = bf16[32,24,640]{2,1,0:T(8,128)(2,1)S(1)} all-to-all(bf16[32,24,640]{2,1,0:T(8,128)(2,1)S(1)} %copy-done.4), channel_id=1, replica_groups=mesh['seq'=32,'tp'=8] {'seq'}, dimensions={0} | all-to-all | bytes 1966080 | tf_op jit(solution)/shard_map/all_to_all | solution.py:110
  217.7 4.9 all-to-all-start.3
  226.1 23.5 %all-to-all-done.3 = bf16[32,24,640]{2,1,0:T(8,128)(2,1)} async-done(((bf16[32,24,640]{2,1,0:T(8,128)(2,1)}), bf16[32,24,640]{2,1,0:T(8,128)(2,1)}, u32[]{:S(2)}, u32[]{:S(2)}) %all-to-all-start.3) | async-done | bytes 983072 | tf_op jit(solution)/shard_map/all_to_all | solution.py:111
  250.8 21.9 %while.24 = (s32[]{:T(128)}, bf16[5,768,128]{2,1,0:T(8,128)(2,1)}, s32[5]{0:T(128)S(1)}, bf16[768,640]{1,0:T(8,128)(2,1)S(1)}, bf16[768,640]{1,0:T(8,128)(2,1)S(...) while((s32[]{:T(128)}, bf16[5,768,128]{2,1,0:T(8,128)(2,1)}, ...), condition=%wide.region_9.10_spmd, body=%wide.region_6.9_spmd.sunk | while | flops 306805248 | bytes 8470711 | solution.py:70
  253.0 2.2 fusion.86
  257.4 2.2 fusion.86
  261.7 2.2 fusion.86
  266.1 2.2 fusion.86
  270.5 2.2 fusion.86
  272.7 3.4 copy.42
  276.1 3.6 reshape_reshape.12
  279.7 31.8 %all_to_all.47 = bf16[32,24,640]{2,1,0:T(8,128)(2,1)S(1)} all-to-all(bf16[32,24,640]{2,1,0:T(8,128)(2,1)} %reshape_reshape.12), channel_id=1, replica_groups=mesh['seq'=32,'tp'=8] {'seq'}, dimensions={0} | all-to-all | bytes 1966080 | tf_op jit(solution)/shard_map/all_to_all | solution.py:134
  311.5 4.9 all-to-all-start.5
  316.5 2.3 copy.41
  318.8 2.2 gather_fusion.4
  321.0 8.9 %convolution_convert_fusion = bf16[384,5120]{1,0:T(8,128)(2,1)} fusion(bf16[384,640]{1,0:T(8,128)(2,1)S(1)} %gather_fusion.4, bf16[640,5120]{0,1:T(8,128)(2,1)} %all-gather.3.cloned.1.call-done), kind=kOutput, calls=%fused_computation.56 | convolution fusion | flops 2518548480 | bytes 10977280 | tf_op jit(solution)/shard_map/dot_general | solution.py:143
  329.9 6.3 %copy.50 = bf16[384,5120]{0,1:T(8,128)(2,1)} copy(bf16[384,5120]{1,0:T(8,128)(2,1)} %convolution_convert_fusion) | data formatting | bytes 7864320
  336.2 7.2 %all-to-all-done.5 = bf16[32,24,640]{2,1,0:T(8,128)(2,1)} async-done(((bf16[32,24,640]{2,1,0:T(8,128)(2,1)}), bf16[32,24,640]{2,1,0:T(8,128)(2,1)}, u32[]{:S(2)}, u32[]{:S(2)}) %all-to-all-start.5) | async-done | bytes 983072 | tf_op jit(solution)/shard_map/all_to_all | solution.py:152
  345.7 59.3 %while.25 = (s32[]{:T(128)}, bf16[5,768,128]{2,1,0:T(8,128)(2,1)S(1)}, bf16[5,768,128]{2,1,0:T(8,128)(2,1)}, bf16[5,768,128]{2,1,0:T(8,128)(2,1)}, s32[5]{0:T(12...) while((s32[]{:T(128)}, ...), condition=%wide.region_15.16_spmd, body=%wide.region_11.15_spmd.sunk | while | flops 763524864 | bytes 16741615 | solution.py:70
  355.5 2.1 fusion.99
  367.3 2.1 fusion.99
  379.2 2.1 fusion.99
  391.0 2.1 fusion.99
  402.8 2.1 fusion.99
  405.6 2.0 reshape_reshape.13
  407.6 4.9 all-to-all-start.6
  416.4 23.0 %all-to-all-done.6 = bf16[32,24,640]{2,1,0:T(8,128)(2,1)S(1)} async-done(((bf16[32,24,640]{2,1,0:T(8,128)(2,1)}), bf16[32,24,640]{2,1,0:T(8,128)(2,1)S(1)}, u32[]{:S(2)}, u32[]{:S(2)}) %all-to-all-start.6) | async-done | bytes 983072 | tf_op jit(solution)/shard_map/all_to_all | solution.py:165
  439.4 4.8 all-to-all-start.7
  446.1 3.6 reshape_reshape.15
  449.6 21.5 %all-to-all-done.7 = bf16[32,24,640]{2,1,0:T(8,128)(2,1)S(1)} async-done(((bf16[32,24,640]{2,1,0:T(8,128)(2,1)}), bf16[32,24,640]{2,1,0:T(8,128)(2,1)S(1)}, u32[]{:S(2)}, u32[]{:S(2)}) %all-to-all-start.7) | async-done | bytes 983072 | tf_op jit(solution)/shard_map/all_to_all | solution.py:166
  471.2 4.8 all-to-all-start.8
  476.0 2.6 gather_fusion.6
  478.6 2.6 gather_fusion.7
  481.2 21.7 %all-to-all-done.8 = bf16[32,24,640]{2,1,0:T(8,128)(2,1)S(1)} async-done(((bf16[32,24,640]{2,1,0:T(8,128)(2,1)}), bf16[32,24,640]{2,1,0:T(8,128)(2,1)S(1)}, u32[]{:S(2)}, u32[]{:S(2)}) %all-to-all-start.8) | async-done | bytes 983072 | tf_op jit(solution)/shard_map/all_to_all | solution.py:167
  503.0 2.6 gather_fusion.8
  505.6 2.0 copy.51
  (115 shorter events, 72.9 us)
Async XLA Ops:
  7.2 26.7 %copy-start = (bf16[384,640]{1,0:T(8,128)(2,1)S(1)}, bf16[384,640]{1,0:T(8,128)(2,1)}, u32[]{:S(2)}) copy-start(bf16[384,640]{1,0:T(8,128)(2,1)} %param.13) | copy-start | bytes 1474564
  7.2 37.9 %all-gather.5.cloned.1.call-start = ((), (), s32[]{:S(2)}) async-start(), calls=%async_computation.11 | async-start | bytes 4423680 | tf_op jit(solution)/shard_map/all_gather | solution.py:147
  7.9 130.8 %all-gather.3.cloned.1.call-start = ((), (), s32[]{:S(2)}) async-start(), calls=%async_computation.10 | async-start | bytes 6758400 | tf_op jit(solution)/shard_map/all_gather | solution.py:142
  22.2 131.0 %all-to-all-start.2 = ((bf16[32,24,1]{1,2,0:T(2,128)(2,1)}), bf16[32,24,1]{1,2,0:T(2,128)(2,1)S(1)}, u32[]{:S(2)}, u32[]{:S(2)}) async-start(bf16[32,24,1]{1,2,0:T(2,128)(2,1)} %reshape.243), calls=%async_computation.2 | async-start | bytes 32768 | tf_op jit(solution)/shard_map/all_to_all | solution.py:112
  33.8 2.8 copy-start.1
  36.6 3.4 copy-start.2
  153.3 32.7 %copy-start.4 = (bf16[32,24,640]{2,1,0:T(8,128)(2,1)S(1)}, bf16[32,24,640]{2,1,0:T(8,128)(2,1)}, u32[]{:S(2)}) copy-start(bf16[32,24,640]{2,1,0:T(8,128)(2,1)} %get-tuple-element.217) | copy-start | bytes 2949124
  186.0 36.8 %copy-start.6 = (s32[128,128]{1,0:T(8,128)S(1)}, s32[128,128]{1,0:T(8,128)}, u32[]{:S(2)}) copy-start(s32[128,128]{1,0:T(8,128)} %param.19) | copy-start | bytes 196612
  217.7 31.9 %all-to-all-start.3 = ((bf16[32,24,640]{2,1,0:T(8,128)(2,1)}), bf16[32,24,640]{2,1,0:T(8,128)(2,1)}, u32[]{:S(2)}, u32[]{:S(2)}) async-start(bf16[32,24,640]{2,1,0:T(8,128)(2,1)} %get-tuple-element.218), calls=%async_computation.3 | async-start | bytes 1966080 | tf_op jit(solution)/shard_map/all_to_all | solution.py:111
  272.7 3.4 copy-start.3
  311.5 31.9 %all-to-all-start.5 = ((bf16[32,24,640]{2,1,0:T(8,128)(2,1)}), bf16[32,24,640]{2,1,0:T(8,128)(2,1)}, u32[]{:S(2)}, u32[]{:S(2)}) async-start(bf16[32,24,640]{2,1,0:T(8,128)(2,1)} %get-tuple-element.216), calls=%async_computation.5 | async-start | bytes 1966080 | tf_op jit(solution)/shard_map/all_to_all | solution.py:152
  316.4 189.2 %reduce-scatter.4.cloned.1.call-start = ((), (), s32[]{:S(2)}) async-start(), calls=%async_computation.12 | async-start | bytes 4423680
  407.6 31.8 %all-to-all-start.6 = ((bf16[32,24,640]{2,1,0:T(8,128)(2,1)}), bf16[32,24,640]{2,1,0:T(8,128)(2,1)S(1)}, u32[]{:S(2)}, u32[]{:S(2)}) async-start(bf16[32,24,640]{2,1,0:T(8,128)(2,1)} %reshape_reshape.13), calls=%async_computation.6 | async-start | bytes 1966080 | tf_op jit(solution)/shard_map/all_to_all | solution.py:165
  416.4 27.8 %copy-start.5 = (bf16[5,768,128]{2,1,0:T(8,128)(2,1)S(1)}, bf16[5,768,128]{2,1,0:T(8,128)(2,1)}, u32[]{:S(2)}) copy-start(bf16[5,768,128]{2,1,0:T(8,128)(2,1)} %get-tuple-element.103) | copy-start | bytes 2949124
  439.4 31.8 %all-to-all-start.7 = ((bf16[32,24,640]{2,1,0:T(8,128)(2,1)}), bf16[32,24,640]{2,1,0:T(8,128)(2,1)S(1)}, u32[]{:S(2)}, u32[]{:S(2)}) async-start(bf16[32,24,640]{2,1,0:T(8,128)(2,1)} %reshape_reshape.14), calls=%async_computation.7 | async-start | bytes 1966080 | tf_op jit(solution)/shard_map/all_to_all | solution.py:166
  471.2 31.8 %all-to-all-start.8 = ((bf16[32,24,640]{2,1,0:T(8,128)(2,1)}), bf16[32,24,640]{2,1,0:T(8,128)(2,1)S(1)}, u32[]{:S(2)}, u32[]{:S(2)}) async-start(bf16[32,24,640]{2,1,0:T(8,128)(2,1)} %reshape_reshape.15), calls=%async_computation.8 | async-start | bytes 1966080 | tf_op jit(solution)/shard_map/all_to_all | solution.py:167
Sparse Core Ops, SparseCore 0:
  9.9 35.1 all-gather.4
  47.6 91.0 all-gather.2
  336.3 36.2 reduce-scatter.3
where the time goes:
time: 516 us; the launch traced here: 514 us
  waiting for transfers between devices  194 us (38%)
  blocking collectives  96.3 us (19%)
  local copies, waits for them, and re-layouts  80.3 us (16%)
  matrix products  71.4 us (14%)
  starting transfers between devices  35.9 us (7%)
  other arithmetic  15.9 us (3%)
  between operations  14 us (3%)
  loops' own time  6.76 us (1%)
    all_gather x1, waiting for transfers between devices, body(): full_weight = lax.all_gather(out_weight, 'seq', axis=1, tiled=True)  93.6 us
    all_to_all x1, blocking collectives, body(): lax.all_to_all(pack_rows(queries), 'seq', split_axis=0, concat_axis=0, ti...  32.7 us
    all_to_all x1, blocking collectives, body(): lax.all_to_all(attended.reshape(seq_count, slot_size, width_local), 'seq'...  31.8 us
    all_to_all x1, blocking collectives, body(): lax.all_to_all(pack_rows(key_rows), 'seq', split_axis=0, concat_axis=0, t...  31.7 us
    all_to_all x1, waiting for transfers between devices, body(): lax.all_to_all(pack_rows(values), 'seq', split_axis=0, concat_axis=0, til...  23.5 us
    all_to_all x1, waiting for transfers between devices, body(): lax.all_to_all(grad_q_rows, 'seq', split_axis=0, concat_axis=0, tiled=True)  23 us
    all_to_all x1, waiting for transfers between devices, body(): lax.all_to_all(grad_v_rows, 'seq', split_axis=0, concat_axis=0, tiled=True)  21.7 us
    all_to_all x1, waiting for transfers between devices, body(): lax.all_to_all(grad_k_rows, 'seq', split_axis=0, concat_axis=0, tiled=True)  21.5 us
  transfers between devices with their start and end apart: 9, of which 7 were waited for; matrix products, arithmetic and copies ran while one was open for 27% of the time, Pallas kernels for 0%

commit v1 on v0

v1 whole, which is shorter than its diff:
```python
import jax
import jax.numpy as jnp
from jax import lax
from jax.experimental import pallas as pl
from jax.experimental.pallas import tpu as pltpu
from jax.sharding import PartitionSpec as P

HEAD = 128
NEG_FILL = -1e30
VMEM_BYTES = 48 * 1024 * 1024
NT = (((1,), (1,)), ((), ()))


def dot32(left, right):
    return jnp.dot(left, right, preferred_element_type=jnp.float32)


def dot32_nt(left, right):
    return lax.dot_general(left, right, NT, preferred_element_type=jnp.float32)


def params():
    return pltpu.CompilerParams(vmem_limit_bytes=VMEM_BYTES)


def pack_kernel(seq_count, slot_size, label_row, label_col, owner_col, q_ref, k_ref, v_ref, packed, dest_row, dest_col):
    rows = q_ref.shape[0]
    cols = q_ref.shape[1]
    clusters = owner_col.shape[0]
    buffer_rows = packed.shape[0]
    in_cluster = label_row[...] == lax.broadcasted_iota(jnp.int32, (clusters, rows), 0)
    owner_row = jnp.sum(jnp.where(in_cluster, owner_col[...], 0), axis=0, keepdims=True)
    owned = owner_row == lax.broadcasted_iota(jnp.int32, (seq_count, rows), 0)
    earlier = lax.broadcasted_iota(jnp.int32, (rows, rows), 0) < lax.broadcasted_iota(
        jnp.int32, (rows, rows), 1
    )
    before = dot32(
        owned.astype(jnp.float32).astype(jnp.bfloat16), earlier.astype(jnp.float32).astype(jnp.bfloat16)
    )
    rank_row = jnp.sum(jnp.where(owned, before, 0.0), axis=0, keepdims=True)
    dest = owner_row * slot_size + rank_row.astype(jnp.int32)
    dest_row[...] = dest
    wide = jnp.broadcast_to(dest.astype(jnp.float32), (HEAD, rows))
    dest_col[...] = jnp.transpose(wide).astype(jnp.int32)
    select = (lax.broadcasted_iota(jnp.int32, (buffer_rows, rows), 0) == dest).astype(jnp.float32).astype(jnp.bfloat16)
    packed[:, 0:cols] = dot32(select, q_ref[...]).astype(jnp.bfloat16)
    packed[:, cols : 2 * cols] = dot32(select, k_ref[...]).astype(jnp.bfloat16)
    packed[:, 2 * cols : 3 * cols] = dot32(select, v_ref[...]).astype(jnp.bfloat16)
    codes = jnp.broadcast_to((label_col[...] + 1).astype(jnp.float32), (rows, HEAD)).astype(jnp.bfloat16)
    packed[:, 3 * cols :] = dot32(select, codes).astype(jnp.bfloat16)


def pack_inputs(seq_count, slot_size, labels, owner_map, queries, key_rows, values):
    rows, cols = queries.shape
    buffer_rows = seq_count * slot_size
    return pl.pallas_call(
        lambda *refs: pack_kernel(seq_count, slot_size, *refs),
        out_shape=(
            jax.ShapeDtypeStruct((buffer_rows, 3 * cols + HEAD), jnp.bfloat16),
            jax.ShapeDtypeStruct((1, rows), jnp.int32),
            jax.ShapeDtypeStruct((rows, HEAD), jnp.int32),
        ),
        compiler_params=params(),
    )(labels[None, :], labels[:, None], owner_map[:, None], queries, key_rows, values)


def forward_kernel(scale, chunk, q_ref, k_ref, v_ref, code_ref, mask_ref, att_ref, weight_ref, bias):
    rows = q_ref.shape[0]

    @pl.when(pl.program_id(0) == 0)
    def _():
        lane = lax.broadcasted_iota(jnp.int32, (rows, HEAD), 1).astype(jnp.float32) + 1.0
        onehot = (code_ref[...].astype(jnp.float32) == lane).astype(jnp.float32).astype(jnp.bfloat16)
        linked = dot32(onehot, mask_ref[...]).astype(jnp.bfloat16)
        for start in range(0, rows, chunk):
            linked_part = linked[start : start + chunk]
            allowed = dot32_nt(onehot, linked_part) > 0.5
            bias[:, start : start + chunk] = jnp.where(allowed, 0.0, NEG_FILL)

    value_t = jnp.transpose(v_ref[...])
    for start in range(0, rows, chunk):
        part = slice(start, start + chunk)
        scores = dot32_nt(k_ref[...], q_ref[part, :]) * scale + bias[:, part]
        top = jnp.max(scores, axis=0, keepdims=True)
        terms = jnp.exp(scores - top)
        weights = (terms * (1.0 / jnp.sum(terms, axis=0, keepdims=True))).astype(jnp.bfloat16)
        weight_ref[0, :, part] = weights
        att_ref[part, :] = jnp.transpose(dot32(value_t, weights)).astype(jnp.bfloat16)


def backward_kernel(scale, chunk, q_ref, k_ref, v_ref, att_ref, g_ref, weight_ref, out_ref):
    rows = q_ref.shape[0]
    grad = g_ref[...]
    delta = jnp.sum(
        jnp.transpose(grad.astype(jnp.float32) * att_ref[...].astype(jnp.float32)), axis=0, keepdims=True
    )
    key_t = jnp.transpose(k_ref[...])
    grad_key = jnp.zeros((rows, HEAD), jnp.float32)
    grad_value = jnp.zeros((rows, HEAD), jnp.float32)
    for start in range(0, rows, chunk):
        part = slice(start, start + chunk)
        weights = weight_ref[0, :, part]
        grad_part = g_ref[part, :]
        grad_probs = dot32_nt(v_ref[...], grad_part)
        grad_scores = (weights.astype(jnp.float32) * (grad_probs - delta[:, part])).astype(jnp.bfloat16)
        out_ref[part, 0:HEAD] = jnp.transpose(dot32(key_t, grad_scores) * scale).astype(jnp.bfloat16)
        grad_key = grad_key + dot32(grad_scores, q_ref[part, :])
        grad_value = grad_value + dot32(weights, grad_part)
    out_ref[:, HEAD : 2 * HEAD] = (grad_key * scale).astype(jnp.bfloat16)
    out_ref[:, 2 * HEAD :] = grad_value.astype(jnp.bfloat16)


def attention_forward(owned, pair_mask, heads, scale, chunk):
    rows = owned.shape[0]
    block = (rows, HEAD)
    return pl.pallas_call(
        lambda *refs: forward_kernel(scale, chunk, *refs),
        grid=(heads,),
        in_specs=[
            pl.BlockSpec(block, lambda h: (0, h)),
            pl.BlockSpec(block, lambda h: (0, heads + h)),
            pl.BlockSpec(block, lambda h: (0, 2 * heads + h)),
            pl.BlockSpec(block, lambda h: (0, 3 * heads)),
            pl.BlockSpec(pair_mask.shape, lambda h: (0, 0)),
        ],
        out_specs=(
            pl.BlockSpec(block, lambda h: (0, h)),
            pl.BlockSpec((1, rows, rows), lambda h: (h, 0, 0)),
        ),
        out_shape=(
            jax.ShapeDtypeStruct((rows, heads * HEAD), jnp.bfloat16),
            jax.ShapeDtypeStruct((heads, rows, rows), jnp.bfloat16),
        ),
        scratch_shapes=[pltpu.VMEM((rows, rows), jnp.float32)],
        compiler_params=params(),
        cost_estimate=pl.CostEstimate(
            flops=heads * 4 * rows * rows * HEAD,
            bytes_accessed=heads * rows * (8 * HEAD + 2 * rows),
            transcendentals=heads * rows * rows,
        ),
    )(owned, owned, owned, owned, pair_mask)


def attention_backward(owned, attended, grad_owned, weights, heads, scale, chunk):
    rows = owned.shape[0]
    block = (rows, HEAD)
    return pl.pallas_call(
        lambda *refs: backward_kernel(scale, chunk, *refs),
        grid=(heads,),
        in_specs=[
            pl.BlockSpec(block, lambda h: (0, h)),
            pl.BlockSpec(block, lambda h: (0, heads + h)),
            pl.BlockSpec(block, lambda h: (0, 2 * heads + h)),
            pl.BlockSpec(block, lambda h: (0, h)),
            pl.BlockSpec(block, lambda h: (0, h)),
            pl.BlockSpec((1, rows, rows), lambda h: (h, 0, 0)),
        ],
        out_specs=pl.BlockSpec((rows, 3 * HEAD), lambda h: (0, h)),
        out_shape=jax.ShapeDtypeStruct((rows, 3 * heads * HEAD), jnp.bfloat16),
        compiler_params=params(),
        cost_estimate=pl.CostEstimate(
            flops=heads * 8 * rows * rows * HEAD,
            bytes_accessed=heads * rows * (16 * HEAD + 2 * rows),
            transcendentals=0,
        ),
    )(owned, owned, owned, attended, grad_owned, weights)


def unpack_kernel(dest_ref, blocks_ref, q_ref, k_ref, v_ref):
    rows = q_ref.shape[0]
    buffer_rows = blocks_ref.shape[0]
    select = (
        dest_ref[:, 0:1] == lax.broadcasted_iota(jnp.int32, (rows, buffer_rows), 1)
    ).astype(jnp.float32).astype(jnp.bfloat16)
    for place, out_ref in enumerate((q_ref, k_ref, v_ref)):
        part = blocks_ref[:, place * HEAD : (place + 1) * HEAD]
        out_ref[...] = dot32(select, part).astype(jnp.bfloat16)


def unpack_grads(dest_col, blocks, heads):
    rows = dest_col.shape[0]
    buffer_rows = blocks.shape[0]
    out = jax.ShapeDtypeStruct((rows, heads * HEAD), jnp.bfloat16)
    return pl.pallas_call(
        unpack_kernel,
        grid=(heads,),
        in_specs=[
            pl.BlockSpec((rows, HEAD), lambda h: (0, 0)),
            pl.BlockSpec((buffer_rows, 3 * HEAD), lambda h: (0, h)),
        ],
        out_specs=[pl.BlockSpec((rows, HEAD), lambda h: (0, h))] * 3,
        out_shape=(out, out, out),
        compiler_params=params(),
        cost_estimate=pl.CostEstimate(
            flops=6 * heads * rows * buffer_rows * HEAD,
            bytes_accessed=6 * heads * HEAD * (rows + buffer_rows),
            transcendentals=0,
        ),
    )(dest_col, blocks)


def exchange(matrix, seq_count):
    rows, cols = matrix.shape
    blocks = matrix.reshape(seq_count, rows // seq_count, cols)
    return lax.all_to_all(blocks, "seq", split_axis=0, concat_axis=0, tiled=True).reshape(rows, cols)


def body(queries, key_rows, values, out_weight, grad_out, labels, owner_map, pair_mask):
    seq_count = lax.axis_size("seq")
    row_count, width = queries.shape
    heads = width // HEAD
    slot_size = 2 * row_count // seq_count
    buffer_rows = seq_count * slot_size
    scale = HEAD ** (-0.5)
    chunk = 256
    full_weight = lax.all_gather(out_weight, "seq", axis=1, tiled=True)
    grad_full = lax.all_gather(grad_out, "tp", axis=1, tiled=True)
    packed, dest_row, dest_col = pack_inputs(
        seq_count, slot_size, labels, owner_map, queries, key_rows, values
    )
    owned = exchange(packed, seq_count)
    attended, weights = attention_forward(owned, pair_mask.astype(jnp.bfloat16), heads, scale, chunk)
    returned = exchange(attended, seq_count)
    grad_att = lax.dot_general(grad_full, full_weight, NT, preferred_element_type=jnp.float32).astype(
        jnp.bfloat16
    )
    place = jnp.arange(buffer_rows, dtype=jnp.int32)
    grad_packed = dot32((place[:, None] == dest_row).astype(jnp.bfloat16), grad_att).astype(jnp.bfloat16)
    grad_owned = exchange(grad_packed, seq_count)
    attended_local = dot32((dest_col[:, 0:1] == place[None, :]).astype(jnp.bfloat16), returned).astype(
        jnp.bfloat16
    )
    partial_out = dot32(attended_local, full_weight).astype(jnp.bfloat16)
    output = lax.psum_scatter(partial_out, "tp", scatter_dimension=1, tiled=True)
    grads = attention_backward(owned, attended, grad_owned, weights, heads, scale, chunk)
    back = exchange(grads, seq_count)
    grad_q, grad_k, grad_v = unpack_grads(dest_col, back, heads)
    return (output, grad_q, grad_k, grad_v)


def solution(mesh):
    in_specs = (
        P("seq", "tp"),
        P("seq", "tp"),
        P("seq", "tp"),
        P("tp", "seq"),
        P("seq", "tp"),
        P("seq"),
        P(),
        P(),
    )
    out_specs = (P("seq", "tp"), P("seq", "tp"), P("seq", "tp"), P("seq", "tp"))
    return jax.shard_map(body, mesh=mesh, in_specs=in_specs, out_specs=out_specs, check_vma=False)
```

time: 516 us -> 312 us (0.60)
  local copies, waits for them, and re-layouts: 80.3 us -> 16.4 us
  waiting for transfers between devices: 194 us -> 136 us
  matrix products: 71.4 us -> 17.6 us
  Pallas kernels: 0 us -> 31.6 us
  blocking collectives: 96.3 us -> 73.7 us
  other arithmetic: 15.9 us -> 0.03 us
  starting transfers between devices: 35.9 us -> 22.4 us
  loops' own time: 6.76 us -> 0 us
    dot_general x38 -> x2, matrix products: 71.4 us -> 17.6 us  [dot32(): return jnp.dot(left, right, preferred_element_type=jnp.float32)]
    all_gather x1, waiting for transfers between devices: 93.6 us -> 40 us  [body(): full_weight = lax.all_gather(out_weight, 'seq', axis=1, tiled=True)]
    pallas_call x0 -> x4, Pallas kernels: none -> 31.6 us  [the longest x1 13.4 us: attention_forward(): pl.pallas_call(lambda *refs: forward_kernel(scale, chunk, *refs), grid=(h...]
    gather x9 -> x0, local copies, waits for them, and re-layouts: 28.1 us -> none  [the longest x5 18.1 us: pack_rows(): matrix[source_row]]
    all_to_all x3 -> x1, blocking collectives: 96.3 us -> 73.7 us  [exchange(): lax.all_to_all(blocks, 'seq', split_axis=0, concat_axis=0, tiled=True)]
    another operation x8 -> x0, local copies, waits for them, and re-layouts: 14.5 us -> none  [the longest x1 3.57 us: body(): join_heads(stacked[2]).reshape(seq_count, slot_size, width_local)]
    all_to_all x6 -> x3, starting transfers between devices: 35.8 us -> 22.1 us  [exchange(): lax.all_to_all(blocks, 'seq', split_axis=0, concat_axis=0, tiled=True)]
    dynamic_slice x20 -> x0, local copies, waits for them, and re-layouts: 11.4 us -> none  [the longest x10 5.82 us: per_heads(): return lax.map(one_head, jnp.arange(head_total, dtype=jnp.int32))]
  transfers between devices with their start and end apart: 9 -> 6, of which waited for: 7 -> 3; matrix products, arithmetic and copies ran while one was open for 27% -> 8% of each run, Pallas kernels for 0% -> 10%
where the time goes in v1:
time: 312 us
  waiting for transfers between devices  136 us (44%)
  blocking collectives  73.7 us (24%)
  Pallas kernels  31.6 us (10%)
  starting transfers between devices  22.4 us (7%)
  matrix products  17.6 us (6%)
  local copies, waits for them, and re-layouts  16.4 us (5%)
  between operations  13.8 us (4%)
    all_to_all x3, waiting for transfers between devices, exchange(): lax.all_to_all(blocks, 'seq', split_axis=0, concat_axis=0, tiled=True)  94.5 us
    all_to_all x1, blocking collectives, exchange(): lax.all_to_all(blocks, 'seq', split_axis=0, concat_axis=0, tiled=True)  73.7 us
    all_gather x1, waiting for transfers between devices, body(): full_weight = lax.all_gather(out_weight, 'seq', axis=1, tiled=True)  40 us
    all_to_all x3, starting transfers between devices, exchange(): lax.all_to_all(blocks, 'seq', split_axis=0, concat_axis=0, tiled=True)  22.1 us
    dot_general x2, matrix products, dot32(): return jnp.dot(left, right, preferred_element_type=jnp.float32)  17.6 us
    unnamed x18, local copies, waits for them, and re-layouts  14.1 us
    pallas_call x1, Pallas kernels, attention_forward(): pl.pallas_call(lambda *refs: forward_kernel(scale, chunk, *refs), grid=(h...  13.4 us
    pallas_call x1, Pallas kernels, attention_backward(): pl.pallas_call(lambda *refs: backward_kernel(scale, chunk, *refs), grid=(...  11.5 us
  transfers between devices with their start and end apart: 6, of which 3 were waited for; matrix products, arithmetic and copies ran while one was open for 8% of the time, Pallas kernels for 10%

profile of v1, /device:TPU:4, one launch (start us, length us, event | category | flops | bytes accessed | tf_op | source)
XLA Modules:
  0.0 311.6 jit_solution(10478860086389062223)
XLA Ops:
  7.2 0.0 all-gather.5.cloned.1.call-start
  7.2 0.7 all-gather.5.cloned.1.call-update
  7.9 0.0 all-gather.3.cloned.1.call-start
  7.9 0.7 all-gather.3.cloned.1.call-update
  8.6 0.7 broadcast_in_dim.11.refs_0_
  9.3 0.8 broadcast_in_dim.14.refs_1_
  10.1 0.8 copy.16.refs_2_
  10.9 0.0 copy-start.4
  10.9 1.0 copy-done.4
  11.9 0.0 copy-start.5
  11.9 1.0 copy-done.5
  13.0 0.0 copy-start.6
  13.0 1.0 copy-done.6
  14.0 0.0 copy-start.7
  14.0 2.2 shard_map.111
  16.2 0.0 copy-start.3
  16.2 1.7 copy-done.3
  17.9 11.5 %all-to-all-start = ((bf16[32,24,2048]{2,1,0:T(8,128)(2,1)}), bf16[32,24,2048]{2,1,0:T(8,128)(2,1)S(1)}, u32[]{:S(2)}, u32[]{:S(2)}) async-start(bf16[32,24,2048]{2,1,0:T(8,128)(2,1)} %bitcast.25), calls=%async_computation | async-start | bytes 6291456 | tf_op jit(solution)/shard_map/all_to_all | solution.py:205
  29.4 0.0 copy-done.7
  29.5 82.3 %all-to-all-done = bf16[32,24,2048]{2,1,0:T(8,128)(2,1)S(1)} async-done(((bf16[32,24,2048]{2,1,0:T(8,128)(2,1)}), bf16[32,24,2048]{2,1,0:T(8,128)(2,1)S(1)}, u32[]{:S(2)}, u32[]{:S(2)}) %all-to-all-start) | async-done | bytes 3145760 | tf_op jit(solution)/shard_map/all_to_all | solution.py:205
  111.8 0.0 copy-start
  111.8 13.4 %shard_map.112 = (bf16[768,640]{1,0:T(8,128)(2,1)S(1)}, bf16[5,768,768]{2,1,0:T(8,128)(2,1)}) custom-call(bf16[768,2048]{1,0:T(8,128)(2,1)S(1)} %bitcast.15, bf16[768,2048]{1,0:T(8,128)(2,1)S(1)} %bitcast.16, bf16[768,2048]{1,0:T(8,128)(2,1)S(1)} %bitcast.17, bf16[768,2048]{1,0:T(8,128)(2,1)S(1)} %bitcast.18, bf16[128,128]{1,0:T(8,128)(2,1)S(1)} %convert_element_type.17.refs_4_), custom_call_target="tpu_custom_call" | custom-call | flops 1509949440 | bytes 9830400 | tf_op jit(solution)/shard_map/pallas_call | solution.py:116
  125.2 0.0 copy-done
  125.2 0.0 copy-start.1
  125.2 0.9 copy-done.1
  126.1 4.8 %all-to-all-start.1 = ((bf16[32,24,640]{2,1,0:T(8,128)(2,1)}), bf16[32,24,640]{2,1,0:T(8,128)(2,1)S(1)}, u32[]{:S(2)}, u32[]{:S(2)}) async-start(bf16[32,24,640]{2,1,0:T(8,128)(2,1)} %bitcast.23), calls=%async_computation.1 | async-start | bytes 1966080 | tf_op jit(solution)/shard_map/all_to_all | solution.py:205
  130.9 0.1 slice_reduce_fusion
  131.0 0.0 all-gather.5.cloned.1.call-done
  131.1 40.0 %all-gather.3.cloned.1.call-done = bf16[640,5120]{0,1:T(8,128)(2,1)} async-done(((bf16[640,160]{0,1:T(8,128)(2,1)}), bf16[640,5120]{0,1:T(8,128)(2,1)}) %all-gather.3.cloned.1.call-update) | async-done | bytes 6553616 | tf_op jit(solution)/shard_map/all_gather | solution.py:216
  171.0 9.2 %convolution_convert_fusion.1 = bf16[768,640]{1,0:T(8,128)(2,1)} fusion(bf16[384,5120]{1,0:T(8,128)(2,1)} %all-gather.5.cloned.1.call-done, bf16[640,5120]{0,1:T(8,128)(2,1)} %all-gather.3.cloned.1.call-done, s32[384]{0:T(512)S(1)} %reduce.1), kind=kOutput, calls=%fused_computation.1 | convolution fusion | flops 2895101952 | bytes 11470336 | tf_op jit(solution)/shard_map/dot_general | solution.py:15
  180.2 0.0 all-to-all-done.1
  180.2 5.9 %all-to-all-start.2 = ((bf16[32,24,640]{2,1,0:T(8,128)(2,1)}), bf16[32,24,640]{2,1,0:T(8,128)(2,1)S(1)}, u32[]{:S(2)}, u32[]{:S(2)}) async-start(bf16[32,24,640]{2,1,0:T(8,128)(2,1)} %bitcast.5), calls=%async_computation.2 | async-start | bytes 1966080 | tf_op jit(solution)/shard_map/all_to_all | solution.py:205
  186.1 0.2 reduce-scatter.4.cloned.1.call-start
  186.3 8.5 %convolution_convert_fusion = bf16[384,5120]{1,0:T(8,128)(2,1)} fusion(bf16[640,5120]{0,1:T(8,128)(2,1)} %all-gather.3.cloned.1.call-done, bf16[768,640]{1,0:T(8,128)(2,1)S(1)} %bitcast.28, s32[384]{0:T(512)S(1)} %slice_reduce_fusion), kind=kOutput, calls=%fused_computation | convolution fusion | flops 2896576512 | bytes 11470336 | tf_op jit(solution)/shard_map/dot_general | solution.py:15
  194.8 6.3 %copy.17 = bf16[384,5120]{0,1:T(8,128)(2,1)} copy(bf16[384,5120]{1,0:T(8,128)(2,1)} %convolution_convert_fusion) | data formatting | bytes 7864320
  201.1 0.0 copy-start.2
  201.1 0.0 reduce-scatter.4.cloned.1.call-update
  201.1 12.2 %all-to-all-done.2 = bf16[32,24,640]{2,1,0:T(8,128)(2,1)S(1)} async-done(((bf16[32,24,640]{2,1,0:T(8,128)(2,1)}), bf16[32,24,640]{2,1,0:T(8,128)(2,1)S(1)}, u32[]{:S(2)}, u32[]{:S(2)}) %all-to-all-start.2) | async-done | bytes 983072 | tf_op jit(solution)/shard_map/all_to_all | solution.py:205
  213.3 0.0 copy-done.2
  213.3 11.5 %shard_map.113 = bf16[768,1920]{1,0:T(8,128)(2,1)S(1)} custom-call(bf16[768,2048]{1,0:T(8,128)(2,1)} %bitcast.19, bf16[768,2048]{1,0:T(8,128)(2,1)} %bitcast.20, bf16[768,2048]{1,0:T(8,128)(2,1)} %bitcast.21, bf16[768,640]{1,0:T(8,128)(2,1)S(1)} %copy-done.2, bf16[768,640]{1,0:T(8,128)(2,1)S(1)} %bitcast.24, bf16[5,768,768]{2,1,0:T(8,128)(2,1)} %get-tuple-element.16.refs_5_), custom_call_target="tpu_custom_call" | custom-call | flops 3019898880 | bytes 13762560 | tf_op jit(solution)/shard_map/pallas_call | solution.py:147
  224.8 73.7 %all_to_all.20 = bf16[32,24,1920]{2,1,0:T(8,128)(2,1)S(1)} all-to-all(bf16[32,24,1920]{2,1,0:T(8,128)(2,1)S(1)} %bitcast.22), channel_id=1, replica_groups=mesh['seq'=32,'tp'=8] {'seq'}, dimensions={0} | all-to-all | bytes 5898240 | tf_op jit(solution)/shard_map/all_to_all | solution.py:205
  298.5 4.5 %shard_map.114 = (bf16[384,640]{1,0:T(8,128)(2,1)}, bf16[384,640]{1,0:T(8,128)(2,1)}, bf16[384,640]{1,0:T(8,128)(2,1)}) custom-call(s32[384,128]{1,0:T(8,128)S(1)} %get-tuple-element.12.dest_ref, bf16[768,1920]{1,0:T(8,128)(2,1)S(1)} %bitcast.26), custom_call_target="tpu_custom_call" | custom-call | flops 1132462080 | bytes 4423680 | tf_op jit(solution)/shard_map/pallas_call | solution.py:184
  303.0 0.0 reduce-scatter.4.cloned.1.call-done
  303.0 2.0 copy.18
  (2 shorter events, 0.0 us)
Async XLA Ops:
  7.2 123.9 %all-gather.5.cloned.1.call-start = ((), (), s32[]{:S(2)}) async-start(), calls=%async_computation.6 | async-start | bytes 4423680 | tf_op jit(solution)/shard_map/all_gather | solution.py:217
  7.9 163.1 %all-gather.3.cloned.1.call-start = ((), (), s32[]{:S(2)}) async-start(), calls=%async_computation.5 | async-start | bytes 6758400 | tf_op jit(solution)/shard_map/all_gather | solution.py:216
  10.9 1.0 copy-start.4
  11.9 1.0 copy-start.5
  13.0 1.0 copy-start.6
  14.0 15.5 %copy-start.7 = (s32[128,128]{1,0:T(8,128)S(1)}, s32[128,128]{1,0:T(8,128)}, u32[]{:S(2)}) copy-start(s32[128,128]{1,0:T(8,128)} %param.15) | copy-start | bytes 196612
  16.2 1.7 copy-start.3
  17.9 93.8 %all-to-all-start = ((bf16[32,24,2048]{2,1,0:T(8,128)(2,1)}), bf16[32,24,2048]{2,1,0:T(8,128)(2,1)S(1)}, u32[]{:S(2)}, u32[]{:S(2)}) async-start(bf16[32,24,2048]{2,1,0:T(8,128)(2,1)} %bitcast.25), calls=%async_computation | async-start | bytes 6291456 | tf_op jit(solution)/shard_map/all_to_all | solution.py:205
  111.8 13.4 %copy-start = (bf16[32,24,2048]{2,1,0:T(8,128)(2,1)}, bf16[32,24,2048]{2,1,0:T(8,128)(2,1)S(1)}, u32[]{:S(2)}) copy-start(bf16[32,24,2048]{2,1,0:T(8,128)(2,1)S(1)} %all-to-all-done) | copy-start | bytes 9437188
  125.2 0.9 copy-start.1
  126.1 54.1 %all-to-all-start.1 = ((bf16[32,24,640]{2,1,0:T(8,128)(2,1)}), bf16[32,24,640]{2,1,0:T(8,128)(2,1)S(1)}, u32[]{:S(2)}, u32[]{:S(2)}) async-start(bf16[32,24,640]{2,1,0:T(8,128)(2,1)} %bitcast.23), calls=%async_computation.1 | async-start | bytes 1966080 | tf_op jit(solution)/shard_map/all_to_all | solution.py:205
  180.2 33.1 %all-to-all-start.2 = ((bf16[32,24,640]{2,1,0:T(8,128)(2,1)}), bf16[32,24,640]{2,1,0:T(8,128)(2,1)S(1)}, u32[]{:S(2)}, u32[]{:S(2)}) async-start(bf16[32,24,640]{2,1,0:T(8,128)(2,1)} %bitcast.5), calls=%async_computation.2 | async-start | bytes 1966080 | tf_op jit(solution)/shard_map/all_to_all | solution.py:205
  186.1 116.9 %reduce-scatter.4.cloned.1.call-start = ((), (), s32[]{:S(2)}) async-start(), calls=%async_computation.7 | async-start | bytes 4423680
  201.1 12.2 %copy-start.2 = (bf16[768,640]{1,0:T(8,128)(2,1)S(1)}, bf16[768,640]{1,0:T(8,128)(2,1)}, u32[]{:S(2)}) copy-start(bf16[768,640]{1,0:T(8,128)(2,1)} %copy-done.1) | copy-start | bytes 2949124
Sparse Core Ops, SparseCore 0:
  9.8 35.1 all-gather.4
  47.6 123.4 all-gather.2
  201.2 36.3 reduce-scatter.3

commit v2 on v1

--- a/solution.py
+++ b/solution.py
@@ -23,31 +23,37 @@
     return pltpu.CompilerParams(vmem_limit_bytes=VMEM_BYTES)
 
 
-def pack_kernel(seq_count, slot_size, label_row, label_col, owner_col, q_ref, k_ref, v_ref, packed, dest_row, dest_col):
-    rows = q_ref.shape[0]
-    cols = q_ref.shape[1]
-    clusters = owner_col.shape[0]
+def as_bf16(flags):
+    return flags.astype(jnp.float32).astype(jnp.bfloat16)
+
+
+def column_of(row):
+    wide = jnp.broadcast_to(row.astype(jnp.float32), (HEAD, row.shape[1]))
+    return jnp.transpose(wide)
+
+
+def pack_kernel(seq_count, slot_size, label_row, owner_row_ref, q_ref, k_ref, v_ref, packed, dest_row, dest_col):
+    rows, cols = q_ref.shape
+    clusters = owner_row_ref.shape[1]
     buffer_rows = packed.shape[0]
-    in_cluster = label_row[...] == lax.broadcasted_iota(jnp.int32, (clusters, rows), 0)
-    owner_row = jnp.sum(jnp.where(in_cluster, owner_col[...], 0), axis=0, keepdims=True)
+    labels = label_row[...]
+    owner_col = column_of(owner_row_ref[...])[:, 0:1].astype(jnp.int32)
+    in_cluster = labels == lax.broadcasted_iota(jnp.int32, (clusters, rows), 0)
+    owner_row = jnp.sum(jnp.where(in_cluster, owner_col, 0), axis=0, keepdims=True)
     owned = owner_row == lax.broadcasted_iota(jnp.int32, (seq_count, rows), 0)
     earlier = lax.broadcasted_iota(jnp.int32, (rows, rows), 0) < lax.broadcasted_iota(
         jnp.int32, (rows, rows), 1
     )
-    before = dot32(
-        owned.astype(jnp.float32).astype(jnp.bfloat16), earlier.astype(jnp.float32).astype(jnp.bfloat16)
-    )
+    before = dot32(as_bf16(owned), as_bf16(earlier))
     rank_row = jnp.sum(jnp.where(owned, before, 0.0), axis=0, keepdims=True)
     dest = owner_row * slot_size + rank_row.astype(jnp.int32)
     dest_row[...] = dest
-    wide = jnp.broadcast_to(dest.astype(jnp.float32), (HEAD, rows))
-    dest_col[...] = jnp.transpose(wide).astype(jnp.int32)
-    select = (lax.broadcasted_iota(jnp.int32, (buffer_rows, rows), 0) == dest).astype(jnp.float32).astype(jnp.bfloat16)
+    dest_col[...] = column_of(dest).astype(jnp.int32)
+    select = as_bf16(lax.broadcasted_iota(jnp.int32, (buffer_rows, rows), 0) == dest)
     packed[:, 0:cols] = dot32(select, q_ref[...]).astype(jnp.bfloat16)
     packed[:, cols : 2 * cols] = dot32(select, k_ref[...]).astype(jnp.bfloat16)
     packed[:, 2 * cols : 3 * cols] = dot32(select, v_ref[...]).astype(jnp.bfloat16)
-    codes = jnp.broadcast_to((label_col[...] + 1).astype(jnp.float32), (rows, HEAD)).astype(jnp.bfloat16)
-    packed[:, 3 * cols :] = dot32(select, codes).astype(jnp.bfloat16)
+    packed[:, 3 * cols :] = dot32(select, column_of(labels + 1).astype(jnp.bfloat16)).astype(jnp.bfloat16)
 
 
 def pack_inputs(seq_count, slot_size, labels, owner_map, queries, key_rows, values):
@@ -61,7 +67,92 @@
             jax.ShapeDtypeStruct((rows, HEAD), jnp.int32),
         ),
         compiler_params=params(),
-    )(labels[None, :], labels[:, None], owner_map[:, None], queries, key_rows, values)
+    )(labels[None, :], owner_map[None, :], queries, key_rows, values)
+
+
+def grad_kernel(order_ref, grad_ref, weight_ref, dest_row, packed, total):
+    step = pl.program_id(0)
+
+    @pl.when(step == 0)
+    def _():
+        total[...] = jnp.zeros_like(total)
+
+    total[...] += dot32(grad_ref[0], weight_ref[...])
+
+    @pl.when(step == pl.num_programs(0) - 1)
+    def _():
+        select = as_bf16(lax.broadcasted_iota(jnp.int32, (packed.shape[0], total.shape[0]), 0) == dest_row[...])
+        packed[...] = dot32(select, total[...].astype(jnp.bfloat16)).astype(jnp.bfloat16)
+
+
+def project_grads(order, grad_blocks, weight_t, dest_row, buffer_rows):
+    groups, rows, width = grad_blocks.shape
+    return pl.pallas_call(
+        grad_kernel,
+        grid_spec=pltpu.PrefetchScalarGridSpec(
+            num_scalar_prefetch=1,
+            grid=(groups,),
+            in_specs=[
+                pl.BlockSpec((1, rows, width), lambda g, order: (g, 0, 0)),
+                pl.BlockSpec((width, width), lambda g, order: (order[g], 0)),
+                pl.BlockSpec((1, rows), lambda g, order: (0, 0)),
+            ],
+            out_specs=pl.BlockSpec((buffer_rows, width), lambda g, order: (0, 0)),
+            scratch_shapes=[pltpu.VMEM((rows, width), jnp.float32)],
+        ),
+        out_shape=jax.ShapeDtypeStruct((buffer_rows, width), jnp.bfloat16),
+        compiler_params=params(),
+        cost_estimate=pl.CostEstimate(
+            flops=2 * groups * rows * width * width + 2 * buffer_rows * rows * width,
+            bytes_accessed=2 * groups * width * (rows + width),
+            transcendentals=0,
+        ),
+    )(order, grad_blocks, weight_t, dest_row)
+
+
+def output_kernel(dest_col, returned, weight_ref, out_ref, local):
+    @pl.when(pl.program_id(0) == 0)
+    def _():
+        place = lax.broadcasted_iota(jnp.int32, (local.shape[0], returned.shape[0]), 1)
+        local[...] = dot32(as_bf16(dest_col[:, 0:1] == place), returned[...]).astype(jnp.bfloat16)
+
+    out_ref[0] = dot32_nt(local[...], weight_ref[...]).astype(jnp.bfloat16)
+
+
+def project_output(dest_col, returned, weight_t, groups):
+    rows = dest_col.shape[0]
+    buffer_rows, width = returned.shape
+    return pl.pallas_call(
+        output_kernel,
+        grid=(groups,),
+        in_specs=[
+            pl.BlockSpec((rows, HEAD), lambda g: (0, 0)),
+            pl.BlockSpec((buffer_rows, width), lambda g: (0, 0)),
+            pl.BlockSpec((width, width), lambda g: (g, 0)),
+        ],
+        out_specs=pl.BlockSpec((1, rows, width), lambda g: (g, 0, 0)),
+        out_shape=jax.ShapeDtypeStruct((groups, rows, width), jnp.bfloat16),
+        scratch_shapes=[pltpu.VMEM((rows, width), jnp.bfloat16)],
+        compiler_params=params(),
+        cost_estimate=pl.CostEstimate(
+            flops=2 * groups * rows * width * width + 2 * buffer_rows * rows * width,
+            bytes_accessed=2 * groups * width * (rows + width),
+            transcendentals=0,
+        ),
+    )(dest_col, returned, weight_t)
+
+
+def gather_groups(block):
+    tp_count = lax.axis_size("tp")
+    half = tp_count // 2
+    near = [block]
+    for shift in range(1, half):
+        near.append(lax.ppermute(block, "tp", [(t, (t + 2 * shift) % tp_count) for t in range(tp_count)]))
+    near = jnp.stack(near)
+    far = lax.ppermute(near, "tp", [(t, t ^ 1) for t in range(tp_count)])
+    me = lax.axis_index("tp")
+    own = (me + tp_count - 2 * jnp.arange(half, dtype=jnp.int32)) % tp_count
+    return jnp.concatenate([near, far], axis=0), jnp.concatenate([own, own ^ 1])
 
 
 def forward_kernel(scale, chunk, q_ref, k_ref, v_ref, code_ref, mask_ref, att_ref, weight_ref, bias):
@@ -70,7 +161,7 @@
     @pl.when(pl.program_id(0) == 0)
     def _():
         lane = lax.broadcasted_iota(jnp.int32, (rows, HEAD), 1).astype(jnp.float32) + 1.0
-        onehot = (code_ref[...].astype(jnp.float32) == lane).astype(jnp.float32).astype(jnp.bfloat16)
+        onehot = as_bf16(code_ref[...].astype(jnp.float32) == lane)
         linked = dot32(onehot, mask_ref[...]).astype(jnp.bfloat16)
         for start in range(0, rows, chunk):
             linked_part = linked[start : start + chunk]
@@ -169,9 +260,7 @@
 def unpack_kernel(dest_ref, blocks_ref, q_ref, k_ref, v_ref):
     rows = q_ref.shape[0]
     buffer_rows = blocks_ref.shape[0]
-    select = (
-        dest_ref[:, 0:1] == lax.broadcasted_iota(jnp.int32, (rows, buffer_rows), 1)
-    ).astype(jnp.float32).astype(jnp.bfloat16)
+    select = as_bf16(dest_ref[:, 0:1] == lax.broadcasted_iota(jnp.int32, (rows, buffer_rows), 1))
     for place, out_ref in enumerate((q_ref, k_ref, v_ref)):
         part = blocks_ref[:, place * HEAD : (place + 1) * HEAD]
         out_ref[...] = dot32(select, part).astype(jnp.bfloat16)
@@ -213,25 +302,17 @@
     buffer_rows = seq_count * slot_size
     scale = HEAD ** (-0.5)
     chunk = 256
-    full_weight = lax.all_gather(out_weight, "seq", axis=1, tiled=True)
-    grad_full = lax.all_gather(grad_out, "tp", axis=1, tiled=True)
+    weight_t = lax.all_gather(out_weight.T, "seq", axis=0, tiled=True)
+    grad_blocks, order = gather_groups(grad_out)
     packed, dest_row, dest_col = pack_inputs(
         seq_count, slot_size, labels, owner_map, queries, key_rows, values
     )
     owned = exchange(packed, seq_count)
     attended, weights = attention_forward(owned, pair_mask.astype(jnp.bfloat16), heads, scale, chunk)
     returned = exchange(attended, seq_count)
-    grad_att = lax.dot_general(grad_full, full_weight, NT, preferred_element_type=jnp.float32).astype(
-        jnp.bfloat16
-    )
-    place = jnp.arange(buffer_rows, dtype=jnp.int32)
-    grad_packed = dot32((place[:, None] == dest_row).astype(jnp.bfloat16), grad_att).astype(jnp.bfloat16)
-    grad_owned = exchange(grad_packed, seq_count)
-    attended_local = dot32((dest_col[:, 0:1] == place[None, :]).astype(jnp.bfloat16), returned).astype(
-        jnp.bfloat16
-    )
-    partial_out = dot32(attended_local, full_weight).astype(jnp.bfloat16)
-    output = lax.psum_scatter(partial_out, "tp", scatter_dimension=1, tiled=True)
+    grad_owned = exchange(project_grads(order, grad_blocks, weight_t, dest_row, buffer_rows), seq_count)
+    partial_out = project_output(dest_col, returned, weight_t, lax.axis_size("tp"))
+    output = lax.psum_scatter(partial_out, "tp", scatter_dimension=0, tiled=False)
     grads = attention_backward(owned, attended, grad_owned, weights, heads, scale, chunk)
     back = exchange(grads, seq_count)
     grad_q, grad_k, grad_v = unpack_grads(dest_col, back, heads)

time: 312 us -> 296 us (0.949)
  waiting for transfers between devices: 136 us -> 108 us
  Pallas kernels: 31.6 us -> 50.4 us
  matrix products: 17.6 us -> 0 us
  starting transfers between devices: 22.4 us -> 28.3 us
    all_gather x2 -> x1, waiting for transfers between devices: 40 us -> 0.01 us  [body(): weight_t = lax.all_gather(out_weight.T, 'seq', axis=0, tiled=True)]
    ppermute x0 -> x4, waiting for transfers between devices: none -> 22.1 us  [the longest x3 22.1 us: gather_groups(): lax.ppermute(block, 'tp', [(t, (t + 2 * shift) % tp_count) for t in range...]
    pallas_call x0 -> x2, Pallas kernels: none -> 18.8 us  [the longest x1 10.2 us: project_grads(): pl.pallas_call(grad_kernel, grid_spec=pltpu.PrefetchScalarGridSpec(num_sc...]
    dot_general x2 -> x0, matrix products: 17.6 us -> none  [dot32(): return jnp.dot(left, right, preferred_element_type=jnp.float32)]
    all_to_all x3, waiting for transfers between devices: 94.5 us -> 85.4 us  [exchange(): lax.all_to_all(blocks, 'seq', split_axis=0, concat_axis=0, tiled=True)]
    ppermute x0 -> x4, starting transfers between devices: none -> 3.22 us  [the longest x3 3.22 us: gather_groups(): lax.ppermute(block, 'tp', [(t, (t + 2 * shift) % tp_count) for t in range...]
    unnamed x18 -> x38, local copies, waits for them, and re-layouts: 14.1 us -> 14.6 us
  transfers between devices with their start and end apart: 6 -> 9, of which waited for: 3 -> 6; matrix products, arithmetic and copies ran while one was open for 8% -> 3% of each run, Pallas kernels for 10% -> 17%
where the time goes in v2:
time: 296 us; the launch traced here: 295 us
  waiting for transfers between devices  108 us (36%)
  blocking collectives  73.8 us (25%)
  Pallas kernels  50.4 us (17%)
  starting transfers between devices  28.3 us (10%)
  local copies, waits for them, and re-layouts  17.1 us (6%)
  between operations  14.2 us (5%)
    all_to_all x3, waiting for transfers between devices, exchange(): lax.all_to_all(blocks, 'seq', split_axis=0, concat_axis=0, tiled=True)  85.4 us
    all_to_all x1, blocking collectives, exchange(): lax.all_to_all(blocks, 'seq', split_axis=0, concat_axis=0, tiled=True)  73.8 us
    all_to_all x3, starting transfers between devices, exchange(): lax.all_to_all(blocks, 'seq', split_axis=0, concat_axis=0, tiled=True)  24.8 us
    ppermute x3, waiting for transfers between devices, gather_groups(): lax.ppermute(block, 'tp', [(t, (t + 2 * shift) % tp_count) for t in range...  22.1 us
    unnamed x38, local copies, waits for them, and re-layouts  14.6 us
    pallas_call x1, Pallas kernels, attention_forward(): pl.pallas_call(lambda *refs: forward_kernel(scale, chunk, *refs), grid=(h...  13.4 us
    pallas_call x1, Pallas kernels, attention_backward(): pl.pallas_call(lambda *refs: backward_kernel(scale, chunk, *refs), grid=(...  11.4 us
    pallas_call x1, Pallas kernels, project_grads(): pl.pallas_call(grad_kernel, grid_spec=pltpu.PrefetchScalarGridSpec(num_sc...  10.2 us
  transfers between devices with their start and end apart: 9, of which 6 were waited for; matrix products, arithmetic and copies ran while one was open for 3% of the time, Pallas kernels for 17%

profile of v2, /device:TPU:4, one launch (start us, length us, event | category | flops | bytes accessed | tf_op | source)
XLA Modules:
  0.0 294.9 jit_solution(12133817720357394585)
XLA Ops:
  7.2 0.0 all-gather.2.cloned.1.call-start
  7.2 0.7 all-gather.2.cloned.1.call-update
  7.9 0.7 broadcast_in_dim.6.refs_0_
  8.6 1.0 copy-done.7
  9.6 1.0 copy-done.8
  10.6 1.0 copy-done.9
  11.7 0.7 copy-done.10
  12.3 2.3 shard_map.111
  14.7 0.0 copy-start.6
  14.7 1.7 copy-done.6
  16.4 11.6 %all-to-all-start = ((bf16[32,24,2048]{2,1,0:T(8,128)(2,1)}), bf16[32,24,2048]{2,1,0:T(8,128)(2,1)S(1)}, u32[]{:S(2)}, u32[]{:S(2)}) async-start(bf16[32,24,2048]{2,1,0:T(8,128)(2,1)} %bitcast.30), calls=%async_computation | async-start | bytes 6291456 | tf_op jit(solution)/shard_map/all_to_all | solution.py:294
  28.0 1.3 collective-permute-start
  29.3 0.8 collective-permute-start.1
  30.1 1.1 collective-permute-start.2
  31.2 11.2 %collective-permute-done = bf16[384,640]{1,0:T(8,128)(2,1)S(1)} collective-permute-done((bf16[384,640]{1,0:T(8,128)(2,1)}, bf16[384,640]{1,0:T(8,128)(2,1)S(1)}, u32[]{:S(2)}, u32[]{:S(2)}) %collective-permute-start) | collective-permute-done | bytes 491552 | tf_op jit(solution)/shard_map/ppermute | solution.py:150
  42.5 9.1 %collective-permute-done.1 = bf16[384,640]{1,0:T(8,128)(2,1)S(1)} collective-permute-done((bf16[384,640]{1,0:T(8,128)(2,1)}, bf16[384,640]{1,0:T(8,128)(2,1)S(1)}, u32[]{:S(2)}, u32[]{:S(2)}) %collective-permute-start.1) | collective-permute-done | bytes 491552 | tf_op jit(solution)/shard_map/ppermute | solution.py:150
  51.5 1.8 collective-permute-done.2
  53.3 2.8 pad_maximum_fusion
  56.1 0.0 collective-permute-start.3
  56.1 0.0 copy-done.11
  56.1 0.0 copy-done.12
  56.1 0.0 copy-done.14
  56.2 0.0 copy-done.16
  56.2 60.5 %all-to-all-done = bf16[32,24,2048]{2,1,0:T(8,128)(2,1)S(1)} async-done(((bf16[32,24,2048]{2,1,0:T(8,128)(2,1)}), bf16[32,24,2048]{2,1,0:T(8,128)(2,1)S(1)}, u32[]{:S(2)}, u32[]{:S(2)}) %all-to-all-start) | async-done | bytes 3145760 | tf_op jit(solution)/shard_map/all_to_all | solution.py:294
  116.7 13.4 %shard_map.112 = (bf16[768,640]{1,0:T(8,128)(2,1)S(1)}, bf16[5,768,768]{2,1,0:T(8,128)(2,1)}) custom-call(bf16[768,2048]{1,0:T(8,128)(2,1)S(1)} %bitcast.19, bf16[768,2048]{1,0:T(8,128)(2,1)S(1)} %bitcast.20, bf16[768,2048]{1,0:T(8,128)(2,1)S(1)} %bitcast.21, bf16[768,2048]{1,0:T(8,128)(2,1)S(1)} %bitcast.22, bf16[128,128]{1,0:T(8,128)(2,1)S(1)} %convert_element_type.3.refs_4_), custom_call_target="tpu_custom_call" | custom-call | flops 1509949440 | bytes 9830400 | tf_op jit(solution)/shard_map/pallas_call | solution.py:207
  130.1 1.0 copy-done.4
  131.1 8.3 %all-to-all-start.1 = ((bf16[32,24,640]{2,1,0:T(8,128)(2,1)}), bf16[32,24,640]{2,1,0:T(8,128)(2,1)S(1)}, u32[]{:S(2)}, u32[]{:S(2)}) async-start(bf16[32,24,640]{2,1,0:T(8,128)(2,1)} %bitcast.27), calls=%async_computation.1 | async-start | bytes 1966080 | tf_op jit(solution)/shard_map/all_to_all | solution.py:294
  139.5 0.1 pad_add_fusion.order_ref
  139.5 1.1 constant_dynamic-update-slice_fusion.4
  140.6 1.1 constant_dynamic-update-slice_fusion.3
  141.7 0.1 constant_dynamic-update-slice_fusion.2
  141.8 0.1 constant_dynamic-update-slice_fusion.1
  141.9 0.0 collective-permute-done.3
  141.9 1.9 constant_dynamic-update-slice_fusion.grad_ref
  143.8 0.0 copy-start.2
  143.8 1.8 copy-done.2
  145.6 2.1 copy-done.3
  147.7 10.2 %shard_map.114 = bf16[768,640]{1,0:T(8,128)(2,1)} custom-call(s32[8]{0:T(128)S(1)} %pad_add_fusion.order_ref, bf16[8,384,640]{2,1,0:T(8,128)(2,1)S(1)} %copy-done.3, bf16[5120,640]{1,0:T(8,128)(2,1)} %all-gather.2.cloned.1.call-done.weight_ref, s32[1,384]{1,0:T(1,128)S(1)} %get-tuple-element.15.dest_row), custom_call_target="tpu_custom_call" | custom-call | flops 2894069760 | bytes 10485760 | tf_op jit(solution)/shard_map/pallas_call | solution.py:90
  157.9 8.6 %all-to-all-done.1 = bf16[32,24,640]{2,1,0:T(8,128)(2,1)S(1)} async-done(((bf16[32,24,640]{2,1,0:T(8,128)(2,1)}), bf16[32,24,640]{2,1,0:T(8,128)(2,1)S(1)}, u32[]{:S(2)}, u32[]{:S(2)}) %all-to-all-start.1) | async-done | bytes 983072 | tf_op jit(solution)/shard_map/all_to_all | solution.py:294
  166.5 4.8 %all-to-all-start.2 = ((bf16[32,24,640]{2,1,0:T(8,128)(2,1)}), bf16[32,24,640]{2,1,0:T(8,128)(2,1)S(1)}, u32[]{:S(2)}, u32[]{:S(2)}) async-start(bf16[32,24,640]{2,1,0:T(8,128)(2,1)} %bitcast.11), calls=%async_computation.3 | async-start | bytes 1966080 | tf_op jit(solution)/shard_map/all_to_all | solution.py:294
  171.4 0.2 reduce-scatter.2.cloned.1.call-start
  171.6 8.6 %shard_map.113 = bf16[8,384,640]{2,1,0:T(8,128)(2,1)S(1)} custom-call(s32[384,128]{1,0:T(8,128)S(1)} %get-tuple-element.12.dest_col.dest_ref, bf16[768,640]{1,0:T(8,128)(2,1)S(1)} %bitcast.28, bf16[5120,640]{1,0:T(8,128)(2,1)} %all-gather.2.cloned.1.call-done.weight_ref), custom_call_target="tpu_custom_call" | custom-call | flops 2894069760 | bytes 10485760 | tf_op jit(solution)/shard_map/pallas_call | solution.py:125
  180.2 1.9 copy-done.1
  182.1 0.0 reduce-scatter.2.cloned.1.call-update
  182.1 16.3 %all-to-all-done.2 = bf16[32,24,640]{2,1,0:T(8,128)(2,1)S(1)} async-done(((bf16[32,24,640]{2,1,0:T(8,128)(2,1)}), bf16[32,24,640]{2,1,0:T(8,128)(2,1)S(1)}, u32[]{:S(2)}, u32[]{:S(2)}) %all-to-all-start.2) | async-done | bytes 983072 | tf_op jit(solution)/shard_map/all_to_all | solution.py:294
  198.4 11.4 %shard_map.115 = bf16[768,1920]{1,0:T(8,128)(2,1)S(1)} custom-call(bf16[768,2048]{1,0:T(8,128)(2,1)} %bitcast.23, bf16[768,2048]{1,0:T(8,128)(2,1)} %bitcast.24, bf16[768,2048]{1,0:T(8,128)(2,1)} %bitcast.25, bf16[768,640]{1,0:T(8,128)(2,1)S(1)} %copy-done.5, bf16[768,640]{1,0:T(8,128)(2,1)S(1)} %bitcast.29, bf16[5,768,768]{2,1,0:T(8,128)(2,1)} %get-tuple-element.16.refs_5_), custom_call_target="tpu_custom_call" | custom-call | flops 3019898880 | bytes 13762560 | tf_op jit(solution)/shard_map/pallas_call | solution.py:238
  209.8 73.8 %all_to_all.20 = bf16[32,24,1920]{2,1,0:T(8,128)(2,1)S(1)} all-to-all(bf16[32,24,1920]{2,1,0:T(8,128)(2,1)S(1)} %bitcast.26), channel_id=1, replica_groups=mesh['seq'=32,'tp'=8] {'seq'}, dimensions={0} | all-to-all | bytes 5898240 | tf_op jit(solution)/shard_map/all_to_all | solution.py:294
  283.6 4.5 %shard_map.116 = (bf16[384,640]{1,0:T(8,128)(2,1)}, bf16[384,640]{1,0:T(8,128)(2,1)}, bf16[384,640]{1,0:T(8,128)(2,1)}) custom-call(s32[384,128]{1,0:T(8,128)S(1)} %get-tuple-element.12.dest_col.dest_ref, bf16[768,1920]{1,0:T(8,128)(2,1)S(1)} %bitcast.31), custom_call_target="tpu_custom_call" | custom-call | flops 1132462080 | bytes 4423680 | tf_op jit(solution)/shard_map/pallas_call | solution.py:273
  (23 shorter events, 0.1 us)
Async XLA Ops:
  7.2 138.5 %all-gather.2.cloned.1.call-start = ((), (), s32[]{:S(2)}) async-start(), calls=%async_computation.5 | async-start | bytes 6758400 | tf_op jit(solution)/shard_map/all_gather | solution.py:305
  8.6 1.0 copy-start.7
  9.6 1.0 copy-start.8
  10.6 1.0 copy-start.9
  11.7 0.7 copy-start.10
  14.7 1.7 copy-start.6
  16.4 39.8 %copy-start.16 = (s32[128,128]{1,0:T(8,128)S(1)}, s32[128,128]{1,0:T(8,128)}, u32[]{:S(2)}) copy-start(s32[128,128]{1,0:T(8,128)} %param.15) | copy-start | bytes 196612
  16.4 100.3 %all-to-all-start = ((bf16[32,24,2048]{2,1,0:T(8,128)(2,1)}), bf16[32,24,2048]{2,1,0:T(8,128)(2,1)S(1)}, u32[]{:S(2)}, u32[]{:S(2)}) async-start(bf16[32,24,2048]{2,1,0:T(8,128)(2,1)} %bitcast.30), calls=%async_computation | async-start | bytes 6291456 | tf_op jit(solution)/shard_map/all_to_all | solution.py:294
  28.0 14.4 %collective-permute-start = (bf16[384,640]{1,0:T(8,128)(2,1)}, bf16[384,640]{1,0:T(8,128)(2,1)S(1)}, u32[]{:S(2)}, u32[]{:S(2)}) collective-permute-start(bf16[384,640]{1,0:T(8,128)(2,1)} %param.12), channel_id=1, source_target_pairs={{0,2},{1,3},{2,4},{3,5},{4,6},{5,7},{6,0},{7,1},{8,10},{9,11},{10,... | collective-permute-start | bytes 1474568 | tf_op jit(solution)/shard_map/ppermute | solution.py:150
  29.3 22.2 %collective-permute-start.1 = (bf16[384,640]{1,0:T(8,128)(2,1)}, bf16[384,640]{1,0:T(8,128)(2,1)S(1)}, u32[]{:S(2)}, u32[]{:S(2)}) collective-permute-start(bf16[384,640]{1,0:T(8,128)(2,1)} %param.12), channel_id=1, source_target_pairs={{0,4},{1,5},{2,6},{3,7},{4,0},{5,1},{6,2},{7,3},{8,12},{9,13},{10,... | collective-permute-start | bytes 1474568 | tf_op jit(solution)/shard_map/ppermute | solution.py:150
  30.1 23.3 %collective-permute-start.2 = (bf16[384,640]{1,0:T(8,128)(2,1)}, bf16[384,640]{1,0:T(8,128)(2,1)S(1)}, u32[]{:S(2)}, u32[]{:S(2)}) collective-permute-start(bf16[384,640]{1,0:T(8,128)(2,1)} %param.12), channel_id=1, source_target_pairs={{0,6},{1,7},{2,0},{3,1},{4,2},{5,3},{6,4},{7,5},{8,14},{9,15},{10,... | collective-permute-start | bytes 1474568 | tf_op jit(solution)/shard_map/ppermute | solution.py:150
  42.5 13.7 %copy-start.11 = (bf16[384,640]{1,0:T(8,128)(2,1)}, bf16[384,640]{1,0:T(8,128)(2,1)S(1)}, u32[]{:S(2)}) copy-start(bf16[384,640]{1,0:T(8,128)(2,1)S(1)} %collective-permute-done) | copy-start | bytes 1474564
  51.5 4.6 %copy-start.12 = (bf16[384,640]{1,0:T(8,128)(2,1)}, bf16[384,640]{1,0:T(8,128)(2,1)S(1)}, u32[]{:S(2)}) copy-start(bf16[384,640]{1,0:T(8,128)(2,1)S(1)} %collective-permute-done.1) | copy-start | bytes 1474564
  53.3 2.8 copy-start.14
  56.1 85.7 %collective-permute-start.3 = (bf16[4,384,640]{2,1,0:T(8,128)(2,1)}, bf16[4,384,640]{2,1,0:T(8,128)(2,1)}, u32[]{:S(2)}, u32[]{:S(2)}) collective-permute-start(bf16[4,384,640]{2,1,0:T(8,128)(2,1)} %pad_maximum_fusion), channel_id=1, source_target_pairs={{0,1},{1,0},{2,3},{3,2},{4,5},{5,4},{6,7},{7,6},{8,9},{9,8},{10,11... | collective-permute-start | bytes 5898248 | tf_op jit(solution)/shard_map/ppermute | solution.py:152
  116.7 13.4 %copy-start = (bf16[32,24,2048]{2,1,0:T(8,128)(2,1)}, bf16[32,24,2048]{2,1,0:T(8,128)(2,1)S(1)}, u32[]{:S(2)}) copy-start(bf16[32,24,2048]{2,1,0:T(8,128)(2,1)S(1)} %all-to-all-done) | copy-start | bytes 9437188
  130.1 1.0 copy-start.4
  131.1 10.6 %copy-start.13 = (bf16[384,640]{1,0:T(8,128)(2,1)S(1)}, bf16[384,640]{1,0:T(8,128)(2,1)}, u32[]{:S(2)}) copy-start(bf16[384,640]{1,0:T(8,128)(2,1)} %copy-done.12) | copy-start | bytes 1474564
  131.1 10.7 %copy-start.15 = (bf16[384,640]{1,0:T(8,128)(2,1)S(1)}, bf16[384,640]{1,0:T(8,128)(2,1)}, u32[]{:S(2)}) copy-start(bf16[384,640]{1,0:T(8,128)(2,1)} %copy-done.14) | copy-start | bytes 1474564
  131.1 35.4 %all-to-all-start.1 = ((bf16[32,24,640]{2,1,0:T(8,128)(2,1)}), bf16[32,24,640]{2,1,0:T(8,128)(2,1)S(1)}, u32[]{:S(2)}, u32[]{:S(2)}) async-start(bf16[32,24,640]{2,1,0:T(8,128)(2,1)} %bitcast.27), calls=%async_computation.1 | async-start | bytes 1966080 | tf_op jit(solution)/shard_map/all_to_all | solution.py:294
  143.8 1.9 copy-start.2
  145.6 2.1 copy-start.3
  166.5 31.8 %all-to-all-start.2 = ((bf16[32,24,640]{2,1,0:T(8,128)(2,1)}), bf16[32,24,640]{2,1,0:T(8,128)(2,1)S(1)}, u32[]{:S(2)}, u32[]{:S(2)}) async-start(bf16[32,24,640]{2,1,0:T(8,128)(2,1)} %bitcast.11), calls=%async_computation.3 | async-start | bytes 1966080 | tf_op jit(solution)/shard_map/all_to_all | solution.py:294
  171.4 116.7 %reduce-scatter.2.cloned.1.call-start = ((), (), s32[]{:S(2)}) async-start(), calls=%async_computation.6 | async-start | bytes 4423680 | tf_op jit(solution)/shard_map/reduce_scatter | solution.py:315
  180.2 1.9 copy-start.1
  182.1 16.3 %copy-start.5 = (bf16[768,640]{1,0:T(8,128)(2,1)S(1)}, bf16[768,640]{1,0:T(8,128)(2,1)}, u32[]{:S(2)}) copy-start(bf16[768,640]{1,0:T(8,128)(2,1)} %copy-done.4) | copy-start | bytes 2949124
Sparse Core Ops, SparseCore 0:
  10.6 126.6 all-gather.1
  182.2 36.3 reduce-scatter.1

commit v3 on v2

--- a/solution.py
+++ b/solution.py
@@ -7,7 +7,9 @@
 
 HEAD = 128
 NEG_FILL = -1e30
+LOG2_E = 1.4426950408889634
 VMEM_BYTES = 48 * 1024 * 1024
+VMEM_WHOLE = 60 * 1024 * 1024
 NT = (((1,), (1,)), ((), ()))
 
 
@@ -19,8 +21,8 @@
     return lax.dot_general(left, right, NT, preferred_element_type=jnp.float32)
 
 
-def params():
-    return pltpu.CompilerParams(vmem_limit_bytes=VMEM_BYTES)
+def params(limit=VMEM_BYTES):
+    return pltpu.CompilerParams(vmem_limit_bytes=limit)
 
 
 def as_bf16(flags):
@@ -32,10 +34,16 @@
     return jnp.transpose(wide)
 
 
-def pack_kernel(seq_count, slot_size, label_row, owner_row_ref, q_ref, k_ref, v_ref, packed, dest_row, dest_col):
+def pack_kernel(
+    seq_count, slot_size, label_row, owner_row_ref, q_ref, k_ref, v_ref, packed, dest_row, dest_col, held, parts, in_sems, out_sems
+):
+    sources = (q_ref, k_ref, v_ref)
     rows, cols = q_ref.shape
     clusters = owner_row_ref.shape[1]
     buffer_rows = packed.shape[0]
+    loads = [pltpu.make_async_copy(ref, held.at[i], in_sems.at[i]) for i, ref in enumerate(sources)]
+    for load in loads:
+        load.start()
     labels = label_row[...]
     owner_col = column_of(owner_row_ref[...])[:, 0:1].astype(jnp.int32)
     in_cluster = labels == lax.broadcasted_iota(jnp.int32, (clusters, rows), 0)
@@ -50,10 +58,17 @@
     dest_row[...] = dest
     dest_col[...] = column_of(dest).astype(jnp.int32)
     select = as_bf16(lax.broadcasted_iota(jnp.int32, (buffer_rows, rows), 0) == dest)
-    packed[:, 0:cols] = dot32(select, q_ref[...]).astype(jnp.bfloat16)
-    packed[:, cols : 2 * cols] = dot32(select, k_ref[...]).astype(jnp.bfloat16)
-    packed[:, 2 * cols : 3 * cols] = dot32(select, v_ref[...]).astype(jnp.bfloat16)
-    packed[:, 3 * cols :] = dot32(select, column_of(labels + 1).astype(jnp.bfloat16)).astype(jnp.bfloat16)
+    width = 3 * cols
+    parts[:, width:] = dot32(select, column_of(labels + 1).astype(jnp.bfloat16)).astype(jnp.bfloat16)
+    stores = []
+    for i, load in enumerate(loads):
+        load.wait()
+        parts[:, i * cols : (i + 1) * cols] = dot32(select, held[i]).astype(jnp.bfloat16)
+        part = slice(i * cols, (i + 1) * cols if i < 2 else width + HEAD)
+        stores.append(pltpu.make_async_copy(parts.at[:, part], packed.at[:, part], out_sems.at[i]))
+        stores[-1].start()
+    for store in stores:
+        store.wait()
 
 
 def pack_inputs(seq_count, slot_size, labels, owner_map, queries, key_rows, values):
@@ -66,7 +81,15 @@
             jax.ShapeDtypeStruct((1, rows), jnp.int32),
             jax.ShapeDtypeStruct((rows, HEAD), jnp.int32),
         ),
-        compiler_params=params(),
+        in_specs=[pl.BlockSpec(memory_space=pltpu.VMEM)] * 2 + [pl.BlockSpec(memory_space=pl.ANY)] * 3,
+        out_specs=(pl.BlockSpec(memory_space=pl.ANY),) + (pl.BlockSpec(memory_space=pltpu.VMEM),) * 2,
+        scratch_shapes=[
+            pltpu.VMEM((3, rows, cols), jnp.bfloat16),
+            pltpu.VMEM((buffer_rows, 3 * cols + HEAD), jnp.bfloat16),
+            pltpu.SemaphoreType.DMA((3,)),
+            pltpu.SemaphoreType.DMA((3,)),
+        ],
+        compiler_params=params(VMEM_WHOLE),
     )(labels[None, :], owner_map[None, :], queries, key_rows, values)
 
 
@@ -101,7 +124,7 @@
             scratch_shapes=[pltpu.VMEM((rows, width), jnp.float32)],
         ),
         out_shape=jax.ShapeDtypeStruct((buffer_rows, width), jnp.bfloat16),
-        compiler_params=params(),
+        compiler_params=params(VMEM_WHOLE),
         cost_estimate=pl.CostEstimate(
             flops=2 * groups * rows * width * width + 2 * buffer_rows * rows * width,
             bytes_accessed=2 * groups * width * (rows + width),
@@ -155,57 +178,47 @@
     return jnp.concatenate([near, far], axis=0), jnp.concatenate([own, own ^ 1])
 
 
-def forward_kernel(scale, chunk, q_ref, k_ref, v_ref, code_ref, mask_ref, att_ref, weight_ref, bias):
+def forward_kernel(scale, q_ref, k_ref, v_ref, code_ref, mask_ref, att_ref, weight_ref, keys, asks):
     rows = q_ref.shape[0]
 
     @pl.when(pl.program_id(0) == 0)
     def _():
         lane = lax.broadcasted_iota(jnp.int32, (rows, HEAD), 1).astype(jnp.float32) + 1.0
-        onehot = as_bf16(code_ref[...].astype(jnp.float32) == lane)
-        linked = dot32(onehot, mask_ref[...]).astype(jnp.bfloat16)
-        for start in range(0, rows, chunk):
-            linked_part = linked[start : start + chunk]
-            allowed = dot32_nt(onehot, linked_part) > 0.5
-            bias[:, start : start + chunk] = jnp.where(allowed, 0.0, NEG_FILL)
-
-    value_t = jnp.transpose(v_ref[...])
-    for start in range(0, rows, chunk):
-        part = slice(start, start + chunk)
-        scores = dot32_nt(k_ref[...], q_ref[part, :]) * scale + bias[:, part]
-        top = jnp.max(scores, axis=0, keepdims=True)
-        terms = jnp.exp(scores - top)
-        weights = (terms * (1.0 / jnp.sum(terms, axis=0, keepdims=True))).astype(jnp.bfloat16)
-        weight_ref[0, :, part] = weights
-        att_ref[part, :] = jnp.transpose(dot32(value_t, weights)).astype(jnp.bfloat16)
-
-
-def backward_kernel(scale, chunk, q_ref, k_ref, v_ref, att_ref, g_ref, weight_ref, out_ref):
-    rows = q_ref.shape[0]
+        code = code_ref[...].astype(jnp.float32)
+        onehot = as_bf16((code == lane) | (code == 0.0))
+        linked = dot32(onehot, mask_ref[...])
+        keys[:, HEAD:] = onehot
+        asks[:, HEAD:] = jnp.where(linked > 0.5, 0.0, NEG_FILL).astype(jnp.bfloat16)
+
+    keys[:, :HEAD] = k_ref[...]
+    asks[:, :HEAD] = q_ref[...]
+    scores = dot32_nt(keys[...], asks[...])
+    top = jnp.max(scores, axis=0, keepdims=True)
+    terms = jnp.exp2((scores - top) * (scale * LOG2_E))
+    weights = (terms * (1.0 / jnp.sum(terms, axis=0, keepdims=True))).astype(jnp.bfloat16)
+    weight_ref[0] = weights
+    att_ref[...] = jnp.transpose(dot32(jnp.transpose(v_ref[...]), weights)).astype(jnp.bfloat16)
+
+
+def backward_kernel(scale, q_ref, k_ref, v_ref, att_ref, g_ref, weight_ref, out_ref):
     grad = g_ref[...]
+    weights = weight_ref[0]
     delta = jnp.sum(
         jnp.transpose(grad.astype(jnp.float32) * att_ref[...].astype(jnp.float32)), axis=0, keepdims=True
     )
-    key_t = jnp.transpose(k_ref[...])
-    grad_key = jnp.zeros((rows, HEAD), jnp.float32)
-    grad_value = jnp.zeros((rows, HEAD), jnp.float32)
-    for start in range(0, rows, chunk):
-        part = slice(start, start + chunk)
-        weights = weight_ref[0, :, part]
-        grad_part = g_ref[part, :]
-        grad_probs = dot32_nt(v_ref[...], grad_part)
-        grad_scores = (weights.astype(jnp.float32) * (grad_probs - delta[:, part])).astype(jnp.bfloat16)
-        out_ref[part, 0:HEAD] = jnp.transpose(dot32(key_t, grad_scores) * scale).astype(jnp.bfloat16)
-        grad_key = grad_key + dot32(grad_scores, q_ref[part, :])
-        grad_value = grad_value + dot32(weights, grad_part)
-    out_ref[:, HEAD : 2 * HEAD] = (grad_key * scale).astype(jnp.bfloat16)
-    out_ref[:, 2 * HEAD :] = grad_value.astype(jnp.bfloat16)
-
-
-def attention_forward(owned, pair_mask, heads, scale, chunk):
+    grad_probs = dot32_nt(v_ref[...], grad)
+    grad_scores = (weights.astype(jnp.float32) * (grad_probs - delta)).astype(jnp.bfloat16)
+    grad_query = dot32(jnp.transpose(k_ref[...]), grad_scores) * scale
+    out_ref[:, 0:HEAD] = jnp.transpose(grad_query).astype(jnp.bfloat16)
+    out_ref[:, HEAD : 2 * HEAD] = (dot32(grad_scores, q_ref[...]) * scale).astype(jnp.bfloat16)
+    out_ref[:, 2 * HEAD :] = dot32(weights, grad).astype(jnp.bfloat16)
+
+
+def attention_forward(owned, pair_mask, heads, scale):
     rows = owned.shape[0]
     block = (rows, HEAD)
     return pl.pallas_call(
-        lambda *refs: forward_kernel(scale, chunk, *refs),
+        lambda *refs: forward_kernel(scale, *refs),
         grid=(heads,),
         in_specs=[
             pl.BlockSpec(block, lambda h: (0, h)),
@@ -222,7 +235,7 @@
             jax.ShapeDtypeStruct((rows, heads * HEAD), jnp.bfloat16),
             jax.ShapeDtypeStruct((heads, rows, rows), jnp.bfloat16),
         ),
-        scratch_shapes=[pltpu.VMEM((rows, rows), jnp.float32)],
+        scratch_shapes=[pltpu.VMEM((rows, 2 * HEAD), jnp.bfloat16)] * 2,
         compiler_params=params(),
         cost_estimate=pl.CostEstimate(
             flops=heads * 4 * rows * rows * HEAD,
@@ -232,11 +245,11 @@
     )(owned, owned, owned, owned, pair_mask)
 
 
-def attention_backward(owned, attended, grad_owned, weights, heads, scale, chunk):
+def attention_backward(owned, attended, grad_owned, weights, heads, scale):
     rows = owned.shape[0]
     block = (rows, HEAD)
     return pl.pallas_call(
-        lambda *refs: backward_kernel(scale, chunk, *refs),
+        lambda *refs: backward_kernel(scale, *refs),
         grid=(heads,),
         in_specs=[
             pl.BlockSpec(block, lambda h: (0, h)),
@@ -257,13 +270,15 @@
     )(owned, owned, owned, attended, grad_owned, weights)
 
 
-def unpack_kernel(dest_ref, blocks_ref, q_ref, k_ref, v_ref):
-    rows = q_ref.shape[0]
-    buffer_rows = blocks_ref.shape[0]
-    select = as_bf16(dest_ref[:, 0:1] == lax.broadcasted_iota(jnp.int32, (rows, buffer_rows), 1))
-    for place, out_ref in enumerate((q_ref, k_ref, v_ref)):
-        part = blocks_ref[:, place * HEAD : (place + 1) * HEAD]
-        out_ref[...] = dot32(select, part).astype(jnp.bfloat16)
+def unpack_kernel(dest_ref, blocks_ref, q_ref, k_ref, v_ref, select):
+    @pl.when(pl.program_id(0) == 0)
+    def _():
+        select[...] = as_bf16(dest_ref[:, 0:1] == lax.broadcasted_iota(jnp.int32, select.shape, 1))
+
+    picked = dot32(select[...], blocks_ref[...]).astype(jnp.bfloat16)
+    q_ref[...] = picked[:, 0:HEAD]
+    k_ref[...] = picked[:, HEAD : 2 * HEAD]
+    v_ref[...] = picked[:, 2 * HEAD :]
 
 
 def unpack_grads(dest_col, blocks, heads):
@@ -279,6 +294,7 @@
         ],
         out_specs=[pl.BlockSpec((rows, HEAD), lambda h: (0, h))] * 3,
         out_shape=(out, out, out),
+        scratch_shapes=[pltpu.VMEM((rows, buffer_rows), jnp.bfloat16)],
         compiler_params=params(),
         cost_estimate=pl.CostEstimate(
             flops=6 * heads * rows * buffer_rows * HEAD,
@@ -301,19 +317,18 @@
     slot_size = 2 * row_count // seq_count
     buffer_rows = seq_count * slot_size
     scale = HEAD ** (-0.5)
-    chunk = 256
     weight_t = lax.all_gather(out_weight.T, "seq", axis=0, tiled=True)
     grad_blocks, order = gather_groups(grad_out)
     packed, dest_row, dest_col = pack_inputs(
         seq_count, slot_size, labels, owner_map, queries, key_rows, values
     )
     owned = exchange(packed, seq_count)
-    attended, weights = attention_forward(owned, pair_mask.astype(jnp.bfloat16), heads, scale, chunk)
+    attended, weights = attention_forward(owned, pair_mask.astype(jnp.bfloat16), heads, scale)
     returned = exchange(attended, seq_count)
     grad_owned = exchange(project_grads(order, grad_blocks, weight_t, dest_row, buffer_rows), seq_count)
     partial_out = project_output(dest_col, returned, weight_t, lax.axis_size("tp"))
     output = lax.psum_scatter(partial_out, "tp", scatter_dimension=0, tiled=False)
-    grads = attention_backward(owned, attended, grad_owned, weights, heads, scale, chunk)
+    grads = attention_backward(owned, attended, grad_owned, weights, heads, scale)
     back = exchange(grads, seq_count)
     grad_q, grad_k, grad_v = unpack_grads(dest_col, back, heads)
     return (output, grad_q, grad_k, grad_v)

time: 296 us -> 290 us (0.980)
  local copies, waits for them, and re-layouts: 17.1 us -> 12.5 us
  Pallas kernels: 50.4 us -> 47.2 us
    pallas_call x2, Pallas kernels: 24.8 us -> 17.8 us  [the longest x1 8.98 us: attention_backward(): pl.pallas_call(lambda *refs: backward_kernel(scale, *refs), grid=(heads,)...]
    unnamed x38 -> x26, local copies, waits for them, and re-layouts: 14.6 us -> 8.27 us
    pallas_call x1, Pallas kernels: 2.33 us -> 5.81 us  [pack_inputs(): pl.pallas_call(lambda *refs: pack_kernel(seq_count, slot_size, *refs), ou...]
  transfers between devices with their start and end apart: 9 -> 9, of which waited for: 6 -> 6; matrix products, arithmetic and copies ran while one was open for 3% -> 5% of each run, Pallas kernels for 17% -> 16%
where the time goes in v3:
time: 290 us; the launch traced here: 289 us
  waiting for transfers between devices  109 us (38%)
  blocking collectives  73.6 us (25%)
  Pallas kernels  47.2 us (16%)
  starting transfers between devices  28.5 us (10%)
  between operations  14.2 us (5%)
  local copies, waits for them, and re-layouts  12.5 us (4%)
  other arithmetic  3.42 us (1%)
    all_to_all x3, waiting for transfers between devices, exchange(): lax.all_to_all(blocks, 'seq', split_axis=0, concat_axis=0, tiled=True)  86.6 us
    all_to_all x1, blocking collectives, exchange(): lax.all_to_all(blocks, 'seq', split_axis=0, concat_axis=0, tiled=True)  73.6 us
    all_to_all x3, starting transfers between devices, exchange(): lax.all_to_all(blocks, 'seq', split_axis=0, concat_axis=0, tiled=True)  25 us
    ppermute x3, waiting for transfers between devices, gather_groups(): lax.ppermute(block, 'tp', [(t, (t + 2 * shift) % tp_count) for t in range...  22.1 us
    pallas_call x1, Pallas kernels, project_grads(): pl.pallas_call(grad_kernel, grid_spec=pltpu.PrefetchScalarGridSpec(num_sc...  11.1 us
    pallas_call x1, Pallas kernels, attention_backward(): pl.pallas_call(lambda *refs: backward_kernel(scale, *refs), grid=(heads,)...  8.98 us
    pallas_call x1, Pallas kernels, attention_forward(): pl.pallas_call(lambda *refs: forward_kernel(scale, *refs), grid=(heads,),...  8.83 us
    pallas_call x1, Pallas kernels, project_output(): pl.pallas_call(output_kernel, grid=(groups,), in_specs=[pl.BlockSpec((row...  8.55 us
  transfers between devices with their start and end apart: 9, of which 6 were waited for; matrix products, arithmetic and copies ran while one was open for 5% of the time, Pallas kernels for 16%

profile of v3, /device:TPU:4, one launch (start us, length us, event | category | flops | bytes accessed | tf_op | source)
XLA Modules:
  0.0 288.8 jit_solution(9997099032166794427)
XLA Ops:
  7.2 0.0 all-gather.2.cloned.1.call-start
  7.2 0.7 all-gather.2.cloned.1.call-update
  7.9 1.2 broadcast_in_dim.6.refs_0_
  9.1 5.8 %shard_map.111 = (bf16[768,2048]{1,0:T(8,128)(2,1)}, s32[1,384]{1,0:T(1,128)}, s32[384,128]{1,0:T(8,128)}) custom-call(s32[1,384]{1,0:T(1,128)} %broadcast_in_dim.6.refs_0_, s32[1,128]{1,0:T(1,128)} %bitcast.38, bf16[384,640]{1,0:T(8,128)(2,1)} %refs_2_.1, bf16[384,640]{1,0:T(8,128)(2,1)} %refs_3_.1, bf16[384,640]{1,0:T(8,128)(2,1)} %refs_4_.1), custom_call_target="tpu_custom_call" | custom-call | tf_op jit(solution)/shard_map/pallas_call | solution.py:77
  15.0 0.0 copy-start.10
  15.0 11.6 %all-to-all-start = ((bf16[32,24,2048]{2,1,0:T(8,128)(2,1)}), bf16[32,24,2048]{2,1,0:T(8,128)(2,1)S(1)}, u32[]{:S(2)}, u32[]{:S(2)}) async-start(bf16[32,24,2048]{2,1,0:T(8,128)(2,1)} %bitcast.32), calls=%async_computation | async-start | bytes 6291456 | tf_op jit(solution)/shard_map/all_to_all | solution.py:310
  26.6 1.3 collective-permute-start
  27.9 0.8 collective-permute-start.1
  28.7 1.1 collective-permute-start.2
  29.8 11.2 %collective-permute-done = bf16[384,640]{1,0:T(8,128)(2,1)S(1)} collective-permute-done((bf16[384,640]{1,0:T(8,128)(2,1)}, bf16[384,640]{1,0:T(8,128)(2,1)S(1)}, u32[]{:S(2)}, u32[]{:S(2)}) %collective-permute-start) | collective-permute-done | bytes 491552 | tf_op jit(solution)/shard_map/ppermute | solution.py:173
  41.1 0.0 copy-start.5
  41.1 9.1 %collective-permute-done.1 = bf16[384,640]{1,0:T(8,128)(2,1)S(1)} collective-permute-done((bf16[384,640]{1,0:T(8,128)(2,1)}, bf16[384,640]{1,0:T(8,128)(2,1)S(1)}, u32[]{:S(2)}, u32[]{:S(2)}) %collective-permute-start.1) | collective-permute-done | bytes 491552 | tf_op jit(solution)/shard_map/ppermute | solution.py:173
  50.1 0.0 copy-start.6
  50.1 1.8 collective-permute-done.2
  51.9 2.8 pad_maximum_fusion
  54.8 0.0 collective-permute-start.3
  54.8 0.0 copy-done.5
  54.8 0.0 copy-done.6
  54.8 0.0 copy-done.8
  54.8 0.0 copy-done.10
  54.8 63.2 %all-to-all-done = bf16[32,24,2048]{2,1,0:T(8,128)(2,1)S(1)} async-done(((bf16[32,24,2048]{2,1,0:T(8,128)(2,1)}), bf16[32,24,2048]{2,1,0:T(8,128)(2,1)S(1)}, u32[]{:S(2)}, u32[]{:S(2)}) %all-to-all-start) | async-done | bytes 3145760 | tf_op jit(solution)/shard_map/all_to_all | solution.py:310
  118.0 8.8 %shard_map.112 = (bf16[768,640]{1,0:T(8,128)(2,1)S(1)}, bf16[5,768,768]{2,1,0:T(8,128)(2,1)}) custom-call(bf16[768,2048]{1,0:T(8,128)(2,1)S(1)} %bitcast.19, bf16[768,2048]{1,0:T(8,128)(2,1)S(1)} %bitcast.20, bf16[768,2048]{1,0:T(8,128)(2,1)S(1)} %bitcast.21, bf16[768,2048]{1,0:T(8,128)(2,1)S(1)} %bitcast.22, bf16[128,128]{1,0:T(8,128)(2,1)S(1)} %convert_element_type.3.refs_4_), custom_call_target="tpu_custom_call" | custom-call | flops 1509949440 | bytes 9830400 | tf_op jit(solution)/shard_map/pallas_call | solution.py:220
  126.8 0.0 copy-done
  126.8 1.0 copy-done.2
  127.8 8.6 %all-to-all-start.1 = ((bf16[32,24,640]{2,1,0:T(8,128)(2,1)}), bf16[32,24,640]{2,1,0:T(8,128)(2,1)S(1)}, u32[]{:S(2)}, u32[]{:S(2)}) async-start(bf16[32,24,640]{2,1,0:T(8,128)(2,1)} %bitcast.27), calls=%async_computation.1 | async-start | bytes 1966080 | tf_op jit(solution)/shard_map/all_to_all | solution.py:310
  136.4 0.6 pad_add_fusion.order_ref
  137.0 1.9 constant_dynamic-update-slice_fusion.4
  138.8 1.9 constant_dynamic-update-slice_fusion.3
  140.7 0.0 copy-done.7
  140.7 0.8 constant_dynamic-update-slice_fusion.2
  141.6 0.0 copy-done.9
  141.6 0.8 constant_dynamic-update-slice_fusion.1
  142.4 0.0 collective-permute-done.3
  142.4 3.0 %constant_dynamic-update-slice_fusion.grad_ref = bf16[8,384,640]{2,1,0:T(8,128)(2,1)} fusion(bf16[8,384,640]{2,1,0:T(8,128)(2,1)} %constant_dynamic-update-slice_fusion.1, bf16[4,384,640]{2,1,0:T(8,128)(2,1)} %collective-permute-done.3), kind=kLoop, calls=%fused_computation.1 | loop fusion | bytes 3932160 | tf_op jit(solution)/shard_map/concatenate | solution.py:178
  145.4 11.1 %shard_map.114 = bf16[768,640]{1,0:T(8,128)(2,1)} custom-call(s32[8]{0:T(128)} %pad_add_fusion.order_ref, bf16[8,384,640]{2,1,0:T(8,128)(2,1)} %constant_dynamic-update-slice_fusion.grad_ref, bf16[5120,640]{1,0:T(8,128)(2,1)} %all-gather.2.cloned.1.call-done.weight_ref, s32[1,384]{1,0:T(1,128)} %get-tuple-element.15.dest_row), custom_call_target="tpu_custom_call" | custom-call | flops 2894069760 | bytes 10485760 | tf_op jit(solution)/shard_map/pallas_call | solution.py:113
  156.5 7.1 %all-to-all-done.1 = bf16[32,24,640]{2,1,0:T(8,128)(2,1)S(1)} async-done(((bf16[32,24,640]{2,1,0:T(8,128)(2,1)}), bf16[32,24,640]{2,1,0:T(8,128)(2,1)S(1)}, u32[]{:S(2)}, u32[]{:S(2)}) %all-to-all-start.1) | async-done | bytes 983072 | tf_op jit(solution)/shard_map/all_to_all | solution.py:310
  163.6 4.8 %all-to-all-start.2 = ((bf16[32,24,640]{2,1,0:T(8,128)(2,1)}), bf16[32,24,640]{2,1,0:T(8,128)(2,1)S(1)}, u32[]{:S(2)}, u32[]{:S(2)}) async-start(bf16[32,24,640]{2,1,0:T(8,128)(2,1)} %bitcast.31), calls=%async_computation.3 | async-start | bytes 1966080 | tf_op jit(solution)/shard_map/all_to_all | solution.py:310
  168.5 0.2 reduce-scatter.2.cloned.1.call-start
  168.7 0.0 copy-done.4
  168.7 8.6 %shard_map.113 = bf16[8,384,640]{2,1,0:T(8,128)(2,1)S(1)} custom-call(s32[384,128]{1,0:T(8,128)S(1)} %copy-done.4, bf16[768,640]{1,0:T(8,128)(2,1)S(1)} %bitcast.28, bf16[5120,640]{1,0:T(8,128)(2,1)} %all-gather.2.cloned.1.call-done.weight_ref), custom_call_target="tpu_custom_call" | custom-call | flops 2894069760 | bytes 10485760 | tf_op jit(solution)/shard_map/pallas_call | solution.py:148
  177.3 0.0 copy-start.1
  177.3 1.9 copy-done.1
  179.1 0.0 reduce-scatter.2.cloned.1.call-update
  179.2 16.3 %all-to-all-done.2 = bf16[32,24,640]{2,1,0:T(8,128)(2,1)S(1)} async-done(((bf16[32,24,640]{2,1,0:T(8,128)(2,1)}), bf16[32,24,640]{2,1,0:T(8,128)(2,1)S(1)}, u32[]{:S(2)}, u32[]{:S(2)}) %all-to-all-start.2) | async-done | bytes 983072 | tf_op jit(solution)/shard_map/all_to_all | solution.py:310
  195.5 0.0 copy-done.3
  195.5 9.0 %shard_map.115 = bf16[768,1920]{1,0:T(8,128)(2,1)S(1)} custom-call(bf16[768,2048]{1,0:T(8,128)(2,1)} %bitcast.23, bf16[768,2048]{1,0:T(8,128)(2,1)} %bitcast.24, bf16[768,2048]{1,0:T(8,128)(2,1)} %bitcast.25, bf16[768,640]{1,0:T(8,128)(2,1)S(1)} %copy-done.3, bf16[768,640]{1,0:T(8,128)(2,1)S(1)} %bitcast.29, bf16[5,768,768]{2,1,0:T(8,128)(2,1)} %get-tuple-element.16.refs_5_), custom_call_target="tpu_custom_call" | custom-call | flops 3019898880 | bytes 13762560 | tf_op jit(solution)/shard_map/pallas_call | solution.py:251
  204.5 73.6 %all_to_all.20 = bf16[32,24,1920]{2,1,0:T(8,128)(2,1)S(1)} all-to-all(bf16[32,24,1920]{2,1,0:T(8,128)(2,1)S(1)} %bitcast.26), channel_id=1, replica_groups=mesh['seq'=32,'tp'=8] {'seq'}, dimensions={0} | all-to-all | bytes 5898240 | tf_op jit(solution)/shard_map/all_to_all | solution.py:310
  278.1 3.9 %shard_map.116 = (bf16[384,640]{1,0:T(8,128)(2,1)}, bf16[384,640]{1,0:T(8,128)(2,1)}, bf16[384,640]{1,0:T(8,128)(2,1)}) custom-call(s32[384,128]{1,0:T(8,128)S(1)} %copy-done.4, bf16[768,1920]{1,0:T(8,128)(2,1)S(1)} %bitcast.30), custom_call_target="tpu_custom_call" | custom-call | flops 1132462080 | bytes 4423680 | tf_op jit(solution)/shard_map/pallas_call | solution.py:288
  (11 shorter events, 0.0 us)
Async XLA Ops:
  7.2 138.2 %all-gather.2.cloned.1.call-start = ((), (), s32[]{:S(2)}) async-start(), calls=%async_computation.5 | async-start | bytes 6758400 | tf_op jit(solution)/shard_map/all_gather | solution.py:320
  15.0 39.8 %copy-start.10 = (s32[128,128]{1,0:T(8,128)S(1)}, s32[128,128]{1,0:T(8,128)}, u32[]{:S(2)}) copy-start(s32[128,128]{1,0:T(8,128)} %param.15) | copy-start | bytes 196612
  15.0 103.0 %all-to-all-start = ((bf16[32,24,2048]{2,1,0:T(8,128)(2,1)}), bf16[32,24,2048]{2,1,0:T(8,128)(2,1)S(1)}, u32[]{:S(2)}, u32[]{:S(2)}) async-start(bf16[32,24,2048]{2,1,0:T(8,128)(2,1)} %bitcast.32), calls=%async_computation | async-start | bytes 6291456 | tf_op jit(solution)/shard_map/all_to_all | solution.py:310
  26.6 14.4 %collective-permute-start = (bf16[384,640]{1,0:T(8,128)(2,1)}, bf16[384,640]{1,0:T(8,128)(2,1)S(1)}, u32[]{:S(2)}, u32[]{:S(2)}) collective-permute-start(bf16[384,640]{1,0:T(8,128)(2,1)} %param.12), channel_id=1, source_target_pairs={{0,2},{1,3},{2,4},{3,5},{4,6},{5,7},{6,0},{7,1},{8,10},{9,11},{10,... | collective-permute-start | bytes 1474568 | tf_op jit(solution)/shard_map/ppermute | solution.py:173
  27.9 22.2 %collective-permute-start.1 = (bf16[384,640]{1,0:T(8,128)(2,1)}, bf16[384,640]{1,0:T(8,128)(2,1)S(1)}, u32[]{:S(2)}, u32[]{:S(2)}) collective-permute-start(bf16[384,640]{1,0:T(8,128)(2,1)} %param.12), channel_id=1, source_target_pairs={{0,4},{1,5},{2,6},{3,7},{4,0},{5,1},{6,2},{7,3},{8,12},{9,13},{10,... | collective-permute-start | bytes 1474568 | tf_op jit(solution)/shard_map/ppermute | solution.py:173
  28.7 23.3 %collective-permute-start.2 = (bf16[384,640]{1,0:T(8,128)(2,1)}, bf16[384,640]{1,0:T(8,128)(2,1)S(1)}, u32[]{:S(2)}, u32[]{:S(2)}) collective-permute-start(bf16[384,640]{1,0:T(8,128)(2,1)} %param.12), channel_id=1, source_target_pairs={{0,6},{1,7},{2,0},{3,1},{4,2},{5,3},{6,4},{7,5},{8,14},{9,15},{10,... | collective-permute-start | bytes 1474568 | tf_op jit(solution)/shard_map/ppermute | solution.py:173
  41.1 13.7 %copy-start.5 = (bf16[384,640]{1,0:T(8,128)(2,1)}, bf16[384,640]{1,0:T(8,128)(2,1)S(1)}, u32[]{:S(2)}) copy-start(bf16[384,640]{1,0:T(8,128)(2,1)S(1)} %collective-permute-done) | copy-start | bytes 1474564
  50.1 4.7 %copy-start.6 = (bf16[384,640]{1,0:T(8,128)(2,1)}, bf16[384,640]{1,0:T(8,128)(2,1)S(1)}, u32[]{:S(2)}) copy-start(bf16[384,640]{1,0:T(8,128)(2,1)S(1)} %collective-permute-done.1) | copy-start | bytes 1474564
  51.9 2.8 copy-start.8
  54.8 87.6 %collective-permute-start.3 = (bf16[4,384,640]{2,1,0:T(8,128)(2,1)}, bf16[4,384,640]{2,1,0:T(8,128)(2,1)}, u32[]{:S(2)}, u32[]{:S(2)}) collective-permute-start(bf16[4,384,640]{2,1,0:T(8,128)(2,1)} %pad_maximum_fusion), channel_id=1, source_target_pairs={{0,1},{1,0},{2,3},{3,2},{4,5},{5,4},{6,7},{7,6},{8,9},{9,8},{10,11... | collective-permute-start | bytes 5898248 | tf_op jit(solution)/shard_map/ppermute | solution.py:175
  118.0 8.8 %copy-start = (bf16[32,24,2048]{2,1,0:T(8,128)(2,1)}, bf16[32,24,2048]{2,1,0:T(8,128)(2,1)S(1)}, u32[]{:S(2)}) copy-start(bf16[32,24,2048]{2,1,0:T(8,128)(2,1)S(1)} %all-to-all-done) | copy-start | bytes 9437188
  126.8 1.0 copy-start.2
  127.8 12.9 %copy-start.7 = (bf16[384,640]{1,0:T(8,128)(2,1)S(1)}, bf16[384,640]{1,0:T(8,128)(2,1)}, u32[]{:S(2)}) copy-start(bf16[384,640]{1,0:T(8,128)(2,1)} %copy-done.6) | copy-start | bytes 1474564
  127.8 13.8 %copy-start.9 = (bf16[384,640]{1,0:T(8,128)(2,1)S(1)}, bf16[384,640]{1,0:T(8,128)(2,1)}, u32[]{:S(2)}) copy-start(bf16[384,640]{1,0:T(8,128)(2,1)} %copy-done.8) | copy-start | bytes 1474564
  127.8 35.8 %all-to-all-start.1 = ((bf16[32,24,640]{2,1,0:T(8,128)(2,1)}), bf16[32,24,640]{2,1,0:T(8,128)(2,1)S(1)}, u32[]{:S(2)}, u32[]{:S(2)}) async-start(bf16[32,24,640]{2,1,0:T(8,128)(2,1)} %bitcast.27), calls=%async_computation.1 | async-start | bytes 1966080 | tf_op jit(solution)/shard_map/all_to_all | solution.py:310
  145.4 23.3 %copy-start.4 = (s32[384,128]{1,0:T(8,128)S(1)}, s32[384,128]{1,0:T(8,128)}, u32[]{:S(2)}) copy-start(s32[384,128]{1,0:T(8,128)} %get-tuple-element.12.dest_col.dest_ref) | copy-start | bytes 589828
  163.6 31.8 %all-to-all-start.2 = ((bf16[32,24,640]{2,1,0:T(8,128)(2,1)}), bf16[32,24,640]{2,1,0:T(8,128)(2,1)S(1)}, u32[]{:S(2)}, u32[]{:S(2)}) async-start(bf16[32,24,640]{2,1,0:T(8,128)(2,1)} %bitcast.31), calls=%async_computation.3 | async-start | bytes 1966080 | tf_op jit(solution)/shard_map/all_to_all | solution.py:310
  168.5 113.5 %reduce-scatter.2.cloned.1.call-start = ((), (), s32[]{:S(2)}) async-start(), calls=%async_computation.6 | async-start | bytes 4423680 | tf_op jit(solution)/shard_map/reduce_scatter | solution.py:330
  177.3 1.9 copy-start.1
  179.1 16.3 %copy-start.3 = (bf16[768,640]{1,0:T(8,128)(2,1)S(1)}, bf16[768,640]{1,0:T(8,128)(2,1)}, u32[]{:S(2)}) copy-start(bf16[768,640]{1,0:T(8,128)(2,1)} %copy-done.2) | copy-start | bytes 2949124
Sparse Core Ops, SparseCore 0:
  10.6 125.8 all-gather.1
  179.3 36.3 reduce-scatter.1

commit v4 on v3

--- a/solution.py
+++ b/solution.py
@@ -44,7 +44,7 @@
     loads = [pltpu.make_async_copy(ref, held.at[i], in_sems.at[i]) for i, ref in enumerate(sources)]
     for load in loads:
         load.start()
-    labels = label_row[...]
+    labels = label_row[...].reshape(1, rows)
     owner_col = column_of(owner_row_ref[...])[:, 0:1].astype(jnp.int32)
     in_cluster = labels == lax.broadcasted_iota(jnp.int32, (clusters, rows), 0)
     owner_row = jnp.sum(jnp.where(in_cluster, owner_col, 0), axis=0, keepdims=True)
@@ -56,19 +56,24 @@
     rank_row = jnp.sum(jnp.where(owned, before, 0.0), axis=0, keepdims=True)
     dest = owner_row * slot_size + rank_row.astype(jnp.int32)
     dest_row[...] = dest
-    dest_col[...] = column_of(dest).astype(jnp.int32)
     select = as_bf16(lax.broadcasted_iota(jnp.int32, (buffer_rows, rows), 0) == dest)
     width = 3 * cols
-    parts[:, width:] = dot32(select, column_of(labels + 1).astype(jnp.bfloat16)).astype(jnp.bfloat16)
     stores = []
+
+    def store(start, stop):
+        part = slice(start, stop)
+        stores.append(pltpu.make_async_copy(parts.at[:, part], packed.at[:, part], out_sems.at[len(stores)]))
+        stores[-1].start()
+
     for i, load in enumerate(loads):
         load.wait()
         parts[:, i * cols : (i + 1) * cols] = dot32(select, held[i]).astype(jnp.bfloat16)
-        part = slice(i * cols, (i + 1) * cols if i < 2 else width + HEAD)
-        stores.append(pltpu.make_async_copy(parts.at[:, part], packed.at[:, part], out_sems.at[i]))
-        stores[-1].start()
-    for store in stores:
-        store.wait()
+        store(i * cols, (i + 1) * cols)
+    parts[:, width:] = dot32(select, column_of(labels + 1).astype(jnp.bfloat16)).astype(jnp.bfloat16)
+    store(width, width + HEAD)
+    dest_col[...] = column_of(dest).astype(jnp.int32)
+    for copy in stores:
+        copy.wait()
 
 
 def pack_inputs(seq_count, slot_size, labels, owner_map, queries, key_rows, values):
@@ -87,10 +92,10 @@
             pltpu.VMEM((3, rows, cols), jnp.bfloat16),
             pltpu.VMEM((buffer_rows, 3 * cols + HEAD), jnp.bfloat16),
             pltpu.SemaphoreType.DMA((3,)),
-            pltpu.SemaphoreType.DMA((3,)),
+            pltpu.SemaphoreType.DMA((4,)),
         ],
         compiler_params=params(VMEM_WHOLE),
-    )(labels[None, :], owner_map[None, :], queries, key_rows, values)
+    )(labels, owner_map[None, :], queries, key_rows, values)
 
 
 def grad_kernel(order_ref, grad_ref, weight_ref, dest_row, packed, total):

time: 290 us -> 287 us (0.990)
  transfers between devices with their start and end apart: 9 -> 9, of which waited for: 6 -> 6; matrix products, arithmetic and copies ran while one was open for 5% -> 4% of each run, Pallas kernels for 16% -> 17%
where the time goes in v4:
time: 287 us; the launch traced here: 286 us
  waiting for transfers between devices  108 us (38%)
  blocking collectives  73.8 us (26%)
  Pallas kernels  47.1 us (16%)
  starting transfers between devices  28 us (10%)
  between operations  14.2 us (5%)
  local copies, waits for them, and re-layouts  11.3 us (4%)
  other arithmetic  3.42 us (1%)
    all_to_all x3, waiting for transfers between devices, exchange(): lax.all_to_all(blocks, 'seq', split_axis=0, concat_axis=0, tiled=True)  85 us
    all_to_all x1, blocking collectives, exchange(): lax.all_to_all(blocks, 'seq', split_axis=0, concat_axis=0, tiled=True)  73.8 us
    all_to_all x3, starting transfers between devices, exchange(): lax.all_to_all(blocks, 'seq', split_axis=0, concat_axis=0, tiled=True)  24.5 us
    ppermute x3, waiting for transfers between devices, gather_groups(): lax.ppermute(block, 'tp', [(t, (t + 2 * shift) % tp_count) for t in range...  22.1 us
    pallas_call x1, Pallas kernels, project_grads(): pl.pallas_call(grad_kernel, grid_spec=pltpu.PrefetchScalarGridSpec(num_sc...  11.1 us
    pallas_call x1, Pallas kernels, attention_backward(): pl.pallas_call(lambda *refs: backward_kernel(scale, *refs), grid=(heads,)...  8.86 us
    pallas_call x1, Pallas kernels, attention_forward(): pl.pallas_call(lambda *refs: forward_kernel(scale, *refs), grid=(heads,),...  8.84 us
    pallas_call x1, Pallas kernels, project_output(): pl.pallas_call(output_kernel, grid=(groups,), in_specs=[pl.BlockSpec((row...  8.55 us
  transfers between devices with their start and end apart: 9, of which 6 were waited for; matrix products, arithmetic and copies ran while one was open for 4% of the time, Pallas kernels for 17%

profile of v4, /device:TPU:4, one launch (start us, length us, event | category | flops | bytes accessed | tf_op | source)
XLA Modules:
  0.0 285.5 jit_solution(946424791407216432)
XLA Ops:
  7.2 0.0 all-gather.2.cloned.1.call-start
  7.2 0.7 all-gather.2.cloned.1.call-update
  7.9 5.8 %shard_map.111 = (bf16[768,2048]{1,0:T(8,128)(2,1)}, s32[1,384]{1,0:T(1,128)}, s32[384,128]{1,0:T(8,128)}) custom-call(s32[384]{0:T(512)} %refs_0_.1, s32[1,128]{1,0:T(1,128)} %bitcast.38, bf16[384,640]{1,0:T(8,128)(2,1)} %refs_2_.1, bf16[384,640]{1,0:T(8,128)(2,1)} %refs_3_.1, bf16[384,640]{1,0:T(8,128)(2,1)} %refs_4_.1), custom_call_target="tpu_custom_call" | custom-call | tf_op jit(solution)/shard_map/pallas_call | solution.py:82
  13.8 0.0 copy-start.10
  13.8 11.6 %all-to-all-start = ((bf16[32,24,2048]{2,1,0:T(8,128)(2,1)}), bf16[32,24,2048]{2,1,0:T(8,128)(2,1)S(1)}, u32[]{:S(2)}, u32[]{:S(2)}) async-start(bf16[32,24,2048]{2,1,0:T(8,128)(2,1)} %bitcast.32), calls=%async_computation | async-start | bytes 6291456 | tf_op jit(solution)/shard_map/all_to_all | solution.py:315
  25.4 1.3 collective-permute-start
  26.7 0.8 collective-permute-start.1
  27.5 1.1 collective-permute-start.2
  28.6 11.2 %collective-permute-done = bf16[384,640]{1,0:T(8,128)(2,1)S(1)} collective-permute-done((bf16[384,640]{1,0:T(8,128)(2,1)}, bf16[384,640]{1,0:T(8,128)(2,1)S(1)}, u32[]{:S(2)}, u32[]{:S(2)}) %collective-permute-start) | collective-permute-done | bytes 491552 | tf_op jit(solution)/shard_map/ppermute | solution.py:178
  39.9 0.0 copy-start.5
  39.9 9.0 %collective-permute-done.1 = bf16[384,640]{1,0:T(8,128)(2,1)S(1)} collective-permute-done((bf16[384,640]{1,0:T(8,128)(2,1)}, bf16[384,640]{1,0:T(8,128)(2,1)S(1)}, u32[]{:S(2)}, u32[]{:S(2)}) %collective-permute-start.1) | collective-permute-done | bytes 491552 | tf_op jit(solution)/shard_map/ppermute | solution.py:178
  48.9 0.0 copy-start.6
  48.9 1.8 collective-permute-done.2
  50.7 0.0 copy-start.8
  50.7 2.8 pad_maximum_fusion
  53.6 0.0 collective-permute-start.3
  53.6 0.0 copy-done.5
  53.6 0.0 copy-done.6
  53.6 0.0 copy-done.8
  53.6 0.0 copy-done.10
  53.6 61.5 %all-to-all-done = bf16[32,24,2048]{2,1,0:T(8,128)(2,1)S(1)} async-done(((bf16[32,24,2048]{2,1,0:T(8,128)(2,1)}), bf16[32,24,2048]{2,1,0:T(8,128)(2,1)S(1)}, u32[]{:S(2)}, u32[]{:S(2)}) %all-to-all-start) | async-done | bytes 3145760 | tf_op jit(solution)/shard_map/all_to_all | solution.py:315
  115.1 8.8 %shard_map.112 = (bf16[768,640]{1,0:T(8,128)(2,1)S(1)}, bf16[5,768,768]{2,1,0:T(8,128)(2,1)}) custom-call(bf16[768,2048]{1,0:T(8,128)(2,1)S(1)} %bitcast.19, bf16[768,2048]{1,0:T(8,128)(2,1)S(1)} %bitcast.20, bf16[768,2048]{1,0:T(8,128)(2,1)S(1)} %bitcast.21, bf16[768,2048]{1,0:T(8,128)(2,1)S(1)} %bitcast.22, bf16[128,128]{1,0:T(8,128)(2,1)S(1)} %convert_element_type.3.refs_4_), custom_call_target="tpu_custom_call" | custom-call | flops 1509949440 | bytes 9830400 | tf_op jit(solution)/shard_map/pallas_call | solution.py:225
  123.9 0.0 copy-done
  123.9 1.0 copy-done.2
  124.9 7.9 %all-to-all-start.1 = ((bf16[32,24,640]{2,1,0:T(8,128)(2,1)}), bf16[32,24,640]{2,1,0:T(8,128)(2,1)S(1)}, u32[]{:S(2)}, u32[]{:S(2)}) async-start(bf16[32,24,640]{2,1,0:T(8,128)(2,1)} %bitcast.27), calls=%async_computation.1 | async-start | bytes 1966080 | tf_op jit(solution)/shard_map/all_to_all | solution.py:315
  132.9 0.6 pad_add_fusion.order_ref
  133.4 1.9 constant_dynamic-update-slice_fusion.4
  135.3 1.9 constant_dynamic-update-slice_fusion.3
  137.2 0.0 copy-done.7
  137.2 0.8 constant_dynamic-update-slice_fusion.2
  138.0 0.0 copy-done.9
  138.0 0.8 constant_dynamic-update-slice_fusion.1
  138.9 0.0 collective-permute-done.3
  138.9 3.0 %constant_dynamic-update-slice_fusion.grad_ref = bf16[8,384,640]{2,1,0:T(8,128)(2,1)} fusion(bf16[8,384,640]{2,1,0:T(8,128)(2,1)} %constant_dynamic-update-slice_fusion.1, bf16[4,384,640]{2,1,0:T(8,128)(2,1)} %collective-permute-done.3), kind=kLoop, calls=%fused_computation.1 | loop fusion | bytes 3932160 | tf_op jit(solution)/shard_map/concatenate | solution.py:183
  141.9 11.1 %shard_map.114 = bf16[768,640]{1,0:T(8,128)(2,1)} custom-call(s32[8]{0:T(128)} %pad_add_fusion.order_ref, bf16[8,384,640]{2,1,0:T(8,128)(2,1)} %constant_dynamic-update-slice_fusion.grad_ref, bf16[5120,640]{1,0:T(8,128)(2,1)} %all-gather.2.cloned.1.call-done.weight_ref, s32[1,384]{1,0:T(1,128)} %get-tuple-element.15.dest_row), custom_call_target="tpu_custom_call" | custom-call | flops 2894069760 | bytes 10485760 | tf_op jit(solution)/shard_map/pallas_call | solution.py:118
  153.0 7.2 %all-to-all-done.1 = bf16[32,24,640]{2,1,0:T(8,128)(2,1)S(1)} async-done(((bf16[32,24,640]{2,1,0:T(8,128)(2,1)}), bf16[32,24,640]{2,1,0:T(8,128)(2,1)S(1)}, u32[]{:S(2)}, u32[]{:S(2)}) %all-to-all-start.1) | async-done | bytes 983072 | tf_op jit(solution)/shard_map/all_to_all | solution.py:315
  160.2 4.9 %all-to-all-start.2 = ((bf16[32,24,640]{2,1,0:T(8,128)(2,1)}), bf16[32,24,640]{2,1,0:T(8,128)(2,1)S(1)}, u32[]{:S(2)}, u32[]{:S(2)}) async-start(bf16[32,24,640]{2,1,0:T(8,128)(2,1)} %bitcast.31), calls=%async_computation.3 | async-start | bytes 1966080 | tf_op jit(solution)/shard_map/all_to_all | solution.py:315
  165.1 0.2 reduce-scatter.2.cloned.1.call-start
  165.4 0.0 copy-done.4
  165.4 8.6 %shard_map.113 = bf16[8,384,640]{2,1,0:T(8,128)(2,1)S(1)} custom-call(s32[384,128]{1,0:T(8,128)S(1)} %copy-done.4, bf16[768,640]{1,0:T(8,128)(2,1)S(1)} %bitcast.28, bf16[5120,640]{1,0:T(8,128)(2,1)} %all-gather.2.cloned.1.call-done.weight_ref), custom_call_target="tpu_custom_call" | custom-call | flops 2894069760 | bytes 10485760 | tf_op jit(solution)/shard_map/pallas_call | solution.py:153
  173.9 0.0 copy-start.1
  173.9 1.9 copy-done.1
  175.8 0.0 reduce-scatter.2.cloned.1.call-update
  175.8 16.3 %all-to-all-done.2 = bf16[32,24,640]{2,1,0:T(8,128)(2,1)S(1)} async-done(((bf16[32,24,640]{2,1,0:T(8,128)(2,1)}), bf16[32,24,640]{2,1,0:T(8,128)(2,1)S(1)}, u32[]{:S(2)}, u32[]{:S(2)}) %all-to-all-start.2) | async-done | bytes 983072 | tf_op jit(solution)/shard_map/all_to_all | solution.py:315
  192.1 0.0 copy-done.3
  192.1 8.9 %shard_map.115 = bf16[768,1920]{1,0:T(8,128)(2,1)S(1)} custom-call(bf16[768,2048]{1,0:T(8,128)(2,1)} %bitcast.23, bf16[768,2048]{1,0:T(8,128)(2,1)} %bitcast.24, bf16[768,2048]{1,0:T(8,128)(2,1)} %bitcast.25, bf16[768,640]{1,0:T(8,128)(2,1)S(1)} %copy-done.3, bf16[768,640]{1,0:T(8,128)(2,1)S(1)} %bitcast.29, bf16[5,768,768]{2,1,0:T(8,128)(2,1)} %get-tuple-element.16.refs_5_), custom_call_target="tpu_custom_call" | custom-call | flops 3019898880 | bytes 13762560 | tf_op jit(solution)/shard_map/pallas_call | solution.py:256
  201.0 73.8 %all_to_all.20 = bf16[32,24,1920]{2,1,0:T(8,128)(2,1)S(1)} all-to-all(bf16[32,24,1920]{2,1,0:T(8,128)(2,1)S(1)} %bitcast.26), channel_id=1, replica_groups=mesh['seq'=32,'tp'=8] {'seq'}, dimensions={0} | all-to-all | bytes 5898240 | tf_op jit(solution)/shard_map/all_to_all | solution.py:315
  274.8 3.9 %shard_map.116 = (bf16[384,640]{1,0:T(8,128)(2,1)}, bf16[384,640]{1,0:T(8,128)(2,1)}, bf16[384,640]{1,0:T(8,128)(2,1)}) custom-call(s32[384,128]{1,0:T(8,128)S(1)} %copy-done.4, bf16[768,1920]{1,0:T(8,128)(2,1)S(1)} %bitcast.30), custom_call_target="tpu_custom_call" | custom-call | flops 1132462080 | bytes 4423680 | tf_op jit(solution)/shard_map/pallas_call | solution.py:293
  (10 shorter events, 0.0 us)
Async XLA Ops:
  7.2 134.7 %all-gather.2.cloned.1.call-start = ((), (), s32[]{:S(2)}) async-start(), calls=%async_computation.5 | async-start | bytes 6758400 | tf_op jit(solution)/shard_map/all_gather | solution.py:325
  13.8 39.8 %copy-start.10 = (s32[128,128]{1,0:T(8,128)S(1)}, s32[128,128]{1,0:T(8,128)}, u32[]{:S(2)}) copy-start(s32[128,128]{1,0:T(8,128)} %param.15) | copy-start | bytes 196612
  13.8 101.3 %all-to-all-start = ((bf16[32,24,2048]{2,1,0:T(8,128)(2,1)}), bf16[32,24,2048]{2,1,0:T(8,128)(2,1)S(1)}, u32[]{:S(2)}, u32[]{:S(2)}) async-start(bf16[32,24,2048]{2,1,0:T(8,128)(2,1)} %bitcast.32), calls=%async_computation | async-start | bytes 6291456 | tf_op jit(solution)/shard_map/all_to_all | solution.py:315
  25.4 14.5 %collective-permute-start = (bf16[384,640]{1,0:T(8,128)(2,1)}, bf16[384,640]{1,0:T(8,128)(2,1)S(1)}, u32[]{:S(2)}, u32[]{:S(2)}) collective-permute-start(bf16[384,640]{1,0:T(8,128)(2,1)} %param.12), channel_id=1, source_target_pairs={{0,2},{1,3},{2,4},{3,5},{4,6},{5,7},{6,0},{7,1},{8,10},{9,11},{10,... | collective-permute-start | bytes 1474568 | tf_op jit(solution)/shard_map/ppermute | solution.py:178
  26.7 22.2 %collective-permute-start.1 = (bf16[384,640]{1,0:T(8,128)(2,1)}, bf16[384,640]{1,0:T(8,128)(2,1)S(1)}, u32[]{:S(2)}, u32[]{:S(2)}) collective-permute-start(bf16[384,640]{1,0:T(8,128)(2,1)} %param.12), channel_id=1, source_target_pairs={{0,4},{1,5},{2,6},{3,7},{4,0},{5,1},{6,2},{7,3},{8,12},{9,13},{10,... | collective-permute-start | bytes 1474568 | tf_op jit(solution)/shard_map/ppermute | solution.py:178
  27.5 23.3 %collective-permute-start.2 = (bf16[384,640]{1,0:T(8,128)(2,1)}, bf16[384,640]{1,0:T(8,128)(2,1)S(1)}, u32[]{:S(2)}, u32[]{:S(2)}) collective-permute-start(bf16[384,640]{1,0:T(8,128)(2,1)} %param.12), channel_id=1, source_target_pairs={{0,6},{1,7},{2,0},{3,1},{4,2},{5,3},{6,4},{7,5},{8,14},{9,15},{10,... | collective-permute-start | bytes 1474568 | tf_op jit(solution)/shard_map/ppermute | solution.py:178
  39.9 13.7 %copy-start.5 = (bf16[384,640]{1,0:T(8,128)(2,1)}, bf16[384,640]{1,0:T(8,128)(2,1)S(1)}, u32[]{:S(2)}) copy-start(bf16[384,640]{1,0:T(8,128)(2,1)S(1)} %collective-permute-done) | copy-start | bytes 1474564
  48.9 4.7 %copy-start.6 = (bf16[384,640]{1,0:T(8,128)(2,1)}, bf16[384,640]{1,0:T(8,128)(2,1)S(1)}, u32[]{:S(2)}) copy-start(bf16[384,640]{1,0:T(8,128)(2,1)S(1)} %collective-permute-done.1) | copy-start | bytes 1474564
  50.7 2.8 copy-start.8
  53.6 85.3 %collective-permute-start.3 = (bf16[4,384,640]{2,1,0:T(8,128)(2,1)}, bf16[4,384,640]{2,1,0:T(8,128)(2,1)}, u32[]{:S(2)}, u32[]{:S(2)}) collective-permute-start(bf16[4,384,640]{2,1,0:T(8,128)(2,1)} %pad_maximum_fusion), channel_id=1, source_target_pairs={{0,1},{1,0},{2,3},{3,2},{4,5},{5,4},{6,7},{7,6},{8,9},{9,8},{10,11... | collective-permute-start | bytes 5898248 | tf_op jit(solution)/shard_map/ppermute | solution.py:180
  115.1 8.8 %copy-start = (bf16[32,24,2048]{2,1,0:T(8,128)(2,1)}, bf16[32,24,2048]{2,1,0:T(8,128)(2,1)S(1)}, u32[]{:S(2)}) copy-start(bf16[32,24,2048]{2,1,0:T(8,128)(2,1)S(1)} %all-to-all-done) | copy-start | bytes 9437188
  123.9 1.0 copy-start.2
  124.9 12.3 %copy-start.7 = (bf16[384,640]{1,0:T(8,128)(2,1)S(1)}, bf16[384,640]{1,0:T(8,128)(2,1)}, u32[]{:S(2)}) copy-start(bf16[384,640]{1,0:T(8,128)(2,1)} %copy-done.6) | copy-start | bytes 1474564
  124.9 13.1 %copy-start.9 = (bf16[384,640]{1,0:T(8,128)(2,1)S(1)}, bf16[384,640]{1,0:T(8,128)(2,1)}, u32[]{:S(2)}) copy-start(bf16[384,640]{1,0:T(8,128)(2,1)} %copy-done.8) | copy-start | bytes 1474564
  124.9 35.3 %all-to-all-start.1 = ((bf16[32,24,640]{2,1,0:T(8,128)(2,1)}), bf16[32,24,640]{2,1,0:T(8,128)(2,1)S(1)}, u32[]{:S(2)}, u32[]{:S(2)}) async-start(bf16[32,24,640]{2,1,0:T(8,128)(2,1)} %bitcast.27), calls=%async_computation.1 | async-start | bytes 1966080 | tf_op jit(solution)/shard_map/all_to_all | solution.py:315
  141.9 23.5 %copy-start.4 = (s32[384,128]{1,0:T(8,128)S(1)}, s32[384,128]{1,0:T(8,128)}, u32[]{:S(2)}) copy-start(s32[384,128]{1,0:T(8,128)} %get-tuple-element.12.dest_col.dest_ref) | copy-start | bytes 589828
  160.2 31.9 %all-to-all-start.2 = ((bf16[32,24,640]{2,1,0:T(8,128)(2,1)}), bf16[32,24,640]{2,1,0:T(8,128)(2,1)S(1)}, u32[]{:S(2)}, u32[]{:S(2)}) async-start(bf16[32,24,640]{2,1,0:T(8,128)(2,1)} %bitcast.31), calls=%async_computation.3 | async-start | bytes 1966080 | tf_op jit(solution)/shard_map/all_to_all | solution.py:315
  165.1 113.5 %reduce-scatter.2.cloned.1.call-start = ((), (), s32[]{:S(2)}) async-start(), calls=%async_computation.6 | async-start | bytes 4423680 | tf_op jit(solution)/shard_map/reduce_scatter | solution.py:335
  173.9 1.9 copy-start.1
  175.8 16.3 %copy-start.3 = (bf16[768,640]{1,0:T(8,128)(2,1)S(1)}, bf16[768,640]{1,0:T(8,128)(2,1)}, u32[]{:S(2)}) copy-start(bf16[768,640]{1,0:T(8,128)(2,1)} %copy-done.2) | copy-start | bytes 2949124
Sparse Core Ops, SparseCore 0:
  10.6 124.6 all-gather.1
  176.0 36.3 reduce-scatter.1

commit v5 on v4

--- a/solution.py
+++ b/solution.py
@@ -8,6 +8,8 @@
 HEAD = 128
 NEG_FILL = -1e30
 LOG2_E = 1.4426950408889634
+Y_COUNT = 4
+Z_COUNT = 8
 VMEM_BYTES = 48 * 1024 * 1024
 VMEM_WHOLE = 60 * 1024 * 1024
 NT = (((1,), (1,)), ((), ()))
@@ -35,7 +37,7 @@
 
 
 def pack_kernel(
-    seq_count, slot_size, label_row, owner_row_ref, q_ref, k_ref, v_ref, packed, dest_row, dest_col, held, parts, in_sems, out_sems
+    seq_count, slot_size, label_row, owner_row_ref, q_ref, k_ref, v_ref, packed, dest_row, dest_col, code_row, held, parts, in_sems, out_sems
 ):
     sources = (q_ref, k_ref, v_ref)
     rows, cols = q_ref.shape
@@ -57,7 +59,6 @@
     dest = owner_row * slot_size + rank_row.astype(jnp.int32)
     dest_row[...] = dest
     select = as_bf16(lax.broadcasted_iota(jnp.int32, (buffer_rows, rows), 0) == dest)
-    width = 3 * cols
     stores = []
 
     def store(start, stop):
@@ -69,8 +70,8 @@
         load.wait()
         parts[:, i * cols : (i + 1) * cols] = dot32(select, held[i]).astype(jnp.bfloat16)
         store(i * cols, (i + 1) * cols)
-    parts[:, width:] = dot32(select, column_of(labels + 1).astype(jnp.bfloat16)).astype(jnp.bfloat16)
-    store(width, width + HEAD)
+    codes = jnp.broadcast_to((labels + 1).astype(jnp.float32), (16, rows)).astype(jnp.bfloat16)
+    code_row[...] = dot32_nt(codes, select)[0:1].astype(jnp.int32)
     dest_col[...] = column_of(dest).astype(jnp.int32)
     for copy in stores:
         copy.wait()
@@ -82,30 +83,38 @@
     return pl.pallas_call(
         lambda *refs: pack_kernel(seq_count, slot_size, *refs),
         out_shape=(
-            jax.ShapeDtypeStruct((buffer_rows, 3 * cols + HEAD), jnp.bfloat16),
+            jax.ShapeDtypeStruct((buffer_rows, 3 * cols), jnp.bfloat16),
             jax.ShapeDtypeStruct((1, rows), jnp.int32),
             jax.ShapeDtypeStruct((rows, HEAD), jnp.int32),
+            jax.ShapeDtypeStruct((1, buffer_rows), jnp.int32),
         ),
         in_specs=[pl.BlockSpec(memory_space=pltpu.VMEM)] * 2 + [pl.BlockSpec(memory_space=pl.ANY)] * 3,
-        out_specs=(pl.BlockSpec(memory_space=pl.ANY),) + (pl.BlockSpec(memory_space=pltpu.VMEM),) * 2,
+        out_specs=(pl.BlockSpec(memory_space=pl.ANY),) + (pl.BlockSpec(memory_space=pltpu.VMEM),) * 3,
         scratch_shapes=[
             pltpu.VMEM((3, rows, cols), jnp.bfloat16),
-            pltpu.VMEM((buffer_rows, 3 * cols + HEAD), jnp.bfloat16),
+            pltpu.VMEM((buffer_rows, 3 * cols), jnp.bfloat16),
             pltpu.SemaphoreType.DMA((3,)),
-            pltpu.SemaphoreType.DMA((4,)),
+            pltpu.SemaphoreType.DMA((3,)),
         ],
         compiler_params=params(VMEM_WHOLE),
     )(labels, owner_map[None, :], queries, key_rows, values)
 
 
-def grad_kernel(order_ref, grad_ref, weight_ref, dest_row, packed, total):
+def grad_kernel(order_ref, near_ref, far_ref, weight_ref, dest_row, packed, total):
     step = pl.program_id(0)
+    half = pl.num_programs(0) // 2
 
     @pl.when(step == 0)
     def _():
         total[...] = jnp.zeros_like(total)
 
-    total[...] += dot32(grad_ref[0], weight_ref[...])
+    @pl.when(step < half)
+    def _():
+        total[...] += dot32(near_ref[0], weight_ref[...])
+
+    @pl.when(step >= half)
+    def _():
+        total[...] += dot32(far_ref[0], weight_ref[...])
 
     @pl.when(step == pl.num_programs(0) - 1)
     def _():
@@ -113,15 +122,17 @@
         packed[...] = dot32(select, total[...].astype(jnp.bfloat16)).astype(jnp.bfloat16)
 
 
-def project_grads(order, grad_blocks, weight_t, dest_row, buffer_rows):
-    groups, rows, width = grad_blocks.shape
+def project_grads(order, near, far, weight_t, dest_row, buffer_rows):
+    half, rows, width = near.shape
+    groups = 2 * half
     return pl.pallas_call(
         grad_kernel,
         grid_spec=pltpu.PrefetchScalarGridSpec(
             num_scalar_prefetch=1,
             grid=(groups,),
             in_specs=[
-                pl.BlockSpec((1, rows, width), lambda g, order: (g, 0, 0)),
+                pl.BlockSpec((1, rows, width), lambda g, order: (jnp.minimum(g, half - 1), 0, 0)),
+                pl.BlockSpec((1, rows, width), lambda g, order: (jnp.maximum(g - half, 0), 0, 0)),
                 pl.BlockSpec((width, width), lambda g, order: (order[g], 0)),
                 pl.BlockSpec((1, rows), lambda g, order: (0, 0)),
             ],
@@ -135,7 +146,7 @@
             bytes_accessed=2 * groups * width * (rows + width),
             transcendentals=0,
         ),
-    )(order, grad_blocks, weight_t, dest_row)
+    )(order, near, far, weight_t, dest_row)
 
 
 def output_kernel(dest_col, returned, weight_ref, out_ref, local):
@@ -180,7 +191,27 @@
     far = lax.ppermute(near, "tp", [(t, t ^ 1) for t in range(tp_count)])
     me = lax.axis_index("tp")
     own = (me + tp_count - 2 * jnp.arange(half, dtype=jnp.int32)) % tp_count
-    return jnp.concatenate([near, far], axis=0), jnp.concatenate([own, own ^ 1])
+    return near, far, jnp.concatenate([own, own ^ 1])
+
+
+def gather_codes(code_row, slot_size):
+    def move(block, along_y, along_z):
+        steps = [
+            (y * Z_COUNT + z, (y + along_y) % Y_COUNT * Z_COUNT + (z + along_z) % Z_COUNT)
+            for y in range(Y_COUNT)
+            for z in range(Z_COUNT)
+        ]
+        return lax.ppermute(block, "seq", steps)
+
+    rows = jnp.concatenate([code_row] + [move(code_row, turn, 0) for turn in range(1, Y_COUNT)])
+    table = jnp.concatenate([rows] + [move(rows, 0, turn) for turn in range(1, Z_COUNT)])
+    me = lax.axis_index("seq")
+    mine = lax.dynamic_slice_in_dim(table, me * slot_size, slot_size, 1)
+    source = jnp.arange(Y_COUNT * Z_COUNT, dtype=jnp.int32)
+    turn_y = (me // Z_COUNT - source // Z_COUNT + Y_COUNT) % Y_COUNT
+    turn_z = (me - source + Y_COUNT * Z_COUNT) % Z_COUNT
+    codes = mine[turn_z * Y_COUNT + turn_y].reshape(-1, 1)
+    return jnp.broadcast_to(codes, (codes.shape[0], HEAD)).astype(jnp.bfloat16)
 
 
 def forward_kernel(scale, q_ref, k_ref, v_ref, code_ref, mask_ref, att_ref, weight_ref, keys, asks):
@@ -219,7 +250,7 @@
     out_ref[:, 2 * HEAD :] = dot32(weights, grad).astype(jnp.bfloat16)
 
 
-def attention_forward(owned, pair_mask, heads, scale):
+def attention_forward(owned, codes, pair_mask, heads, scale):
     rows = owned.shape[0]
     block = (rows, HEAD)
     return pl.pallas_call(
@@ -229,7 +260,7 @@
             pl.BlockSpec(block, lambda h: (0, h)),
             pl.BlockSpec(block, lambda h: (0, heads + h)),
             pl.BlockSpec(block, lambda h: (0, 2 * heads + h)),
-            pl.BlockSpec(block, lambda h: (0, 3 * heads)),
+            pl.BlockSpec(block, lambda h: (0, 0)),
             pl.BlockSpec(pair_mask.shape, lambda h: (0, 0)),
         ],
         out_specs=(
@@ -247,7 +278,7 @@
             bytes_accessed=heads * rows * (8 * HEAD + 2 * rows),
             transcendentals=heads * rows * rows,
         ),
-    )(owned, owned, owned, owned, pair_mask)
+    )(owned, owned, owned, codes, pair_mask)
 
 
 def attention_backward(owned, attended, grad_owned, weights, heads, scale):
@@ -323,14 +354,16 @@
     buffer_rows = seq_count * slot_size
     scale = HEAD ** (-0.5)
     weight_t = lax.all_gather(out_weight.T, "seq", axis=0, tiled=True)
-    grad_blocks, order = gather_groups(grad_out)
-    packed, dest_row, dest_col = pack_inputs(
+    near, far, order = gather_groups(grad_out)
+    packed, dest_row, dest_col, code_row = pack_inputs(
         seq_count, slot_size, labels, owner_map, queries, key_rows, values
     )
     owned = exchange(packed, seq_count)
-    attended, weights = attention_forward(owned, pair_mask.astype(jnp.bfloat16), heads, scale)
+    code_row, near = lax.optimization_barrier((code_row, near))
+    codes = gather_codes(code_row, slot_size)
+    attended, weights = attention_forward(owned, codes, pair_mask.astype(jnp.bfloat16), heads, scale)
     returned = exchange(attended, seq_count)
-    grad_owned = exchange(project_grads(order, grad_blocks, weight_t, dest_row, buffer_rows), seq_count)
+    grad_owned = exchange(project_grads(order, near, far, weight_t, dest_row, buffer_rows), seq_count)
     partial_out = project_output(dest_col, returned, weight_t, lax.axis_size("tp"))
     output = lax.psum_scatter(partial_out, "tp", scatter_dimension=0, tiled=False)
     grads = attention_backward(owned, attended, grad_owned, weights, heads, scale)

time: 287 us -> 281 us (0.979)
  starting transfers between devices: 28 us -> 45.9 us
  waiting for transfers between devices: 108 us -> 96.1 us
  local copies, waits for them, and re-layouts: 11.3 us -> 3.87 us
  blocking collectives: 73.8 us -> 70.5 us
    all_to_all x3, waiting for transfers between devices: 85 us -> 26.6 us  [exchange(): lax.all_to_all(blocks, 'seq', split_axis=0, concat_axis=0, tiled=True)]
    ppermute x0 -> x10, waiting for transfers between devices: none -> 49.2 us  [move(): return lax.ppermute(block, 'seq', steps)]
    ppermute x0 -> x10, starting transfers between devices: none -> 19.4 us  [move(): return lax.ppermute(block, 'seq', steps)]
    unnamed x26 -> x16, local copies, waits for them, and re-layouts: 8.27 us -> 2.85 us
    all_to_all x1, blocking collectives: 73.8 us -> 70.5 us  [exchange(): lax.all_to_all(blocks, 'seq', split_axis=0, concat_axis=0, tiled=True)]
    concatenate x1, local copies, waits for them, and re-layouts: 2.98 us -> 0.11 us  [gather_codes(): jnp.concatenate([rows] + [move(rows, 0, turn) for turn in range(1, Z_COUN...]
  transfers between devices with their start and end apart: 9 -> 19, of which waited for: 6 -> 11; matrix products, arithmetic and copies ran while one was open for 4% -> 1% of each run, Pallas kernels for 17% -> 17%
where the time goes in v5:
time: 281 us; the launch traced here: 280 us
  waiting for transfers between devices  96.1 us (34%)
  blocking collectives  70.5 us (25%)
  Pallas kernels  46.9 us (17%)
  starting transfers between devices  45.9 us (16%)
  between operations  14.2 us (5%)
  local copies, waits for them, and re-layouts  3.87 us (1%)
    all_to_all x1, blocking collectives, exchange(): lax.all_to_all(blocks, 'seq', split_axis=0, concat_axis=0, tiled=True)  70.5 us
    ppermute x10, waiting for transfers between devices, move(): return lax.ppermute(block, 'seq', steps)  49.2 us
    all_to_all x3, waiting for transfers between devices, exchange(): lax.all_to_all(blocks, 'seq', split_axis=0, concat_axis=0, tiled=True)  26.6 us
    all_to_all x3, starting transfers between devices, exchange(): lax.all_to_all(blocks, 'seq', split_axis=0, concat_axis=0, tiled=True)  22.5 us
    ppermute x3, waiting for transfers between devices, gather_groups(): lax.ppermute(block, 'tp', [(t, (t + 2 * shift) % tp_count) for t in range...  19.5 us
    ppermute x10, starting transfers between devices, move(): return lax.ppermute(block, 'seq', steps)  19.4 us
    pallas_call x1, Pallas kernels, project_grads(): pl.pallas_call(grad_kernel, grid_spec=pltpu.PrefetchScalarGridSpec(num_sc...  11.2 us
    pallas_call x1, Pallas kernels, attention_backward(): pl.pallas_call(lambda *refs: backward_kernel(scale, *refs), grid=(heads,)...  8.95 us
  transfers between devices with their start and end apart: 19, of which 11 were waited for; matrix products, arithmetic and copies ran while one was open for 1% of the time, Pallas kernels for 17%

profile of v5, /device:TPU:4, one launch (start us, length us, event | category | flops | bytes accessed | tf_op | source)
XLA Modules:
  0.0 279.6 jit_solution(12549249316892591139)
XLA Ops:
  7.2 0.0 all-gather.2.cloned.1.call-start
  7.2 0.7 all-gather.2.cloned.1.call-update
  7.9 5.8 %shard_map.111 = (bf16[768,1920]{1,0:T(8,128)(2,1)}, s32[1,384]{1,0:T(1,128)}, s32[384,128]{1,0:T(8,128)}, s32[1,768]{1,0:T(1,128)}) custom-call(s32[384]{0:T(512)} %refs_0_.1, s32[1,128]{1,0:T(1,128)} %bitcast.35, bf16[384,640]{1,0:T(8,128)(2,1)} %refs_2_.1, bf16[384,640]{1,0:T(8,128)(2,1)} %refs_3_.1, bf16[384,640]{1,0:T(8,128)(2,1)} %refs_4_.1), custom_call_target="tpu_custom_call" | custom-call | tf_op jit(solution)/shard_map/pallas_call | solution.py:83
  13.7 11.6 %all-to-all-start = ((bf16[32,24,1920]{2,1,0:T(8,128)(2,1)}), bf16[32,24,1920]{2,1,0:T(8,128)(2,1)S(1)}, u32[]{:S(2)}, u32[]{:S(2)}) async-start(bf16[32,24,1920]{2,1,0:T(8,128)(2,1)} %bitcast.29), calls=%async_computation | async-start | bytes 5898240 | tf_op jit(solution)/shard_map/all_to_all | solution.py:346
  25.3 1.3 collective-permute-start
  26.6 0.8 collective-permute-start.2
  27.4 1.7 collective-permute-start.1
  29.2 10.4 %collective-permute-done = bf16[384,640]{1,0:T(8,128)(2,1)S(1)} collective-permute-done((bf16[384,640]{1,0:T(8,128)(2,1)S(1)}, bf16[384,640]{1,0:T(8,128)(2,1)S(1)}, u32[]{:S(2)}, u32[]{:S(2)}) %collective-permute-start) | collective-permute-done | bytes 491552 | tf_op jit(solution)/shard_map/ppermute | solution.py:189
  39.6 1.2 collective-permute-done.2
  40.8 7.9 %collective-permute-done.1 = bf16[384,640]{1,0:T(8,128)(2,1)S(1)} collective-permute-done((bf16[384,640]{1,0:T(8,128)(2,1)S(1)}, bf16[384,640]{1,0:T(8,128)(2,1)S(1)}, u32[]{:S(2)}, u32[]{:S(2)}) %collective-permute-start.1) | collective-permute-done | bytes 491552 | tf_op jit(solution)/shard_map/ppermute | solution.py:189
  48.6 1.5 pad_maximum_fusion.near_ref
  50.2 2.8 collective-permute-start.5
  52.9 0.8 collective-permute-start.4
  53.8 0.9 collective-permute-start.3
  54.6 3.4 %collective-permute-done.4 = s32[1,768]{1,0:T(1,128)S(1)} collective-permute-done((s32[1,768]{1,0:T(1,128)S(1)}, s32[1,768]{1,0:T(1,128)S(1)}, u32[]{:S(2)}, u32[]{:S(2)}) %collective-permute-start.4) | collective-permute-done | bytes 3104 | tf_op jit(solution)/shard_map/ppermute | solution.py:204
  58.1 0.5 collective-permute-done.3
  58.6 2.8 collective-permute-start.12
  61.4 2.4 collective-permute-start.11
  63.7 1.5 collective-permute-start.10
  65.2 0.1 collective-permute-start.13
  65.3 3.7 %collective-permute-start.9 = (s32[4,768]{1,0:T(4,128)S(1)}, s32[4,768]{1,0:T(4,128)S(1)}, u32[]{:S(2)}, u32[]{:S(2)}) collective-permute-start(s32[4,768]{1,0:T(4,128)S(1)} %pad_add_fusion), channel_id=1, source_target_pairs={{0,32},{8,40},{16,48},{24,56},{32,0},{40,8},{48,16},{56,24},{64,96... | collective-permute-start | bytes 36872 | tf_op jit(solution)/shard_map/ppermute | solution.py:204
  69.0 40.8 %collective-permute-done.12 = s32[4,768]{1,0:T(4,128)S(1)} collective-permute-done((s32[4,768]{1,0:T(4,128)S(1)}, s32[4,768]{1,0:T(4,128)S(1)}, u32[]{:S(2)}, u32[]{:S(2)}) %collective-permute-start.12) | collective-permute-done | bytes 12320 | tf_op jit(solution)/shard_map/ppermute | solution.py:204
  109.7 2.4 collective-permute-start.8
  112.1 1.8 collective-permute-start.7
  113.9 0.6 collective-permute-start.6
  114.5 2.2 collective-permute-done.8
  116.7 1.5 collective-permute-done.7
  118.1 0.9 collective-permute-done.6
  119.0 0.1 concatenate.11
  119.1 0.1 constant_dynamic-slice_fusion
  119.2 0.6 gather_fusion
  119.8 0.1 convert_element_type.9
  119.9 0.2 broadcast_in_dim.10.refs_3_
  120.1 8.6 %shard_map.112 = (bf16[768,640]{1,0:T(8,128)(2,1)S(1)}, bf16[5,768,768]{2,1,0:T(8,128)(2,1)}) custom-call(bf16[768,1920]{1,0:T(8,128)(2,1)S(1)} %bitcast.17, bf16[768,1920]{1,0:T(8,128)(2,1)S(1)} %bitcast.18, bf16[768,1920]{1,0:T(8,128)(2,1)S(1)} %bitcast.19, bf16[768,128]{1,0:T(8,128)(2,1)S(1)} %broadcast_in_dim.10.refs_3_, ...), custom_call_target="tpu_custom_call" | custom-call | flops 1509949440 | bytes 9830400 | tf_op jit(solution)/shard_map/pallas_call | solution.py:256
  128.6 1.0 copy-done.2
  129.6 5.8 %all-to-all-start.1 = ((bf16[32,24,640]{2,1,0:T(8,128)(2,1)}), bf16[32,24,640]{2,1,0:T(8,128)(2,1)S(1)}, u32[]{:S(2)}, u32[]{:S(2)}) async-start(bf16[32,24,640]{2,1,0:T(8,128)(2,1)} %bitcast.24), calls=%async_computation.1 | async-start | bytes 1966080 | tf_op jit(solution)/shard_map/all_to_all | solution.py:346
  135.4 0.6 pad_add_fusion.1.order_ref
  136.0 11.2 %shard_map.114 = bf16[768,640]{1,0:T(8,128)(2,1)} custom-call(s32[8]{0:T(128)} %pad_add_fusion.1.order_ref, bf16[4,384,640]{2,1,0:T(8,128)(2,1)} %pad_maximum_fusion.near_ref, bf16[4,384,640]{2,1,0:T(8,128)(2,1)} %collective-permute-done.13.far_ref, bf16[5120,640]{1,0:T(8,128)(2,1)} %all-gather.2.cloned.1.call-done.weight_ref, ...), custom_call_target="tpu_custom_call" | custom-call | flops 2894069760 | bytes 10485760 | tf_op jit(solution)/shard_map/pallas_call | solution.py:128
  147.2 13.3 %all-to-all-done.1 = bf16[32,24,640]{2,1,0:T(8,128)(2,1)S(1)} async-done(((bf16[32,24,640]{2,1,0:T(8,128)(2,1)}), bf16[32,24,640]{2,1,0:T(8,128)(2,1)S(1)}, u32[]{:S(2)}, u32[]{:S(2)}) %all-to-all-start.1) | async-done | bytes 983072 | tf_op jit(solution)/shard_map/all_to_all | solution.py:346
  160.5 5.1 %all-to-all-start.2 = ((bf16[32,24,640]{2,1,0:T(8,128)(2,1)}), bf16[32,24,640]{2,1,0:T(8,128)(2,1)S(1)}, u32[]{:S(2)}, u32[]{:S(2)}) async-start(bf16[32,24,640]{2,1,0:T(8,128)(2,1)} %bitcast.28), calls=%async_computation.3 | async-start | bytes 1966080 | tf_op jit(solution)/shard_map/all_to_all | solution.py:346
  165.5 0.0 reduce-scatter.2.cloned.1.call-start
  165.6 8.6 %shard_map.113 = bf16[8,384,640]{2,1,0:T(8,128)(2,1)S(1)} custom-call(s32[384,128]{1,0:T(8,128)S(1)} %copy-done.4, bf16[768,640]{1,0:T(8,128)(2,1)S(1)} %bitcast.25, bf16[5120,640]{1,0:T(8,128)(2,1)} %all-gather.2.cloned.1.call-done.weight_ref), custom_call_target="tpu_custom_call" | custom-call | flops 2894069760 | bytes 10485760 | tf_op jit(solution)/shard_map/pallas_call | solution.py:164
  174.2 1.9 copy-done.1
  176.0 0.0 reduce-scatter.2.cloned.1.call-update
  176.1 13.3 %all-to-all-done.2 = bf16[32,24,640]{2,1,0:T(8,128)(2,1)S(1)} async-done(((bf16[32,24,640]{2,1,0:T(8,128)(2,1)}), bf16[32,24,640]{2,1,0:T(8,128)(2,1)S(1)}, u32[]{:S(2)}, u32[]{:S(2)}) %all-to-all-start.2) | async-done | bytes 983072 | tf_op jit(solution)/shard_map/all_to_all | solution.py:346
  189.4 9.0 %shard_map.115 = bf16[768,1920]{1,0:T(8,128)(2,1)S(1)} custom-call(bf16[768,1920]{1,0:T(8,128)(2,1)} %bitcast.20, bf16[768,1920]{1,0:T(8,128)(2,1)} %bitcast.21, bf16[768,1920]{1,0:T(8,128)(2,1)} %bitcast.22, bf16[768,640]{1,0:T(8,128)(2,1)S(1)} %copy-done.3, bf16[768,640]{1,0:T(8,128)(2,1)S(1)} %bitcast.26, bf16[5,768,768]{2,1,0:T(8,128)(2,1)} %get-tuple-element.22.refs_5_), custom_call_target="tpu_custom_call" | custom-call | flops 3019898880 | bytes 13762560 | tf_op jit(solution)/shard_map/pallas_call | solution.py:287
  198.4 70.5 %all_to_all.20 = bf16[32,24,1920]{2,1,0:T(8,128)(2,1)S(1)} all-to-all(bf16[32,24,1920]{2,1,0:T(8,128)(2,1)S(1)} %bitcast.23), channel_id=1, replica_groups=mesh['seq'=32,'tp'=8] {'seq'}, dimensions={0} | all-to-all | bytes 5898240 | tf_op jit(solution)/shard_map/all_to_all | solution.py:346
  268.8 3.9 %shard_map.116 = (bf16[384,640]{1,0:T(8,128)(2,1)}, bf16[384,640]{1,0:T(8,128)(2,1)}, bf16[384,640]{1,0:T(8,128)(2,1)}) custom-call(s32[384,128]{1,0:T(8,128)S(1)} %copy-done.4, bf16[768,1920]{1,0:T(8,128)(2,1)S(1)} %bitcast.27), custom_call_target="tpu_custom_call" | custom-call | flops 1132462080 | bytes 4423680 | tf_op jit(solution)/shard_map/pallas_call | solution.py:324
  (28 shorter events, 0.1 us)
Async XLA Ops:
  7.2 128.8 %all-gather.2.cloned.1.call-start = ((), (), s32[]{:S(2)}) async-start(), calls=%async_computation.5 | async-start | bytes 6758400 | tf_op jit(solution)/shard_map/all_gather | solution.py:356
  13.7 11.7 %copy-start.5 = (bf16[384,640]{1,0:T(8,128)(2,1)S(1)}, bf16[384,640]{1,0:T(8,128)(2,1)}, u32[]{:S(2)}) copy-start(bf16[384,640]{1,0:T(8,128)(2,1)} %param.12) | copy-start | bytes 1474564
  13.7 106.2 %all-to-all-start = ((bf16[32,24,1920]{2,1,0:T(8,128)(2,1)}), bf16[32,24,1920]{2,1,0:T(8,128)(2,1)S(1)}, u32[]{:S(2)}, u32[]{:S(2)}) async-start(bf16[32,24,1920]{2,1,0:T(8,128)(2,1)} %bitcast.29), calls=%async_computation | async-start | bytes 5898240 | tf_op jit(solution)/shard_map/all_to_all | solution.py:346
  25.3 14.2 %collective-permute-start = (bf16[384,640]{1,0:T(8,128)(2,1)S(1)}, bf16[384,640]{1,0:T(8,128)(2,1)S(1)}, u32[]{:S(2)}, u32[]{:S(2)}) collective-permute-start(bf16[384,640]{1,0:T(8,128)(2,1)S(1)} %copy-done.5), channel_id=1, source_target_pairs={{0,2},{1,3},{2,4},{3,5},{4,6},{5,7},{6,0},{7,1},{8,10},{9,11},{10,... | collective-permute-start | bytes 1474568 | tf_op jit(solution)/shard_map/ppermute | solution.py:189
  26.6 14.2 %collective-permute-start.2 = (bf16[384,640]{1,0:T(8,128)(2,1)S(1)}, bf16[384,640]{1,0:T(8,128)(2,1)S(1)}, u32[]{:S(2)}, u32[]{:S(2)}) collective-permute-start(bf16[384,640]{1,0:T(8,128)(2,1)S(1)} %copy-done.5), channel_id=1, source_target_pairs={{0,6},{1,7},{2,0},{3,1},{4,2},{5,3},{6,4},{7,5},{8,14},{9,15},{10,... | collective-permute-start | bytes 1474568 | tf_op jit(solution)/shard_map/ppermute | solution.py:189
  27.4 21.2 %collective-permute-start.1 = (bf16[384,640]{1,0:T(8,128)(2,1)S(1)}, bf16[384,640]{1,0:T(8,128)(2,1)S(1)}, u32[]{:S(2)}, u32[]{:S(2)}) collective-permute-start(bf16[384,640]{1,0:T(8,128)(2,1)S(1)} %copy-done.5), channel_id=1, source_target_pairs={{0,4},{1,5},{2,6},{3,7},{4,0},{5,1},{6,2},{7,3},{8,12},{9,13},{10,... | collective-permute-start | bytes 1474568 | tf_op jit(solution)/shard_map/ppermute | solution.py:189
  48.6 1.5 copy-start.7
  48.6 65.8 %copy-start.6 = (s32[128,128]{1,0:T(8,128)S(1)}, s32[128,128]{1,0:T(8,128)}, u32[]{:S(2)}) copy-start(s32[128,128]{1,0:T(8,128)} %param.15) | copy-start | bytes 196612
  50.2 4.4 %collective-permute-start.5 = (s32[1,768]{1,0:T(1,128)S(1)}, s32[1,768]{1,0:T(1,128)S(1)}, u32[]{:S(2)}, u32[]{:S(2)}) collective-permute-start(s32[1,768]{1,0:T(1,128)S(1)} %copy-done.7), channel_id=1, source_target_pairs={{0,192},{8,200},{16,208},{24,216},{32,224},{40,232},{48,240},{56,2... | collective-permute-start | bytes 9224 | tf_op jit(solution)/shard_map/ppermute | solution.py:204
  52.9 5.1 %collective-permute-start.4 = (s32[1,768]{1,0:T(1,128)S(1)}, s32[1,768]{1,0:T(1,128)S(1)}, u32[]{:S(2)}, u32[]{:S(2)}) collective-permute-start(s32[1,768]{1,0:T(1,128)S(1)} %copy-done.7), channel_id=1, source_target_pairs={{0,128},{8,136},{16,144},{24,152},{32,160},{40,168},{48,176},{56,1... | collective-permute-start | bytes 9224 | tf_op jit(solution)/shard_map/ppermute | solution.py:204
  53.8 4.8 %collective-permute-start.3 = (s32[1,768]{1,0:T(1,128)S(1)}, s32[1,768]{1,0:T(1,128)S(1)}, u32[]{:S(2)}, u32[]{:S(2)}) collective-permute-start(s32[1,768]{1,0:T(1,128)S(1)} %copy-done.7), channel_id=1, source_target_pairs={{0,64},{8,72},{16,80},{24,88},{32,96},{40,104},{48,112},{56,120},{... | collective-permute-start | bytes 9224 | tf_op jit(solution)/shard_map/ppermute | solution.py:204
  58.6 51.1 %collective-permute-start.12 = (s32[4,768]{1,0:T(4,128)S(1)}, s32[4,768]{1,0:T(4,128)S(1)}, u32[]{:S(2)}, u32[]{:S(2)}) collective-permute-start(s32[4,768]{1,0:T(4,128)S(1)} %pad_add_fusion), channel_id=1, source_target_pairs={{0,56},{8,0},{16,8},{24,16},{32,24},{40,32},{48,40},{56,48},{64,12... | collective-permute-start | bytes 36872 | tf_op jit(solution)/shard_map/ppermute | solution.py:204
  61.4 50.8 %collective-permute-start.11 = (s32[4,768]{1,0:T(4,128)S(1)}, s32[4,768]{1,0:T(4,128)S(1)}, u32[]{:S(2)}, u32[]{:S(2)}) collective-permute-start(s32[4,768]{1,0:T(4,128)S(1)} %pad_add_fusion), channel_id=1, source_target_pairs={{0,48},{8,56},{16,0},{24,8},{32,16},{40,24},{48,32},{56,40},{64,11... | collective-permute-start | bytes 36872 | tf_op jit(solution)/shard_map/ppermute | solution.py:204
  63.7 50.2 %collective-permute-start.10 = (s32[4,768]{1,0:T(4,128)S(1)}, s32[4,768]{1,0:T(4,128)S(1)}, u32[]{:S(2)}, u32[]{:S(2)}) collective-permute-start(s32[4,768]{1,0:T(4,128)S(1)} %pad_add_fusion), channel_id=1, source_target_pairs={{0,40},{8,48},{16,56},{24,0},{32,8},{40,16},{48,24},{56,32},{64,10... | collective-permute-start | bytes 36872 | tf_op jit(solution)/shard_map/ppermute | solution.py:204
  65.2 70.8 %collective-permute-start.13 = (bf16[4,384,640]{2,1,0:T(8,128)(2,1)}, bf16[4,384,640]{2,1,0:T(8,128)(2,1)}, u32[]{:S(2)}, u32[]{:S(2)}) collective-permute-start(bf16[4,384,640]{2,1,0:T(8,128)(2,1)} %pad_maximum_fusion.near_ref), channel_id=1, source_target_pairs={{0,1},{1,0},{2,3},{3,2},{4,5},{5,4},{6,7},{7,6},{8,9},{9,8},{10,11... | collective-permute-start | bytes 5898248 | tf_op jit(solution)/shard_map/ppermute | solution.py:191
  65.3 49.2 %collective-permute-start.9 = (s32[4,768]{1,0:T(4,128)S(1)}, s32[4,768]{1,0:T(4,128)S(1)}, u32[]{:S(2)}, u32[]{:S(2)}) collective-permute-start(s32[4,768]{1,0:T(4,128)S(1)} %pad_add_fusion), channel_id=1, source_target_pairs={{0,32},{8,40},{16,48},{24,56},{32,0},{40,8},{48,16},{56,24},{64,96... | collective-permute-start | bytes 36872 | tf_op jit(solution)/shard_map/ppermute | solution.py:204
  109.7 6.9 %collective-permute-start.8 = (s32[4,768]{1,0:T(4,128)S(1)}, s32[4,768]{1,0:T(4,128)S(1)}, u32[]{:S(2)}, u32[]{:S(2)}) collective-permute-start(s32[4,768]{1,0:T(4,128)S(1)} %pad_add_fusion), channel_id=1, source_target_pairs={{0,24},{8,32},{16,40},{24,48},{32,56},{40,0},{48,8},{56,16},{64,88... | collective-permute-start | bytes 36872 | tf_op jit(solution)/shard_map/ppermute | solution.py:204
  112.1 6.0 %collective-permute-start.7 = (s32[4,768]{1,0:T(4,128)S(1)}, s32[4,768]{1,0:T(4,128)S(1)}, u32[]{:S(2)}, u32[]{:S(2)}) collective-permute-start(s32[4,768]{1,0:T(4,128)S(1)} %pad_add_fusion), channel_id=1, source_target_pairs={{0,16},{8,24},{16,32},{24,40},{32,48},{40,56},{48,0},{56,8},{64,80... | collective-permute-start | bytes 36872 | tf_op jit(solution)/shard_map/ppermute | solution.py:204
  113.9 5.1 %collective-permute-start.6 = (s32[4,768]{1,0:T(4,128)S(1)}, s32[4,768]{1,0:T(4,128)S(1)}, u32[]{:S(2)}, u32[]{:S(2)}) collective-permute-start(s32[4,768]{1,0:T(4,128)S(1)} %pad_add_fusion), channel_id=1, source_target_pairs={{0,8},{8,16},{16,24},{24,32},{32,40},{40,48},{48,56},{56,0},{64,72... | collective-permute-start | bytes 36872 | tf_op jit(solution)/shard_map/ppermute | solution.py:204
  119.9 8.7 %copy-start = (bf16[32,24,1920]{2,1,0:T(8,128)(2,1)}, bf16[32,24,1920]{2,1,0:T(8,128)(2,1)S(1)}, u32[]{:S(2)}) copy-start(bf16[32,24,1920]{2,1,0:T(8,128)(2,1)S(1)} %all-to-all-done) | copy-start | bytes 8847364
  128.6 1.0 copy-start.2
  129.6 30.9 %all-to-all-start.1 = ((bf16[32,24,640]{2,1,0:T(8,128)(2,1)}), bf16[32,24,640]{2,1,0:T(8,128)(2,1)S(1)}, u32[]{:S(2)}, u32[]{:S(2)}) async-start(bf16[32,24,640]{2,1,0:T(8,128)(2,1)} %bitcast.24), calls=%async_computation.1 | async-start | bytes 1966080 | tf_op jit(solution)/shard_map/all_to_all | solution.py:346
  147.2 18.4 %copy-start.4 = (s32[384,128]{1,0:T(8,128)S(1)}, s32[384,128]{1,0:T(8,128)}, u32[]{:S(2)}) copy-start(s32[384,128]{1,0:T(8,128)} %get-tuple-element.15.dest_col.dest_ref) | copy-start | bytes 589828
  160.5 28.9 %all-to-all-start.2 = ((bf16[32,24,640]{2,1,0:T(8,128)(2,1)}), bf16[32,24,640]{2,1,0:T(8,128)(2,1)S(1)}, u32[]{:S(2)}, u32[]{:S(2)}) async-start(bf16[32,24,640]{2,1,0:T(8,128)(2,1)} %bitcast.28), calls=%async_computation.3 | async-start | bytes 1966080 | tf_op jit(solution)/shard_map/all_to_all | solution.py:346
  165.5 107.2 %reduce-scatter.2.cloned.1.call-start = ((), (), s32[]{:S(2)}) async-start(), calls=%async_computation.6 | async-start | bytes 4423680 | tf_op jit(solution)/shard_map/reduce_scatter | solution.py:368
  174.2 1.9 copy-start.1
  176.0 13.4 %copy-start.3 = (bf16[768,640]{1,0:T(8,128)(2,1)S(1)}, bf16[768,640]{1,0:T(8,128)(2,1)}, u32[]{:S(2)}) copy-start(bf16[768,640]{1,0:T(8,128)(2,1)} %copy-done.2) | copy-start | bytes 2949124
Sparse Core Ops, SparseCore 0:
  10.6 122.4 all-gather.1
  176.2 36.3 reduce-scatter.1

commit v6 on v5

--- a/solution.py
+++ b/solution.py
@@ -306,31 +306,34 @@
     )(owned, owned, owned, attended, grad_owned, weights)
 
 
-def unpack_kernel(dest_ref, blocks_ref, q_ref, k_ref, v_ref, select):
-    @pl.when(pl.program_id(0) == 0)
-    def _():
-        select[...] = as_bf16(dest_ref[:, 0:1] == lax.broadcasted_iota(jnp.int32, select.shape, 1))
-
-    picked = dot32(select[...], blocks_ref[...]).astype(jnp.bfloat16)
-    q_ref[...] = picked[:, 0:HEAD]
-    k_ref[...] = picked[:, HEAD : 2 * HEAD]
-    v_ref[...] = picked[:, 2 * HEAD :]
+def unpack_kernel(heads, dest_ref, blocks_ref, *refs):
+    outs, (held, sems) = refs[:3], refs[3:]
+    rows = dest_ref.shape[0]
+    select = as_bf16(dest_ref[:, 0:1] == lax.broadcasted_iota(jnp.int32, (rows, blocks_ref.shape[0]), 1))
+    copies = []
+    for head in range(heads):
+        wide = slice(head * 3 * HEAD, (head + 1) * 3 * HEAD)
+        held[:, wide] = dot32(select, blocks_ref[:, wide]).astype(jnp.bfloat16)
+        for place, out_ref in enumerate(outs):
+            start = (head * 3 + place) * HEAD
+            source = held.at[:, start : start + HEAD]
+            target = out_ref.at[:, head * HEAD : (head + 1) * HEAD]
+            copies.append(pltpu.make_async_copy(source, target, sems.at[head * 3 + place]))
+            copies[-1].start()
+    for copy in copies:
+        copy.wait()
 
 
 def unpack_grads(dest_col, blocks, heads):
     rows = dest_col.shape[0]
-    buffer_rows = blocks.shape[0]
+    buffer_rows, cols = blocks.shape
     out = jax.ShapeDtypeStruct((rows, heads * HEAD), jnp.bfloat16)
     return pl.pallas_call(
-        unpack_kernel,
-        grid=(heads,),
-        in_specs=[
-            pl.BlockSpec((rows, HEAD), lambda h: (0, 0)),
-            pl.BlockSpec((buffer_rows, 3 * HEAD), lambda h: (0, h)),
-        ],
-        out_specs=[pl.BlockSpec((rows, HEAD), lambda h: (0, h))] * 3,
+        lambda *refs: unpack_kernel(heads, *refs),
+        in_specs=[pl.BlockSpec(memory_space=pltpu.VMEM)] * 2,
+        out_specs=(pl.BlockSpec(memory_space=pl.ANY),) * 3,
         out_shape=(out, out, out),
-        scratch_shapes=[pltpu.VMEM((rows, buffer_rows), jnp.bfloat16)],
+        scratch_shapes=[pltpu.VMEM((rows, cols), jnp.bfloat16), pltpu.SemaphoreType.DMA((3 * heads,))],
         compiler_params=params(),
         cost_estimate=pl.CostEstimate(
             flops=6 * heads * rows * buffer_rows * HEAD,

time: 281 us -> 279 us (level)
  transfers between devices with their start and end apart: 19 -> 19, of which waited for: 11 -> 11; matrix products, arithmetic and copies ran while one was open for 1% -> 1% of each run, Pallas kernels for 17% -> 16%
where the time goes in v6:
time: 279 us; the launch traced here: 278 us
  waiting for transfers between devices  96.1 us (34%)
  blocking collectives  70.5 us (25%)
  starting transfers between devices  45.9 us (16%)
  Pallas kernels  45.6 us (16%)
  between operations  14.2 us (5%)
  local copies, waits for them, and re-layouts  3.87 us (1%)
    all_to_all x1, blocking collectives, exchange(): lax.all_to_all(blocks, 'seq', split_axis=0, concat_axis=0, tiled=True)  70.5 us
    ppermute x10, waiting for transfers between devices, move(): return lax.ppermute(block, 'seq', steps)  49.2 us
    all_to_all x3, waiting for transfers between devices, exchange(): lax.all_to_all(blocks, 'seq', split_axis=0, concat_axis=0, tiled=True)  26.6 us
    all_to_all x3, starting transfers between devices, exchange(): lax.all_to_all(blocks, 'seq', split_axis=0, concat_axis=0, tiled=True)  22.5 us
    ppermute x3, waiting for transfers between devices, gather_groups(): lax.ppermute(block, 'tp', [(t, (t + 2 * shift) % tp_count) for t in range...  19.5 us
    ppermute x10, starting transfers between devices, move(): return lax.ppermute(block, 'seq', steps)  19.4 us
    pallas_call x1, Pallas kernels, project_grads(): pl.pallas_call(grad_kernel, grid_spec=pltpu.PrefetchScalarGridSpec(num_sc...  11.2 us
    pallas_call x1, Pallas kernels, attention_backward(): pl.pallas_call(lambda *refs: backward_kernel(scale, *refs), grid=(heads,)...  8.95 us
  transfers between devices with their start and end apart: 19, of which 11 were waited for; matrix products, arithmetic and copies ran while one was open for 1% of the time, Pallas kernels for 16%

profile of v6, /device:TPU:4, one launch (start us, length us, event | category | flops | bytes accessed | tf_op | source)
XLA Modules:
  0.0 278.3 jit_solution(16569066528036774324)
XLA Ops:
  7.2 0.0 all-gather.2.cloned.1.call-start
  7.2 0.7 all-gather.2.cloned.1.call-update
  7.9 5.8 %shard_map.111 = (bf16[768,1920]{1,0:T(8,128)(2,1)}, s32[1,384]{1,0:T(1,128)}, s32[384,128]{1,0:T(8,128)}, s32[1,768]{1,0:T(1,128)}) custom-call(s32[384]{0:T(512)} %refs_0_.1, s32[1,128]{1,0:T(1,128)} %bitcast.35, bf16[384,640]{1,0:T(8,128)(2,1)} %refs_2_.1, bf16[384,640]{1,0:T(8,128)(2,1)} %refs_3_.1, bf16[384,640]{1,0:T(8,128)(2,1)} %refs_4_.1), custom_call_target="tpu_custom_call" | custom-call | tf_op jit(solution)/shard_map/pallas_call | solution.py:83
  13.7 11.6 %all-to-all-start = ((bf16[32,24,1920]{2,1,0:T(8,128)(2,1)}), bf16[32,24,1920]{2,1,0:T(8,128)(2,1)S(1)}, u32[]{:S(2)}, u32[]{:S(2)}) async-start(bf16[32,24,1920]{2,1,0:T(8,128)(2,1)} %bitcast.29), calls=%async_computation | async-start | bytes 5898240 | tf_op jit(solution)/shard_map/all_to_all | solution.py:349
  25.3 1.3 collective-permute-start
  26.6 0.8 collective-permute-start.2
  27.4 1.7 collective-permute-start.1
  29.2 10.4 %collective-permute-done = bf16[384,640]{1,0:T(8,128)(2,1)S(1)} collective-permute-done((bf16[384,640]{1,0:T(8,128)(2,1)S(1)}, bf16[384,640]{1,0:T(8,128)(2,1)S(1)}, u32[]{:S(2)}, u32[]{:S(2)}) %collective-permute-start) | collective-permute-done | bytes 491552 | tf_op jit(solution)/shard_map/ppermute | solution.py:189
  39.6 1.2 collective-permute-done.2
  40.8 7.9 %collective-permute-done.1 = bf16[384,640]{1,0:T(8,128)(2,1)S(1)} collective-permute-done((bf16[384,640]{1,0:T(8,128)(2,1)S(1)}, bf16[384,640]{1,0:T(8,128)(2,1)S(1)}, u32[]{:S(2)}, u32[]{:S(2)}) %collective-permute-start.1) | collective-permute-done | bytes 491552 | tf_op jit(solution)/shard_map/ppermute | solution.py:189
  48.6 1.5 pad_maximum_fusion.near_ref
  50.2 2.8 collective-permute-start.5
  52.9 0.8 collective-permute-start.4
  53.8 0.9 collective-permute-start.3
  54.6 3.4 %collective-permute-done.4 = s32[1,768]{1,0:T(1,128)S(1)} collective-permute-done((s32[1,768]{1,0:T(1,128)S(1)}, s32[1,768]{1,0:T(1,128)S(1)}, u32[]{:S(2)}, u32[]{:S(2)}) %collective-permute-start.4) | collective-permute-done | bytes 3104 | tf_op jit(solution)/shard_map/ppermute | solution.py:204
  58.1 0.5 collective-permute-done.3
  58.6 2.8 collective-permute-start.12
  61.4 2.4 collective-permute-start.11
  63.7 1.5 collective-permute-start.10
  65.2 0.1 collective-permute-start.13
  65.3 3.7 %collective-permute-start.9 = (s32[4,768]{1,0:T(4,128)S(1)}, s32[4,768]{1,0:T(4,128)S(1)}, u32[]{:S(2)}, u32[]{:S(2)}) collective-permute-start(s32[4,768]{1,0:T(4,128)S(1)} %pad_add_fusion), channel_id=1, source_target_pairs={{0,32},{8,40},{16,48},{24,56},{32,0},{40,8},{48,16},{56,24},{64,96... | collective-permute-start | bytes 36872 | tf_op jit(solution)/shard_map/ppermute | solution.py:204
  69.0 40.8 %collective-permute-done.12 = s32[4,768]{1,0:T(4,128)S(1)} collective-permute-done((s32[4,768]{1,0:T(4,128)S(1)}, s32[4,768]{1,0:T(4,128)S(1)}, u32[]{:S(2)}, u32[]{:S(2)}) %collective-permute-start.12) | collective-permute-done | bytes 12320 | tf_op jit(solution)/shard_map/ppermute | solution.py:204
  109.7 2.4 collective-permute-start.8
  112.1 1.8 collective-permute-start.7
  113.9 0.6 collective-permute-start.6
  114.5 2.2 collective-permute-done.8
  116.7 1.5 collective-permute-done.7
  118.1 0.9 collective-permute-done.6
  119.0 0.1 concatenate.11
  119.1 0.1 constant_dynamic-slice_fusion
  119.2 0.6 gather_fusion
  119.8 0.1 convert_element_type.9
  119.9 0.2 broadcast_in_dim.10.refs_3_
  120.1 8.6 %shard_map.112 = (bf16[768,640]{1,0:T(8,128)(2,1)S(1)}, bf16[5,768,768]{2,1,0:T(8,128)(2,1)}) custom-call(bf16[768,1920]{1,0:T(8,128)(2,1)S(1)} %bitcast.17, bf16[768,1920]{1,0:T(8,128)(2,1)S(1)} %bitcast.18, bf16[768,1920]{1,0:T(8,128)(2,1)S(1)} %bitcast.19, bf16[768,128]{1,0:T(8,128)(2,1)S(1)} %broadcast_in_dim.10.refs_3_, ...), custom_call_target="tpu_custom_call" | custom-call | flops 1509949440 | bytes 9830400 | tf_op jit(solution)/shard_map/pallas_call | solution.py:256
  128.6 1.0 copy-done.2
  129.6 5.8 %all-to-all-start.1 = ((bf16[32,24,640]{2,1,0:T(8,128)(2,1)}), bf16[32,24,640]{2,1,0:T(8,128)(2,1)S(1)}, u32[]{:S(2)}, u32[]{:S(2)}) async-start(bf16[32,24,640]{2,1,0:T(8,128)(2,1)} %bitcast.24), calls=%async_computation.1 | async-start | bytes 1966080 | tf_op jit(solution)/shard_map/all_to_all | solution.py:349
  135.4 0.6 pad_add_fusion.1.order_ref
  136.0 11.2 %shard_map.114 = bf16[768,640]{1,0:T(8,128)(2,1)} custom-call(s32[8]{0:T(128)} %pad_add_fusion.1.order_ref, bf16[4,384,640]{2,1,0:T(8,128)(2,1)} %pad_maximum_fusion.near_ref, bf16[4,384,640]{2,1,0:T(8,128)(2,1)} %collective-permute-done.13.far_ref, bf16[5120,640]{1,0:T(8,128)(2,1)} %all-gather.2.cloned.1.call-done.weight_ref, ...), custom_call_target="tpu_custom_call" | custom-call | flops 2894069760 | bytes 10485760 | tf_op jit(solution)/shard_map/pallas_call | solution.py:128
  147.2 13.3 %all-to-all-done.1 = bf16[32,24,640]{2,1,0:T(8,128)(2,1)S(1)} async-done(((bf16[32,24,640]{2,1,0:T(8,128)(2,1)}), bf16[32,24,640]{2,1,0:T(8,128)(2,1)S(1)}, u32[]{:S(2)}, u32[]{:S(2)}) %all-to-all-start.1) | async-done | bytes 983072 | tf_op jit(solution)/shard_map/all_to_all | solution.py:349
  160.5 5.1 %all-to-all-start.2 = ((bf16[32,24,640]{2,1,0:T(8,128)(2,1)}), bf16[32,24,640]{2,1,0:T(8,128)(2,1)S(1)}, u32[]{:S(2)}, u32[]{:S(2)}) async-start(bf16[32,24,640]{2,1,0:T(8,128)(2,1)} %bitcast.28), calls=%async_computation.3 | async-start | bytes 1966080 | tf_op jit(solution)/shard_map/all_to_all | solution.py:349
  165.5 0.0 reduce-scatter.2.cloned.1.call-start
  165.6 8.6 %shard_map.113 = bf16[8,384,640]{2,1,0:T(8,128)(2,1)S(1)} custom-call(s32[384,128]{1,0:T(8,128)S(1)} %copy-done.4, bf16[768,640]{1,0:T(8,128)(2,1)S(1)} %bitcast.25, bf16[5120,640]{1,0:T(8,128)(2,1)} %all-gather.2.cloned.1.call-done.weight_ref), custom_call_target="tpu_custom_call" | custom-call | flops 2894069760 | bytes 10485760 | tf_op jit(solution)/shard_map/pallas_call | solution.py:164
  174.2 1.9 copy-done.1
  176.1 13.3 %all-to-all-done.2 = bf16[32,24,640]{2,1,0:T(8,128)(2,1)S(1)} async-done(((bf16[32,24,640]{2,1,0:T(8,128)(2,1)}), bf16[32,24,640]{2,1,0:T(8,128)(2,1)S(1)}, u32[]{:S(2)}, u32[]{:S(2)}) %all-to-all-start.2) | async-done | bytes 983072 | tf_op jit(solution)/shard_map/all_to_all | solution.py:349
  189.4 9.0 %shard_map.115 = bf16[768,1920]{1,0:T(8,128)(2,1)S(1)} custom-call(bf16[768,1920]{1,0:T(8,128)(2,1)} %bitcast.20, bf16[768,1920]{1,0:T(8,128)(2,1)} %bitcast.21, bf16[768,1920]{1,0:T(8,128)(2,1)} %bitcast.22, bf16[768,640]{1,0:T(8,128)(2,1)S(1)} %copy-done.3, bf16[768,640]{1,0:T(8,128)(2,1)S(1)} %bitcast.26, bf16[5,768,768]{2,1,0:T(8,128)(2,1)} %get-tuple-element.22.refs_5_), custom_call_target="tpu_custom_call" | custom-call | flops 3019898880 | bytes 13762560 | tf_op jit(solution)/shard_map/pallas_call | solution.py:287
  198.4 70.5 %all_to_all.20 = bf16[32,24,1920]{2,1,0:T(8,128)(2,1)S(1)} all-to-all(bf16[32,24,1920]{2,1,0:T(8,128)(2,1)S(1)} %bitcast.23), channel_id=1, replica_groups=mesh['seq'=32,'tp'=8] {'seq'}, dimensions={0} | all-to-all | bytes 5898240 | tf_op jit(solution)/shard_map/all_to_all | solution.py:349
  268.8 2.6 shard_map.116
  271.4 0.0 reduce-scatter.2.cloned.1.call-done
  (28 shorter events, 0.1 us)
Async XLA Ops:
  7.2 128.8 %all-gather.2.cloned.1.call-start = ((), (), s32[]{:S(2)}) async-start(), calls=%async_computation.5 | async-start | bytes 6758400 | tf_op jit(solution)/shard_map/all_gather | solution.py:359
  13.7 11.7 %copy-start.5 = (bf16[384,640]{1,0:T(8,128)(2,1)S(1)}, bf16[384,640]{1,0:T(8,128)(2,1)}, u32[]{:S(2)}) copy-start(bf16[384,640]{1,0:T(8,128)(2,1)} %param.12) | copy-start | bytes 1474564
  13.7 106.2 %all-to-all-start = ((bf16[32,24,1920]{2,1,0:T(8,128)(2,1)}), bf16[32,24,1920]{2,1,0:T(8,128)(2,1)S(1)}, u32[]{:S(2)}, u32[]{:S(2)}) async-start(bf16[32,24,1920]{2,1,0:T(8,128)(2,1)} %bitcast.29), calls=%async_computation | async-start | bytes 5898240 | tf_op jit(solution)/shard_map/all_to_all | solution.py:349
  25.3 14.2 %collective-permute-start = (bf16[384,640]{1,0:T(8,128)(2,1)S(1)}, bf16[384,640]{1,0:T(8,128)(2,1)S(1)}, u32[]{:S(2)}, u32[]{:S(2)}) collective-permute-start(bf16[384,640]{1,0:T(8,128)(2,1)S(1)} %copy-done.5), channel_id=1, source_target_pairs={{0,2},{1,3},{2,4},{3,5},{4,6},{5,7},{6,0},{7,1},{8,10},{9,11},{10,... | collective-permute-start | bytes 1474568 | tf_op jit(solution)/shard_map/ppermute | solution.py:189
  26.6 14.2 %collective-permute-start.2 = (bf16[384,640]{1,0:T(8,128)(2,1)S(1)}, bf16[384,640]{1,0:T(8,128)(2,1)S(1)}, u32[]{:S(2)}, u32[]{:S(2)}) collective-permute-start(bf16[384,640]{1,0:T(8,128)(2,1)S(1)} %copy-done.5), channel_id=1, source_target_pairs={{0,6},{1,7},{2,0},{3,1},{4,2},{5,3},{6,4},{7,5},{8,14},{9,15},{10,... | collective-permute-start | bytes 1474568 | tf_op jit(solution)/shard_map/ppermute | solution.py:189
  27.4 21.2 %collective-permute-start.1 = (bf16[384,640]{1,0:T(8,128)(2,1)S(1)}, bf16[384,640]{1,0:T(8,128)(2,1)S(1)}, u32[]{:S(2)}, u32[]{:S(2)}) collective-permute-start(bf16[384,640]{1,0:T(8,128)(2,1)S(1)} %copy-done.5), channel_id=1, source_target_pairs={{0,4},{1,5},{2,6},{3,7},{4,0},{5,1},{6,2},{7,3},{8,12},{9,13},{10,... | collective-permute-start | bytes 1474568 | tf_op jit(solution)/shard_map/ppermute | solution.py:189
  48.6 1.5 copy-start.7
  48.6 65.8 %copy-start.6 = (s32[128,128]{1,0:T(8,128)S(1)}, s32[128,128]{1,0:T(8,128)}, u32[]{:S(2)}) copy-start(s32[128,128]{1,0:T(8,128)} %param.15) | copy-start | bytes 196612
  50.2 4.4 %collective-permute-start.5 = (s32[1,768]{1,0:T(1,128)S(1)}, s32[1,768]{1,0:T(1,128)S(1)}, u32[]{:S(2)}, u32[]{:S(2)}) collective-permute-start(s32[1,768]{1,0:T(1,128)S(1)} %copy-done.7), channel_id=1, source_target_pairs={{0,192},{8,200},{16,208},{24,216},{32,224},{40,232},{48,240},{56,2... | collective-permute-start | bytes 9224 | tf_op jit(solution)/shard_map/ppermute | solution.py:204
  52.9 5.1 %collective-permute-start.4 = (s32[1,768]{1,0:T(1,128)S(1)}, s32[1,768]{1,0:T(1,128)S(1)}, u32[]{:S(2)}, u32[]{:S(2)}) collective-permute-start(s32[1,768]{1,0:T(1,128)S(1)} %copy-done.7), channel_id=1, source_target_pairs={{0,128},{8,136},{16,144},{24,152},{32,160},{40,168},{48,176},{56,1... | collective-permute-start | bytes 9224 | tf_op jit(solution)/shard_map/ppermute | solution.py:204
  53.8 4.8 %collective-permute-start.3 = (s32[1,768]{1,0:T(1,128)S(1)}, s32[1,768]{1,0:T(1,128)S(1)}, u32[]{:S(2)}, u32[]{:S(2)}) collective-permute-start(s32[1,768]{1,0:T(1,128)S(1)} %copy-done.7), channel_id=1, source_target_pairs={{0,64},{8,72},{16,80},{24,88},{32,96},{40,104},{48,112},{56,120},{... | collective-permute-start | bytes 9224 | tf_op jit(solution)/shard_map/ppermute | solution.py:204
  58.6 51.1 %collective-permute-start.12 = (s32[4,768]{1,0:T(4,128)S(1)}, s32[4,768]{1,0:T(4,128)S(1)}, u32[]{:S(2)}, u32[]{:S(2)}) collective-permute-start(s32[4,768]{1,0:T(4,128)S(1)} %pad_add_fusion), channel_id=1, source_target_pairs={{0,56},{8,0},{16,8},{24,16},{32,24},{40,32},{48,40},{56,48},{64,12... | collective-permute-start | bytes 36872 | tf_op jit(solution)/shard_map/ppermute | solution.py:204
  61.4 50.8 %collective-permute-start.11 = (s32[4,768]{1,0:T(4,128)S(1)}, s32[4,768]{1,0:T(4,128)S(1)}, u32[]{:S(2)}, u32[]{:S(2)}) collective-permute-start(s32[4,768]{1,0:T(4,128)S(1)} %pad_add_fusion), channel_id=1, source_target_pairs={{0,48},{8,56},{16,0},{24,8},{32,16},{40,24},{48,32},{56,40},{64,11... | collective-permute-start | bytes 36872 | tf_op jit(solution)/shard_map/ppermute | solution.py:204
  63.7 50.2 %collective-permute-start.10 = (s32[4,768]{1,0:T(4,128)S(1)}, s32[4,768]{1,0:T(4,128)S(1)}, u32[]{:S(2)}, u32[]{:S(2)}) collective-permute-start(s32[4,768]{1,0:T(4,128)S(1)} %pad_add_fusion), channel_id=1, source_target_pairs={{0,40},{8,48},{16,56},{24,0},{32,8},{40,16},{48,24},{56,32},{64,10... | collective-permute-start | bytes 36872 | tf_op jit(solution)/shard_map/ppermute | solution.py:204
  65.2 70.8 %collective-permute-start.13 = (bf16[4,384,640]{2,1,0:T(8,128)(2,1)}, bf16[4,384,640]{2,1,0:T(8,128)(2,1)}, u32[]{:S(2)}, u32[]{:S(2)}) collective-permute-start(bf16[4,384,640]{2,1,0:T(8,128)(2,1)} %pad_maximum_fusion.near_ref), channel_id=1, source_target_pairs={{0,1},{1,0},{2,3},{3,2},{4,5},{5,4},{6,7},{7,6},{8,9},{9,8},{10,11... | collective-permute-start | bytes 5898248 | tf_op jit(solution)/shard_map/ppermute | solution.py:191
  65.3 49.2 %collective-permute-start.9 = (s32[4,768]{1,0:T(4,128)S(1)}, s32[4,768]{1,0:T(4,128)S(1)}, u32[]{:S(2)}, u32[]{:S(2)}) collective-permute-start(s32[4,768]{1,0:T(4,128)S(1)} %pad_add_fusion), channel_id=1, source_target_pairs={{0,32},{8,40},{16,48},{24,56},{32,0},{40,8},{48,16},{56,24},{64,96... | collective-permute-start | bytes 36872 | tf_op jit(solution)/shard_map/ppermute | solution.py:204
  109.7 6.9 %collective-permute-start.8 = (s32[4,768]{1,0:T(4,128)S(1)}, s32[4,768]{1,0:T(4,128)S(1)}, u32[]{:S(2)}, u32[]{:S(2)}) collective-permute-start(s32[4,768]{1,0:T(4,128)S(1)} %pad_add_fusion), channel_id=1, source_target_pairs={{0,24},{8,32},{16,40},{24,48},{32,56},{40,0},{48,8},{56,16},{64,88... | collective-permute-start | bytes 36872 | tf_op jit(solution)/shard_map/ppermute | solution.py:204
  112.1 6.0 %collective-permute-start.7 = (s32[4,768]{1,0:T(4,128)S(1)}, s32[4,768]{1,0:T(4,128)S(1)}, u32[]{:S(2)}, u32[]{:S(2)}) collective-permute-start(s32[4,768]{1,0:T(4,128)S(1)} %pad_add_fusion), channel_id=1, source_target_pairs={{0,16},{8,24},{16,32},{24,40},{32,48},{40,56},{48,0},{56,8},{64,80... | collective-permute-start | bytes 36872 | tf_op jit(solution)/shard_map/ppermute | solution.py:204
  113.9 5.1 %collective-permute-start.6 = (s32[4,768]{1,0:T(4,128)S(1)}, s32[4,768]{1,0:T(4,128)S(1)}, u32[]{:S(2)}, u32[]{:S(2)}) collective-permute-start(s32[4,768]{1,0:T(4,128)S(1)} %pad_add_fusion), channel_id=1, source_target_pairs={{0,8},{8,16},{16,24},{24,32},{32,40},{40,48},{48,56},{56,0},{64,72... | collective-permute-start | bytes 36872 | tf_op jit(solution)/shard_map/ppermute | solution.py:204
  119.9 8.7 %copy-start = (bf16[32,24,1920]{2,1,0:T(8,128)(2,1)}, bf16[32,24,1920]{2,1,0:T(8,128)(2,1)S(1)}, u32[]{:S(2)}) copy-start(bf16[32,24,1920]{2,1,0:T(8,128)(2,1)S(1)} %all-to-all-done) | copy-start | bytes 8847364
  128.6 1.0 copy-start.2
  129.6 30.9 %all-to-all-start.1 = ((bf16[32,24,640]{2,1,0:T(8,128)(2,1)}), bf16[32,24,640]{2,1,0:T(8,128)(2,1)S(1)}, u32[]{:S(2)}, u32[]{:S(2)}) async-start(bf16[32,24,640]{2,1,0:T(8,128)(2,1)} %bitcast.24), calls=%async_computation.1 | async-start | bytes 1966080 | tf_op jit(solution)/shard_map/all_to_all | solution.py:349
  147.2 18.4 %copy-start.4 = (s32[384,128]{1,0:T(8,128)S(1)}, s32[384,128]{1,0:T(8,128)}, u32[]{:S(2)}) copy-start(s32[384,128]{1,0:T(8,128)} %get-tuple-element.15.dest_col.refs_0_) | copy-start | bytes 589828
  160.5 28.9 %all-to-all-start.2 = ((bf16[32,24,640]{2,1,0:T(8,128)(2,1)}), bf16[32,24,640]{2,1,0:T(8,128)(2,1)S(1)}, u32[]{:S(2)}, u32[]{:S(2)}) async-start(bf16[32,24,640]{2,1,0:T(8,128)(2,1)} %bitcast.28), calls=%async_computation.3 | async-start | bytes 1966080 | tf_op jit(solution)/shard_map/all_to_all | solution.py:349
  165.5 105.9 %reduce-scatter.2.cloned.1.call-start = ((), (), s32[]{:S(2)}) async-start(), calls=%async_computation.6 | async-start | bytes 4423680 | tf_op jit(solution)/shard_map/reduce_scatter | solution.py:371
  174.2 1.9 copy-start.1
  176.0 13.4 %copy-start.3 = (bf16[768,640]{1,0:T(8,128)(2,1)S(1)}, bf16[768,640]{1,0:T(8,128)(2,1)}, u32[]{:S(2)}) copy-start(bf16[768,640]{1,0:T(8,128)(2,1)} %copy-done.2) | copy-start | bytes 2949124
Sparse Core Ops, SparseCore 0:
  10.6 122.4 all-gather.1
  176.2 36.3 reduce-scatter.1
